TPU v7x, 32 devices: a whole 2x2x4 slice. The times are simulated.
32 devices in a mesh: section: 2 (over core), shard: 4 (over z), rep: 4 (over y, x).
Axes of the slice: x: 2, y: 2, z: 4, core: 2. Of those that a mesh axis runs over, the one named last changes fastest.
Arguments:
- tokens: bfloat16 [3072, 1024], P(('shard', 'rep')), may hold values from -6 to 6
- doc_lengths: int32 [32, 4], P(('shard', 'rep')), may hold values from 1 to 48, 96 in all within a row
- heads_weight: bfloat16 [2, 1024, 3072], P('section', 'shard'), may hold values from -0.1875 to 0.1875
- merge_weight: bfloat16 [2, 1024, 1024], P('section', 'shard'), may hold values from -0.75 to 0.75
- up_weight: bfloat16 [2, 1024, 4096], P('section', 'shard'), may hold values from -0.1875 to 0.1875
- down_weight: bfloat16 [2, 4096, 1024], P('section', 'shard'), may hold values from -0.125 to 0.125
- first_gain: bfloat16 [2, 1024], P('section', 'shard'), may hold values from 0.5 to 1.5
- first_shift: bfloat16 [2, 1024], P('section', 'shard'), may hold values from -3 to 3
- query_bias: bfloat16 [2, 1024], P('section', 'shard'), may hold values from -3 to 3
- value_bias: bfloat16 [2, 1024], P('section', 'shard'), may hold values from -3 to 3
- output_bias: bfloat16 [2, 1024], P('section', 'shard'), may hold values from -3 to 3
- second_gain: bfloat16 [2, 1024], P('section', 'shard'), may hold values from 0.5 to 1.5
- second_shift: bfloat16 [2, 1024], P('section', 'shard'), may hold values from -3 to 3
- up_bias: bfloat16 [2, 4096], P('section', 'shard'), may hold values from -3 to 3
- down_bias: bfloat16 [2, 1024], P('section', 'shard'), may hold values from -3 to 3
- cotangent: bfloat16 [3072, 1024], P(('shard', 'rep')), may hold values from -6 to 6
Outputs:
- activations: bfloat16 [2, 3072, 1024], P('section', ('shard', 'rep'))
- input_grads: bfloat16 [2, 3072, 1024], P('section', ('shard', 'rep'))
- grad_heads_weight: float32 [2, 1024, 3072], P('section', 'shard')
- grad_merge_weight: float32 [2, 1024, 1024], P('section', 'shard')
- grad_up_weight: float32 [2, 1024, 4096], P('section', 'shard')
- grad_down_weight: float32 [2, 4096, 1024], P('section', 'shard')
- grad_first_gain: float32 [2, 1024], P('section', 'shard')
- grad_first_shift: float32 [2, 1024], P('section', 'shard')
- grad_query_bias: float32 [2, 1024], P('section', 'shard')
- grad_value_bias: float32 [2, 1024], P('section', 'shard')
- grad_output_bias: float32 [2, 1024], P('section', 'shard')
- grad_second_gain: float32 [2, 1024], P('section', 'shard')
- grad_second_shift: float32 [2, 1024], P('section', 'shard')
- grad_up_bias: float32 [2, 4096], P('section', 'shard')
- grad_down_bias: float32 [2, 1024], P('section', 'shard')
Inputs may be any that keep to these rules, and one draw needn't show every extreme that they name: `doc_lengths`: each row holds, in order, the lengths of the 4 sequences packed into one slot of 96 rows; they sum to 96.
All inputs are finite; a program needn't handle non-finite values.
Results may differ from a plain program's by a relative error of at most 0.02.
Values may be sent and summed in bfloat16 or wider, within the bound.
No kernel may reach another device: no remote copies, remote signals or barrier semaphores. Data moves between devices by JAX's collectives and lax.ppermute only.
A program may use at most 192 MiB of HBM per device.

v0:
```python
from functools import reduce
import math

import jax
import jax.numpy as jnp
from jax import lax
from jax.sharding import PartitionSpec as P

HEADS = 16


NORM_EPS = 1e-05
GELU_COEF = 0.7978845608028654


def shifted(block, axis, distance):
    devices = range(lax.axis_size(axis))
    route = [(i - distance, i) for i in devices if i - distance in devices]
    return lax.ppermute(block, axis, route)


def gelu_tanh(entries):
    return (
        0.5
        * entries
        * (1.0 + jnp.tanh(GELU_COEF * (entries + 0.044715 * entries * entries * entries)))
    )


def norm_rows(entries, norm_gain, norm_shift):
    centre = jnp.mean(entries, axis=-1, keepdims=True)
    centred = entries - centre
    spread = jnp.mean(centred * centred, axis=-1, keepdims=True)
    return centred * lax.rsqrt(spread + NORM_EPS) * norm_gain + norm_shift


def visible_mask(lengths, row_count):
    doc_ends = jnp.cumsum(lengths)
    position = jnp.arange(row_count, dtype=jnp.int32)
    segment = jnp.sum((position[:, None] >= doc_ends[None, :]).astype(jnp.int32), axis=1)
    causal = position[None, :] <= position[:, None]
    return jnp.logical_and(segment[:, None] == segment[None, :], causal)


def split_heads(matrix, head_count):
    row_count, features = matrix.shape
    return matrix.reshape(row_count, head_count, features // head_count)


def times_transposed(left, matrix):
    return lax.dot_general(
        left, matrix, (((1,), (1,)), ((), ())), preferred_element_type=jnp.float32
    )


def masked_scores(query_heads, key_heads, visible, score_scale):
    scores = (
        jnp.einsum("qhd,khd->hqk", query_heads, key_heads, preferred_element_type=jnp.float32)
        * score_scale
    )
    return jnp.where(visible[None], scores, -1e30)


def forward_block(hidden, params, visible, head_count):
    (
        heads_weight,
        merge_weight,
        up_weight,
        down_weight,
        first_gain,
        first_shift,
        query_bias,
        value_bias,
        output_bias,
        second_gain,
        second_shift,
        up_bias,
        down_bias,
    ) = params
    row_count, features = hidden.shape
    score_scale = 1.0 / math.sqrt(features // head_count)
    normed = norm_rows(hidden, first_gain, first_shift).astype(jnp.bfloat16)
    joint_bias = jnp.concatenate([query_bias, jnp.zeros_like(query_bias), value_bias])
    joint_rows = (
        jnp.dot(normed, heads_weight, preferred_element_type=jnp.float32) + joint_bias
    ).astype(jnp.bfloat16)
    query_heads = split_heads(joint_rows[:, :features], head_count)
    key_heads = split_heads(joint_rows[:, features : 2 * features], head_count)
    value_heads = split_heads(joint_rows[:, 2 * features :], head_count)
    scores = masked_scores(query_heads, key_heads, visible, score_scale)
    row_top = jnp.max(scores, axis=-1, keepdims=True)
    log_total = row_top + jnp.log(jnp.sum(jnp.exp(scores - row_top), axis=-1, keepdims=True))
    softmax_low = jnp.exp(scores - log_total).astype(jnp.bfloat16)
    attended = jnp.einsum(
        "hqk,khd->qhd", softmax_low, value_heads, preferred_element_type=jnp.float32
    )
    attended = attended.reshape(row_count, features).astype(jnp.bfloat16)
    middle = (
        hidden + jnp.dot(attended, merge_weight, preferred_element_type=jnp.float32) + output_bias
    )
    second = norm_rows(middle, second_gain, second_shift).astype(jnp.bfloat16)
    before = jnp.dot(second, up_weight, preferred_element_type=jnp.float32) + up_bias
    active = gelu_tanh(before).astype(jnp.bfloat16)
    result = middle + jnp.dot(active, down_weight, preferred_element_type=jnp.float32) + down_bias
    return (result, (normed, joint_rows, log_total, attended, middle, second, before, active))


def backward_block(hidden, grad_out, kept_state, params, visible, head_count):
    (
        heads_weight,
        merge_weight,
        up_weight,
        down_weight,
        first_gain,
        first_shift,
        query_bias,
        value_bias,
        output_bias,
        second_gain,
        second_shift,
        up_bias,
        down_bias,
    ) = params
    normed, joint_rows, log_total, attended, middle, second, before, active = kept_state
    row_count, features = hidden.shape
    score_scale = 1.0 / math.sqrt(features // head_count)
    grad_down_in = grad_out.astype(jnp.bfloat16)
    grad_active = times_transposed(grad_down_in, down_weight)
    unused_out, gelu_back = jax.vjp(gelu_tanh, before)
    grad_before = gelu_back(grad_active)[0].astype(jnp.bfloat16)
    grad_second = times_transposed(grad_before, up_weight)
    unused_norm, second_back = jax.vjp(norm_rows, middle, second_gain, second_shift)
    grad_middle_norm, grad_second_gain, grad_second_shift = second_back(grad_second)
    grad_middle = grad_out + grad_middle_norm
    grad_merge_in = grad_middle.astype(jnp.bfloat16)
    grad_attended = times_transposed(grad_merge_in, merge_weight).astype(jnp.bfloat16)
    query_heads = split_heads(joint_rows[:, :features], head_count)
    key_heads = split_heads(joint_rows[:, features : 2 * features], head_count)
    value_heads = split_heads(joint_rows[:, 2 * features :], head_count)
    scores = masked_scores(query_heads, key_heads, visible, score_scale)
    softmax_full = jnp.exp(scores - log_total)
    softmax_low = softmax_full.astype(jnp.bfloat16)
    grad_heads_out = split_heads(grad_attended, head_count)
    grad_probs = jnp.einsum(
        "qhd,khd->hqk", grad_heads_out, value_heads, preferred_element_type=jnp.float32
    )
    row_inner = jnp.sum(softmax_full * grad_probs, axis=-1, keepdims=True)
    grad_scores = (softmax_full * (grad_probs - row_inner)).astype(jnp.bfloat16)
    grad_query = (
        jnp.einsum("hqk,khd->qhd", grad_scores, key_heads, preferred_element_type=jnp.float32)
        * score_scale
    )
    grad_keys = (
        jnp.einsum("hqk,qhd->khd", grad_scores, query_heads, preferred_element_type=jnp.float32)
        * score_scale
    )
    grad_values = jnp.einsum(
        "hqk,qhd->khd", softmax_low, grad_heads_out, preferred_element_type=jnp.float32
    )
    grad_joint = jnp.concatenate(
        [
            grad_query.reshape(row_count, features),
            grad_keys.reshape(row_count, features),
            grad_values.reshape(row_count, features),
        ],
        axis=1,
    ).astype(jnp.bfloat16)
    grad_normed = times_transposed(grad_joint, heads_weight)
    unused_first, first_back = jax.vjp(norm_rows, hidden, first_gain, first_shift)
    grad_hidden_norm, grad_first_gain, grad_first_shift = first_back(grad_normed)
    grad_hidden = grad_middle + grad_hidden_norm
    joint_sums = jnp.sum(grad_joint.astype(jnp.float32), axis=0)
    vector_sums = (
        grad_first_gain,
        grad_first_shift,
        joint_sums[:features],
        joint_sums[2 * features :],
        jnp.sum(grad_merge_in.astype(jnp.float32), axis=0),
        grad_second_gain,
        grad_second_shift,
        jnp.sum(grad_before.astype(jnp.float32), axis=0),
        jnp.sum(grad_down_in.astype(jnp.float32), axis=0),
    )
    return (grad_hidden, vector_sums, (grad_joint, grad_merge_in, grad_before, grad_down_in))


def select_turn(stacked, position):
    return jax.tree.map(
        lambda leaf_array: lax.dynamic_index_in_dim(leaf_array, position, 0, keepdims=False),
        stacked,
    )


def stack_all(items):
    return jax.tree.map(lambda *leaf_arrays: jnp.stack(leaf_arrays), *items)


def outer_sum(left, right):
    return jnp.einsum("rd,re->de", left, right, preferred_element_type=jnp.float32)


def body(
    tokens,
    doc_lengths,
    heads_weight,
    merge_weight,
    up_weight,
    down_weight,
    first_gain,
    first_shift,
    query_bias,
    value_bias,
    output_bias,
    second_gain,
    second_shift,
    up_bias,
    down_bias,
    cotangent,
):
    section_count = lax.axis_size("section")
    section_index = lax.axis_index("section")
    gathered = (
        lax.all_gather(heads_weight, "shard", axis=1, tiled=True),
        lax.all_gather(merge_weight, "shard", axis=1, tiled=True),
        lax.all_gather(up_weight, "shard", axis=1, tiled=True),
        lax.all_gather(down_weight, "shard", axis=1, tiled=True),
        lax.all_gather(first_gain, "shard", axis=1, tiled=True),
        lax.all_gather(first_shift, "shard", axis=1, tiled=True),
        lax.all_gather(query_bias, "shard", axis=1, tiled=True),
        lax.all_gather(value_bias, "shard", axis=1, tiled=True),
        lax.all_gather(output_bias, "shard", axis=1, tiled=True),
        lax.all_gather(second_gain, "shard", axis=1, tiled=True),
        lax.all_gather(second_shift, "shard", axis=1, tiled=True),
        lax.all_gather(up_bias, "shard", axis=1, tiled=True),
        lax.all_gather(down_bias, "shard", axis=1, tiled=True),
    )
    params = tuple((shard_piece[0] for shard_piece in gathered[:4])) + tuple(
        (shard_piece[0].astype(jnp.float32) for shard_piece in gathered[4:])
    )
    batch_count = doc_lengths.shape[0]
    row_count = tokens.shape[0] // batch_count
    features = tokens.shape[1]
    tick_count = batch_count + section_count - 1
    visible_all = jnp.stack(
        [visible_mask(doc_lengths[number], row_count) for number in range(batch_count)]
    )
    local_inputs = tokens.reshape(batch_count, row_count, features)
    local_cotangent = cotangent.reshape(batch_count, row_count, features)
    first_section = section_index == 0
    last_section = section_index == section_count - 1
    incoming = jnp.zeros((row_count, features), jnp.bfloat16)
    kept_inputs, kept_states, sent_outputs = ([], [], [])
    for turn_number in range(tick_count):
        batch_index = jnp.clip(turn_number - section_index, 0, batch_count - 1)
        own_rows = local_inputs[min(turn_number, batch_count - 1)]
        arriving = jnp.where(first_section, own_rows, incoming)
        visible = select_turn(visible_all, batch_index)
        result, kept_state = forward_block(arriving.astype(jnp.float32), params, visible, HEADS)
        outgoing = result.astype(jnp.bfloat16)
        kept_inputs.append(arriving)
        kept_states.append(kept_state)
        sent_outputs.append(outgoing)
        if turn_number + 1 < tick_count:
            incoming = shifted(outgoing, "section", 1)
    inputs_stack = jnp.stack(kept_inputs)
    states_stack = stack_all(kept_states)
    outputs_stack = jnp.stack(sent_outputs)
    incoming = jnp.zeros((row_count, features), jnp.bfloat16)
    grad_sent, small_sums, product_pairs = ([], [], [])
    for turn_number in range(tick_count):
        batch_index = jnp.clip(
            turn_number - (section_count - 1 - section_index), 0, batch_count - 1
        )
        forward_turn = batch_index + section_index
        own_grad = local_cotangent[min(turn_number, batch_count - 1)]
        arriving = jnp.where(last_section, own_grad, incoming)
        visible = select_turn(visible_all, batch_index)
        hidden = select_turn(inputs_stack, forward_turn).astype(jnp.float32)
        kept_state = select_turn(states_stack, forward_turn)
        grad_hidden, vector_sums, pairs = backward_block(
            hidden, arriving.astype(jnp.float32), kept_state, params, visible, HEADS
        )
        outgoing = grad_hidden.astype(jnp.bfloat16)
        grad_sent.append(outgoing)
        small_sums.append(vector_sums)
        product_pairs.append(pairs)
        if turn_number + 1 < tick_count:
            incoming = shifted(outgoing, "section", -1)
    grads_stack = jnp.stack(grad_sent)
    sums_stack = stack_all(small_sums)
    pairs_stack = stack_all(product_pairs)
    output_turns = [number + section_index for number in range(batch_count)]
    back_turns = [number + section_count - 1 - section_index for number in range(batch_count)]
    activations = jnp.concatenate(
        [select_turn(outputs_stack, turn_value) for turn_value in output_turns], axis=0
    )[None]
    input_grads = jnp.concatenate(
        [select_turn(grads_stack, turn_value) for turn_value in back_turns], axis=0
    )[None]
    forward_saved = [select_turn(states_stack, turn_value) for turn_value in output_turns]
    backward_saved = [select_turn(pairs_stack, turn_value) for turn_value in back_turns]
    normed_rows = jnp.concatenate([saved[0] for saved in forward_saved], axis=0)
    attended_rows = jnp.concatenate([saved[3] for saved in forward_saved], axis=0)
    second_rows = jnp.concatenate([saved[5] for saved in forward_saved], axis=0)
    active_rows = jnp.concatenate([saved[7] for saved in forward_saved], axis=0)
    joint_grads = jnp.concatenate([saved[0] for saved in backward_saved], axis=0)
    merge_grads = jnp.concatenate([saved[1] for saved in backward_saved], axis=0)
    before_grads = jnp.concatenate([saved[2] for saved in backward_saved], axis=0)
    down_grads = jnp.concatenate([saved[3] for saved in backward_saved], axis=0)
    picked_sums = [select_turn(sums_stack, turn_value) for turn_value in back_turns]
    vector_grads = jax.tree.map(lambda *leaf_arrays: reduce(jnp.add, leaf_arrays), *picked_sums)
    grad_heads = outer_sum(normed_rows, joint_grads)[None]
    grad_merge = outer_sum(attended_rows, merge_grads)[None]
    grad_up = outer_sum(second_rows, before_grads)[None]
    grad_down = outer_sum(active_rows, down_grads)[None]
    (
        grad_first_gain,
        grad_first_shift,
        grad_query,
        grad_value,
        grad_output,
        grad_second_gain,
        grad_second_shift,
        grad_up_bias,
        grad_down_bias,
    ) = tuple((vector_part[None] for vector_part in vector_grads))
    group_parts = (
        lax.psum_scatter(
            grad_heads.astype(jnp.bfloat16), "shard", scatter_dimension=1, tiled=True
        ).astype(jnp.float32),
        lax.psum_scatter(
            grad_merge.astype(jnp.bfloat16), "shard", scatter_dimension=1, tiled=True
        ).astype(jnp.float32),
        lax.psum_scatter(
            grad_up.astype(jnp.bfloat16), "shard", scatter_dimension=1, tiled=True
        ).astype(jnp.float32),
        lax.psum_scatter(
            grad_down.astype(jnp.bfloat16), "shard", scatter_dimension=1, tiled=True
        ).astype(jnp.float32),
        lax.psum_scatter(
            grad_first_gain.astype(jnp.bfloat16), "shard", scatter_dimension=1, tiled=True
        ).astype(jnp.float32),
        lax.psum_scatter(
            grad_first_shift.astype(jnp.bfloat16), "shard", scatter_dimension=1, tiled=True
        ).astype(jnp.float32),
        lax.psum_scatter(
            grad_query.astype(jnp.bfloat16), "shard", scatter_dimension=1, tiled=True
        ).astype(jnp.float32),
        lax.psum_scatter(
            grad_value.astype(jnp.bfloat16), "shard", scatter_dimension=1, tiled=True
        ).astype(jnp.float32),
        lax.psum_scatter(
            grad_output.astype(jnp.bfloat16), "shard", scatter_dimension=1, tiled=True
        ).astype(jnp.float32),
        lax.psum_scatter(
            grad_second_gain.astype(jnp.bfloat16), "shard", scatter_dimension=1, tiled=True
        ).astype(jnp.float32),
        lax.psum_scatter(
            grad_second_shift.astype(jnp.bfloat16), "shard", scatter_dimension=1, tiled=True
        ).astype(jnp.float32),
        lax.psum_scatter(
            grad_up_bias.astype(jnp.bfloat16), "shard", scatter_dimension=1, tiled=True
        ).astype(jnp.float32),
        lax.psum_scatter(
            grad_down_bias.astype(jnp.bfloat16), "shard", scatter_dimension=1, tiled=True
        ).astype(jnp.float32),
    )
    reduced = (
        lax.psum(group_parts[0].astype(jnp.bfloat16), "rep").astype(jnp.float32),
        lax.psum(group_parts[1].astype(jnp.bfloat16), "rep").astype(jnp.float32),
        lax.psum(group_parts[2].astype(jnp.bfloat16), "rep").astype(jnp.float32),
        lax.psum(group_parts[3].astype(jnp.bfloat16), "rep").astype(jnp.float32),
        lax.psum(group_parts[4].astype(jnp.bfloat16), "rep").astype(jnp.float32),
        lax.psum(group_parts[5].astype(jnp.bfloat16), "rep").astype(jnp.float32),
        lax.psum(group_parts[6].astype(jnp.bfloat16), "rep").astype(jnp.float32),
        lax.psum(group_parts[7].astype(jnp.bfloat16), "rep").astype(jnp.float32),
        lax.psum(group_parts[8].astype(jnp.bfloat16), "rep").astype(jnp.float32),
        lax.psum(group_parts[9].astype(jnp.bfloat16), "rep").astype(jnp.float32),
        lax.psum(group_parts[10].astype(jnp.bfloat16), "rep").astype(jnp.float32),
        lax.psum(group_parts[11].astype(jnp.bfloat16), "rep").astype(jnp.float32),
        lax.psum(group_parts[12].astype(jnp.bfloat16), "rep").astype(jnp.float32),
    )
    return (activations, input_grads) + tuple(reduced)


def solution(mesh):
    return jax.shard_map(
        body,
        mesh=mesh,
        in_specs=(
            P(("shard", "rep"), None),
            P(("shard", "rep"), None),
            P("section", "shard", None),
            P("section", "shard", None),
            P("section", "shard", None),
            P("section", "shard", None),
            P("section", "shard"),
            P("section", "shard"),
            P("section", "shard"),
            P("section", "shard"),
            P("section", "shard"),
            P("section", "shard"),
            P("section", "shard"),
            P("section", "shard"),
            P("section", "shard"),
            P(("shard", "rep"), None),
        ),
        out_specs=(
            P("section", ("shard", "rep"), None),
            P("section", ("shard", "rep"), None),
            P("section", "shard", None),
            P("section", "shard", None),
            P("section", "shard", None),
            P("section", "shard", None),
            P("section", "shard"),
            P("section", "shard"),
            P("section", "shard"),
            P("section", "shard"),
            P("section", "shard"),
            P("section", "shard"),
            P("section", "shard"),
            P("section", "shard"),
            P("section", "shard"),
        ),
        check_vma=False,
    )
```

profile of v0, /device:TPU:0, one launch (start us, length us, event | category | flops | bytes accessed | tf_op | source)
XLA Modules:
  0.0 1431.8 jit_solution(3994880810439041070)
XLA Ops:
  10.5 12.6 all_gather.39
  23.1 7.7 all_gather.40
  30.9 11.4 all_gather.42
  42.3 8.5 all_gather.43
  50.8 10.3 all_gather.45
  61.1 8.5 all_gather.46
  69.6 9.9 all_gather.47
  79.6 8.5 all_gather.51
  88.0 16.6 %all_gather.49 = bf16[1,4096]{1,0:T(2,128)(2,1)S(1)} all-gather(bf16[1,1024]{1,0:T(2,128)(2,1)S(1)} %copy-done.142), channel_id=1, replica_groups=mesh['section'=2,'shard'=4,'rep'=4] {'shard'}, dimensions={1}, use_global_device_ids=true | all-gather | bytes 10240 | tf_op jit(solution)/shard_map/all_gather | solution.py:234
  106.0 22.3 %all-gather.5.cloned.1.call-done = bf16[1,1024,3072]{2,1,0:T(8,128)(2,1)} async-done(((bf16[1,256,3072]{2,1,0:T(8,128)(2,1)}), bf16[1,1024,3072]{2,1,0:T(8,128)(2,1)}) %all-gather.5.cloned.1.call-update) | async-done | bytes 6291472 | tf_op jit(solution)/shard_map/all_gather | solution.py:223
  128.3 4.0 fusion.60
  134.5 39.5 %all-gather.7.cloned.1.call-done = bf16[1,1024,1024]{2,1,0:T(8,128)(2,1)} async-done(((bf16[1,256,1024]{2,1,0:T(8,128)(2,1)}), bf16[1,1024,1024]{2,1,0:T(8,128)(2,1)}) %all-gather.7.cloned.1.call-update) | async-done | bytes 2097168 | tf_op jit(solution)/shard_map/all_gather | solution.py:224
  176.5 147.5 %all-gather.9.cloned.1.call-done = bf16[1,1024,4096]{2,1,0:T(8,128)(2,1)} async-done(((bf16[1,256,4096]{2,1,0:T(8,128)(2,1)}), bf16[1,1024,4096]{2,1,0:T(8,128)(2,1)}) %all-gather.9.cloned.1.call-update) | async-done | bytes 8388624 | tf_op jit(solution)/shard_map/all_gather | solution.py:225
  324.0 4.9 fusion.36
  328.9 144.4 %all-gather.11.cloned.1.call-done = bf16[1,4096,1024]{2,1,0:T(8,128)(2,1)} async-done(((bf16[1,1024,1024]{2,1,0:T(8,128)(2,1)}), bf16[1,4096,1024]{2,1,0:T(8,128)(2,1)}) %all-gather.11.cloned.1.call-update) | async-done | bytes 8388624 | tf_op jit(solution)/shard_map/all_gather | solution.py:226
  473.3 4.9 fusion.195
  478.2 2.6 collective-permute-start
  481.6 4.0 fusion.57
  492.9 5.1 fusion.39
  522.8 5.1 fusion.42
  530.0 9.6 convert_reduce_fusion.2
  539.7 3.5 multiply_reduce_fusion.5
  571.2 5.7 fusion.236
  582.3 8.1 convert_reduce_fusion.1
  590.5 3.4 multiply_reduce_fusion.4
  604.1 5.7 fusion.245
  614.9 8.1 convert_reduce_fusion
  623.0 3.4 multiply_reduce_fusion.3
  633.6 6.0 fusion.254
  641.4 4.2 maximum_maximum_fusion
  645.7 5.2 convert_bitcast_fusion.2
  656.3 5.6 convert_bitcast_fusion
  665.6 5.7 convert_bitcast_fusion.1
  684.5 100.4 %reduce-scatter.32.cloned.1.call-done = bf16[1,256,3072]{2,1,0:T(8,128)(2,1)} async-done(((bf16[1,1024,3072]{2,1,0:T(8,128)(2,1)}), bf16[1,256,3072]{2,1,0:T(8,128)(2,1)}) %reduce-scatter.32.cloned.1.call-update) | async-done | bytes 1572880 | tf_op jit(solution)/shard_map/reduce_scatter | solution.py:328
  784.9 147.5 %reduce-scatter.38.cloned.1.call-done = bf16[1,1024,1024]{2,1,0:T(8,128)(2,1)} async-done(((bf16[1,4096,1024]{2,1,0:T(8,128)(2,1)}), bf16[1,1024,1024]{2,1,0:T(8,128)(2,1)}) %reduce-scatter.38.cloned.1.call-update) | async-done | bytes 2097168 | tf_op jit(solution)/shard_map/reduce_scatter | solution.py:337
  932.4 147.7 %reduce-scatter.36.cloned.1.call-done = bf16[1,256,4096]{2,1,0:T(8,128)(2,1)} async-done(((bf16[1,1024,4096]{2,1,0:T(8,128)(2,1)}), bf16[1,256,4096]{2,1,0:T(8,128)(2,1)}) %reduce-scatter.36.cloned.1.call-update) | async-done | bytes 2097168 | tf_op jit(solution)/shard_map/reduce_scatter | solution.py:334
  1081.1 4.9 fusion.207
  1088.2 14.6 %reduce-scatter.48.cloned.1.call-done = bf16[256,1]{1,0:T(8,128)(2,1)} async-done(((bf16[1024,1]{1,0:T(8,128)(2,1)}), bf16[256,1]{1,0:T(8,128)(2,1)}) %reduce-scatter.48.cloned.1.call-update) | async-done | bytes 528
  1103.7 19.1 %reduce-scatter.52.cloned.1.call-done = bf16[256,1]{1,0:T(8,128)(2,1)} async-done(((bf16[1024,1]{1,0:T(8,128)(2,1)}), bf16[256,1]{1,0:T(8,128)(2,1)}) %reduce-scatter.52.cloned.1.call-update) | async-done | bytes 528
  1123.7 19.4 %reduce-scatter.50.cloned.1.call-done = bf16[256,1]{1,0:T(8,128)(2,1)} async-done(((bf16[1024,1]{1,0:T(8,128)(2,1)}), bf16[256,1]{1,0:T(8,128)(2,1)}) %reduce-scatter.50.cloned.1.call-update) | async-done | bytes 528
  1144.1 19.1 %reduce-scatter.56.cloned.1.call-done = bf16[256,1]{1,0:T(8,128)(2,1)} async-done(((bf16[1024,1]{1,0:T(8,128)(2,1)}), bf16[256,1]{1,0:T(8,128)(2,1)}) %reduce-scatter.56.cloned.1.call-update) | async-done | bytes 528
  1164.0 19.4 %reduce-scatter.46.cloned.1.call-done = bf16[256,1]{1,0:T(8,128)(2,1)} async-done(((bf16[1024,1]{1,0:T(8,128)(2,1)}), bf16[256,1]{1,0:T(8,128)(2,1)}) %reduce-scatter.46.cloned.1.call-update) | async-done | bytes 528
  1184.4 19.1 %reduce-scatter.44.cloned.1.call-done = bf16[256,1]{1,0:T(8,128)(2,1)} async-done(((bf16[1024,1]{1,0:T(8,128)(2,1)}), bf16[256,1]{1,0:T(8,128)(2,1)}) %reduce-scatter.44.cloned.1.call-update) | async-done | bytes 528
  1204.4 19.9 %reduce-scatter.42.cloned.1.call-done = bf16[256,1]{1,0:T(8,128)(2,1)} async-done(((bf16[1024,1]{1,0:T(8,128)(2,1)}), bf16[256,1]{1,0:T(8,128)(2,1)}) %reduce-scatter.42.cloned.1.call-update) | async-done | bytes 528
  1225.2 19.7 %reduce-scatter.40.cloned.1.call-done = bf16[256,1]{1,0:T(8,128)(2,1)} async-done(((bf16[1024,1]{1,0:T(8,128)(2,1)}), bf16[256,1]{1,0:T(8,128)(2,1)}) %reduce-scatter.40.cloned.1.call-update) | async-done | bytes 528
  1245.8 27.4 %reduce-scatter.54.cloned.1.call-done = bf16[1024,1]{1,0:T(8,128)(2,1)} async-done(((bf16[4096,1]{1,0:T(8,128)(2,1)}), bf16[1024,1]{1,0:T(8,128)(2,1)}) %reduce-scatter.54.cloned.1.call-update) | async-done | bytes 2064
  1274.3 16.4 %all-reduce = (bf16[1,256]{1,0:T(2,128)(2,1)S(1)}, bf16[1,256]{1,0:T(2,128)(2,1)S(1)}, bf16[1,256]{1,0:T(2,128)(2,1)S(1)}, bf16[1,256]{1,0:T(2,128)(2,1)S(1)}, b...) all-reduce(bf16[1,256]{1,0:T(2,128)(2,1)S(1)} %copy.170, ...), channel_id=1, replica_groups=mesh['section'=2,'shard'=4,'rep'=4] {'rep'}, use_global_device_ids=true, to_apply=%region_61.62 | all-reduce | flops 3072 | bytes 12288 | tf_op jit(solution)/shard_map/psum | solution.py:373
  1295.9 119.3 %all-reduce.4.cloned.1.call-done = (bf16[1,256,3072]{2,1,0:T(8,128)(2,1)}, bf16[1,256,1024]{2,1,0:T(8,128)(2,1)}, bf16[1,256,4096]{2,1,0:T(8,128)(2,1)}, bf16[1,1024,1024]{2,1,0:T(8,128)(2,1)}) async-done(((bf16[1,256,3072]{2,1,0:T(8,128)(2,1)}, bf16[1,256,1024]{2,1,0:T(8,128)(2,1)}, bf16[1,256,4096]{2,1,0:T(8,128)(2,1)}, bf16[1,1024,1024]{2,1,0:T(8,128)(2,1)}), (bf16[1,256,3072]{2,1,0:T(8,128)(2,1)}, ...) | async-done | bytes 6291472 | tf_op jit(solution)/shard_map/psum | solution.py:369
  (634 shorter events, 148.1 us)
Async XLA Ops:
  7.2 121.1 %all-gather.5.cloned.1.call-start = ((), (), s32[]{:S(2)}) async-start(), calls=%async_computation.13 | async-start | bytes 7864320 | tf_op jit(solution)/shard_map/all_gather | solution.py:223
  7.9 166.1 %all-gather.7.cloned.1.call-start = ((), (), s32[]{:S(2)}) async-start(), calls=%async_computation.14 | async-start | bytes 2621440 | tf_op jit(solution)/shard_map/all_gather | solution.py:224
  8.7 315.3 %all-gather.9.cloned.1.call-start = ((), (), s32[]{:S(2)}) async-start(), calls=%async_computation.15 | async-start | bytes 10485760 | tf_op jit(solution)/shard_map/all_gather | solution.py:225
  9.4 13.7 copy-start.157
  9.4 21.5 %copy-start.158 = (bf16[1,256]{1,0:T(2,128)(2,1)S(1)}, bf16[1,256]{1,0:T(2,128)(2,1)}, u32[]{:S(2)}) copy-start(bf16[1,256]{1,0:T(2,128)(2,1)} %param.24) | copy-start | bytes 1540
  9.4 32.8 %copy-start.159 = (bf16[1,256]{1,0:T(2,128)(2,1)S(1)}, bf16[1,256]{1,0:T(2,128)(2,1)}, u32[]{:S(2)}) copy-start(bf16[1,256]{1,0:T(2,128)(2,1)} %param.25) | copy-start | bytes 1540
  9.5 41.3 %copy-start.160 = (bf16[1,256]{1,0:T(2,128)(2,1)S(1)}, bf16[1,256]{1,0:T(2,128)(2,1)}, u32[]{:S(2)}) copy-start(bf16[1,256]{1,0:T(2,128)(2,1)} %param.26) | copy-start | bytes 1540
  9.5 51.6 %copy-start.161 = (bf16[1,256]{1,0:T(2,128)(2,1)S(1)}, bf16[1,256]{1,0:T(2,128)(2,1)}, u32[]{:S(2)}) copy-start(bf16[1,256]{1,0:T(2,128)(2,1)} %param.27) | copy-start | bytes 1540
  9.5 60.2 %copy-start.162 = (bf16[1,256]{1,0:T(2,128)(2,1)S(1)}, bf16[1,256]{1,0:T(2,128)(2,1)}, u32[]{:S(2)}) copy-start(bf16[1,256]{1,0:T(2,128)(2,1)} %param.28) | copy-start | bytes 1540
  9.5 70.1 %copy-start.163 = (bf16[1,256]{1,0:T(2,128)(2,1)S(1)}, bf16[1,256]{1,0:T(2,128)(2,1)}, u32[]{:S(2)}) copy-start(bf16[1,256]{1,0:T(2,128)(2,1)} %param.30) | copy-start | bytes 1540
  9.5 78.5 %copy-start.142 = (bf16[1,1024]{1,0:T(2,128)(2,1)S(1)}, bf16[1,1024]{1,0:T(2,128)(2,1)}, u32[]{:S(2)}) copy-start(bf16[1,1024]{1,0:T(2,128)(2,1)} %param.29) | copy-start | bytes 6148
  9.5 96.2 %copy-start.22 = (bf16[192,1024]{1,0:T(8,128)(2,1)S(1)}, bf16[192,1024]{1,0:T(8,128)(2,1)}, u32[]{:S(2)}) copy-start(bf16[192,1024]{1,0:T(8,128)(2,1)} %param.16) | copy-start | bytes 1179652
  9.5 463.8 %all-gather.11.cloned.1.call-start = ((), (), s32[]{:S(2)}) async-start(), calls=%async_computation.16 | async-start | bytes 10485760 | tf_op jit(solution)/shard_map/all_gather | solution.py:226
  10.1 674.5 %reduce-scatter.34.cloned.1.call-start = ((), (), s32[]{:S(2)}) async-start(), calls=%async_computation.18 | async-start | bytes 2621440 | tf_op jit(solution)/shard_map/reduce_scatter | solution.py:331
  88.0 385.3 %copy-start.146 = (f32[1,1024]{1,0:T(1,128)}, f32[1,1024]{1,0:T(1,128)S(1)}, u32[]{:S(2)}) copy-start(f32[1,1024]{1,0:T(1,128)S(1)} %add.670) | copy-start | bytes 12292
  105.8 26.5 %copy-start.132 = (f32[96]{0:T(128)}, f32[96]{0:T(128)S(1)}, u32[]{:S(2)}) copy-start(f32[96]{0:T(128)S(1)} %broadcast_multiply_fusion.11) | copy-start | bytes 1156
  106.0 26.3 %copy-start.149 = (f32[96]{0:T(128)}, f32[96]{0:T(128)S(1)}, u32[]{:S(2)}) copy-start(f32[96]{0:T(128)S(1)} %add_rsqrt_fusion.5) | copy-start | bytes 1156
  134.5 41.9 %copy-start.81 = (bf16[16,64,96]{2,1,0:T(8,128)(2,1)}, bf16[16,64,96]{2,1,0:T(8,128)(2,1)S(1)}, u32[]{:S(2)}) copy-start(bf16[16,64,96]{2,1,0:T(8,128)(2,1)S(1)} %convolution_convert_fusion.5) | copy-start | bytes 589828
  176.2 297.1 %copy-start.13 = (f32[96,1024]{1,0:T(8,128)}, f32[96,1024]{1,0:T(8,128)S(1)}, u32[]{:S(2)}) copy-start(f32[96,1024]{1,0:T(8,128)S(1)} %get-tuple-element.158) | copy-start | bytes 1179652
  176.5 152.5 %copy-start.130 = (f32[96]{0:T(128)}, f32[96]{0:T(128)S(1)}, u32[]{:S(2)}) copy-start(f32[96]{0:T(128)S(1)} %add_rsqrt_fusion.4) | copy-start | bytes 1156
  328.9 149.3 %copy-start.3 = (f32[96,4096]{1,0:T(8,128)}, f32[96,4096]{1,0:T(8,128)S(1)}, u32[]{:S(2)}) copy-start(f32[96,4096]{1,0:T(8,128)S(1)} %fusion.36) | copy-start | bytes 4718596
  478.2 3.0 collective-permute-start
  492.9 11.3 slice-start.6
  499.6 3.3 collective-permute-start.1
  503.9 17.2 %copy-start.19 = (bf16[96,1024]{1,0:T(8,128)(2,1)}, bf16[96,1024]{1,0:T(8,128)(2,1)S(1)}, u32[]{:S(2)}) copy-start(bf16[96,1024]{1,0:T(8,128)(2,1)S(1)} %get-tuple-element.77) | copy-start | bytes 589828
  521.7 21.5 %copy-start.9 = (f32[96,1024]{1,0:T(8,128)}, f32[96,1024]{1,0:T(8,128)S(1)}, u32[]{:S(2)}) copy-start(f32[96,1024]{1,0:T(8,128)S(1)} %get-tuple-element.166) | copy-start | bytes 1179652
  522.6 17.1 %copy-start.134 = (f32[96]{0:T(128)}, f32[96]{0:T(128)S(1)}, u32[]{:S(2)}) copy-start(f32[96]{0:T(128)S(1)} %broadcast_multiply_fusion.3) | copy-start | bytes 1156
  529.0 10.6 slice-start
  530.0 9.6 slice-start.1
  578.2 3.5 collective-permute-start.2
  579.6 10.8 slice-start.2
  582.3 11.8 copy-start.38
  604.1 18.9 %slice-start.4 = ((s8[8388608]{0:T(1024)(128)(4,1)}), s8[4194304]{0:T(1024)(128)(4,1)S(1)}, s32[]{:S(2)}) async-start(s8[8388608]{0:T(1024)(128)(4,1)} %bitcast.641), calls=%async_computation.35 | async-start | bytes 8388608
  610.9 3.3 collective-permute-start.3
  614.9 11.8 copy-start.41
  630.4 154.5 %reduce-scatter.32.cloned.1.call-start = ((), (), s32[]{:S(2)}) async-start(), calls=%async_computation.17 | async-start | bytes 7864320 | tf_op jit(solution)/shard_map/reduce_scatter | solution.py:328
  651.0 281.4 %reduce-scatter.38.cloned.1.call-start = ((), (), s32[]{:S(2)}) async-start(), calls=%async_computation.20 | async-start | bytes 10485760 | tf_op jit(solution)/shard_map/reduce_scatter | solution.py:337
  662.0 418.1 %reduce-scatter.36.cloned.1.call-start = ((), (), s32[]{:S(2)}) async-start(), calls=%async_computation.19 | async-start | bytes 10485760 | tf_op jit(solution)/shard_map/reduce_scatter | solution.py:334
  671.4 431.4 %reduce-scatter.48.cloned.1.call-start = ((), (), s32[]{:S(2)}) async-start(), calls=%async_computation.25 | async-start | bytes 327680
  675.5 447.4 %reduce-scatter.52.cloned.1.call-start = ((), (), s32[]{:S(2)}) async-start(), calls=%async_computation.27 | async-start | bytes 327680
  676.5 466.7 %reduce-scatter.50.cloned.1.call-start = ((), (), s32[]{:S(2)}) async-start(), calls=%async_computation.26 | async-start | bytes 327680
  677.5 485.6 %reduce-scatter.56.cloned.1.call-start = ((), (), s32[]{:S(2)}) async-start(), calls=%async_computation.29 | async-start | bytes 327680
  678.6 504.9 %reduce-scatter.46.cloned.1.call-start = ((), (), s32[]{:S(2)}) async-start(), calls=%async_computation.24 | async-start | bytes 327680
  679.6 523.9 %reduce-scatter.44.cloned.1.call-start = ((), (), s32[]{:S(2)}) async-start(), calls=%async_computation.23 | async-start | bytes 327680
  680.6 543.7 %reduce-scatter.42.cloned.1.call-start = ((), (), s32[]{:S(2)}) async-start(), calls=%async_computation.22 | async-start | bytes 327680
  681.6 563.3 %reduce-scatter.40.cloned.1.call-start = ((), (), s32[]{:S(2)}) async-start(), calls=%async_computation.21 | async-start | bytes 327680
  682.6 590.6 %reduce-scatter.54.cloned.1.call-start = ((), (), s32[]{:S(2)}) async-start(), calls=%async_computation.28 | async-start | bytes 1310720
  684.2 731.0 %all-reduce.4.cloned.1.call-start = ((), (), s32[]{:S(2)}) async-start(), calls=%async_computation.30 | async-start | bytes 12582912 | tf_op jit(solution)/shard_map/psum | solution.py:369
  (151 other events, 481.7 us)
Sparse Core Ops, SparseCore 0:
  9.6 118.6 all-gather.4
  129.9 44.0 all-gather.6
  175.6 148.3 all-gather.8
  325.4 147.8 all-gather.10
  630.5 42.0 reduce-scatter.33
  674.8 110.0 reduce-scatter.31
  787.4 144.9 reduce-scatter.37
  934.9 145.1 reduce-scatter.35
  1082.5 20.2 reduce-scatter.47
  1104.9 17.8 reduce-scatter.51
  1125.2 17.9 reduce-scatter.49
  1145.3 17.8 reduce-scatter.55
  1165.5 17.9 reduce-scatter.45
  1185.6 17.8 reduce-scatter.43
  1206.2 18.0 reduce-scatter.41
  1227.0 17.8 reduce-scatter.39
  1247.7 25.4 reduce-scatter.53
  1276.9 138.2 all-reduce.3
where the time goes:
time: 1440 us; the launch traced here: 1430 us
  waiting for transfers between devices  1050 us (73%)
  matrix products  131 us (9%)
  blocking collectives  110 us (8%)
  local copies, waits for them, and re-layouts  68 us (5%)
  other arithmetic  43.2 us (3%)
  between operations  17.2 us (1%)
    unnamed x27, waiting for transfers between devices  181 us
    reduce_scatter x1, waiting for transfers between devices, body(): lax.psum_scatter(grad_up.astype(jnp.bfloat16), 'shard', scatter_dimension...  148 us
    all_gather x1, waiting for transfers between devices, body(): lax.all_gather(up_weight, 'shard', axis=1, tiled=True)  148 us
    reduce_scatter x1, waiting for transfers between devices, body(): lax.psum_scatter(grad_down.astype(jnp.bfloat16), 'shard', scatter_dimensi...  148 us
    all_gather x1, waiting for transfers between devices, body(): lax.all_gather(down_weight, 'shard', axis=1, tiled=True)  144 us
    psum x1, waiting for transfers between devices, body(): lax.psum(group_parts[0].astype(jnp.bfloat16), 'rep').astype(jnp.float32)  119 us
    reduce_scatter x1, waiting for transfers between devices, body(): lax.psum_scatter(grad_heads.astype(jnp.bfloat16), 'shard', scatter_dimens...  100 us
    dot_general x12, matrix products, times_transposed(): lax.dot_general(left, matrix, (((1,), (1,)), ((), ())), preferred_element...  57.2 us
  transfers between devices with their start and end apart: 22, of which 21 were waited for; matrix products, arithmetic and copies ran while one was open for 6% of the time, Pallas kernels for 0%

commit v1 on v0

v1 whole, which is shorter than its diff:
```python
import math

import jax
import jax.numpy as jnp
from jax import lax
from jax.experimental import pallas as pl
from jax.experimental.pallas import tpu as pltpu
from jax.sharding import PartitionSpec as P

HEADS = 16
NORM_EPS = 1e-05
GELU_COEF = 0.7978845608028654
GELU_CUBE = 0.044715
LOW = jnp.bfloat16
F32 = jnp.float32


def dot(left, right):
    return jnp.dot(left, right, preferred_element_type=F32)


def dot_t(left, right):
    return lax.dot_general(left, right, (((1,), (1,)), ((), ())), preferred_element_type=F32)


def t_dot(left, right):
    return lax.dot_general(left, right, (((0,), (0,)), ((), ())), preferred_element_type=F32)


def call(kernel, outs, args, flops=0):
    nbytes = sum(a.size * a.dtype.itemsize for a in args) + sum(
        math.prod(o.shape) * jnp.dtype(o.dtype).itemsize for o in outs
    )
    vmem = pl.BlockSpec(memory_space=pltpu.VMEM)
    return pl.pallas_call(
        kernel,
        out_shape=outs,
        in_specs=[vmem] * len(args),
        out_specs=[vmem] * len(outs),
        compiler_params=pltpu.CompilerParams(vmem_limit_bytes=50 * 2**20),
        cost_estimate=pl.CostEstimate(flops=flops, bytes_accessed=nbytes, transcendentals=0),
    )(*args)


def sds(shape, dtype=LOW):
    return jax.ShapeDtypeStruct(shape, dtype)


def normalized(rows):
    centred = rows - jnp.mean(rows, axis=-1, keepdims=True)
    spread = jnp.mean(centred * centred, axis=-1, keepdims=True)
    rstd = lax.rsqrt(spread + NORM_EPS)
    return centred * rstd, rstd


def affine(xhat, gain_ref, shift_ref):
    return (xhat * gain_ref[...].astype(F32) + shift_ref[...].astype(F32)).astype(LOW)


def column_sum(rows):
    return jnp.sum(rows, axis=0, keepdims=True)


def joined(refs):
    return jnp.concatenate([ref[...] for ref in refs], axis=0)


def added(refs):
    total = refs[0][...].astype(F32)
    for ref in refs[1:]:
        total = total + ref[...].astype(F32)
    return total


def store_blocks(refs, rows):
    size = refs[0].shape[0]
    for number, ref in enumerate(refs):
        ref[...] = rows[number * size : (number + 1) * size].astype(ref.dtype)


def norm_kernel(rows_ref, gain_ref, shift_ref, out_ref):
    xhat, _ = normalized(rows_ref[...].astype(F32))
    out_ref[...] = affine(xhat, gain_ref, shift_ref)


def head_masks(width, head_size):
    lane = lax.broadcasted_iota(jnp.int32, (1, width), 1)
    return [
        jnp.logical_and(lane >= h * head_size, lane < (h + 1) * head_size).astype(F32)
        for h in range(width // head_size)
    ]


def stacked_heads(rows, masks):
    wide = rows.astype(F32)
    return jnp.concatenate([(wide * m).astype(LOW) for m in masks], axis=0)


def folded_heads(stacked, masks):
    size = stacked.shape[0] // len(masks)
    total = stacked[:size] * masks[0]
    for h in range(1, len(masks)):
        total = total + stacked[h * size : (h + 1) * size] * masks[h]
    return total


def make_attention_forward(parts, head_size):
    scale = 1.0 / math.sqrt(head_size)

    def kernel(*refs):
        x_refs, (wh, jb, vis, wm) = refs[:parts], refs[parts : parts + 4]
        x_all, joint, probs, attended = refs[parts + 4 : parts + 8]
        blocks = refs[parts + 8 :]
        rows = joined(x_refs)
        x_all[...] = rows
        joint[...] = (dot(rows, wh[...]) + jb[...].astype(F32)).astype(LOW)
        width = wm.shape[0]
        masks = head_masks(width, head_size)
        slots, size, _ = vis.shape
        for b in range(slots):
            at = slice(b * size, (b + 1) * size)
            query = stacked_heads(joint[at, :width], masks)
            scores = dot_t(query, joint[at, width : 2 * width]) * scale
            seen = jnp.concatenate([vis[b]] * len(masks), axis=0) > 0.0
            scores = jnp.where(seen, scores, -1e30)
            top = jnp.max(scores, axis=-1, keepdims=True)
            weights = jnp.exp(scores - top)
            share = weights * (1.0 / jnp.sum(weights, axis=-1, keepdims=True))
            probs[b] = share
            mixed = dot(share.astype(LOW), joint[at, 2 * width :])
            attended[at, :] = folded_heads(mixed, masks).astype(LOW)
        store_blocks(blocks, dot(attended[...], wm[...]))

    return kernel


def make_attention_backward(parts, head_size):
    scale = 1.0 / math.sqrt(head_size)

    def kernel(*refs):
        g_refs, (wm, wh, joint, probs) = refs[:parts], refs[parts : parts + 4]
        g_all, g_joint, g_query, g_value = refs[parts + 4 : parts + 8]
        blocks = refs[parts + 8 :]
        rows = joined(g_refs)
        g_all[...] = rows
        g_attended = dot_t(rows, wm[...]).astype(LOW)
        width = wm.shape[0]
        masks = head_masks(width, head_size)
        slots, _, size = probs.shape
        for b in range(slots):
            at = slice(b * size, (b + 1) * size)
            query = stacked_heads(joint[at, :width], masks)
            g_heads = stacked_heads(g_attended[at], masks)
            share = probs[b]
            g_probs = dot_t(g_heads, joint[at, 2 * width :])
            inner = jnp.sum(share * g_probs, axis=-1, keepdims=True)
            g_scores = (share * (g_probs - inner)).astype(LOW)
            g_q = folded_heads(dot(g_scores, joint[at, width : 2 * width]), masks) * scale
            g_joint[at, :width] = g_q.astype(LOW)
            g_joint[at, width : 2 * width] = (t_dot(g_scores, query) * scale).astype(LOW)
            g_joint[at, 2 * width :] = t_dot(share.astype(LOW), g_heads).astype(LOW)
        store_blocks(blocks, dot_t(g_joint[...], wh[...]))
        g_query[...] = column_sum(g_joint[:, :width].astype(F32))
        g_value[...] = column_sum(g_joint[:, 2 * width :].astype(F32))

    return kernel


def make_middle(parts):
    def kernel(hidden, *refs):
        terms, (bias, gain, shift) = refs[:parts], refs[parts : parts + 3]
        middle, second = refs[parts + 3 :]
        rows = hidden[...].astype(F32) + added(terms) + bias[...].astype(F32)
        middle[...] = rows
        xhat, _ = normalized(rows)
        second[...] = affine(xhat, gain, shift)

    return kernel


def make_block_end(parts, with_norm):
    def kernel(middle, *refs):
        terms, bias = refs[:parts], refs[parts]
        rest = refs[parts + 1 :]
        rows = (middle[...] + added(terms) + bias[...].astype(F32)).astype(LOW)
        if with_norm:
            gain, shift, out, normed = rest
            xhat, _ = normalized(rows.astype(F32))
            normed[...] = affine(xhat, gain, shift)
        else:
            (out,) = rest
        out[...] = rows

    return kernel


def make_mlp_forward(parts):
    def kernel(*refs):
        x_refs, (wu, ub, wd) = refs[:parts], refs[parts : parts + 3]
        x_all, before, active = refs[parts + 3 : parts + 6]
        blocks = refs[parts + 6 :]
        rows = joined(x_refs)
        x_all[...] = rows
        value = dot(rows, wu[...]) + ub[...].astype(F32)
        before[...] = value
        inner = jnp.tanh(GELU_COEF * (value + GELU_CUBE * value * value * value))
        active[...] = (0.5 * value * (1.0 + inner)).astype(LOW)
        if blocks:
            store_blocks(blocks, dot(active[...], wd[...]))

    return kernel


def make_mlp_backward(parts):
    def kernel(*refs):
        g_refs, (wd, wu, before) = refs[:parts], refs[parts : parts + 3]
        g_all, g_before, g_bias = refs[parts + 3 : parts + 6]
        blocks = refs[parts + 6 :]
        rows = joined(g_refs)
        g_all[...] = rows
        g_active = dot_t(rows, wd[...])
        value = before[...]
        inner = jnp.tanh(GELU_COEF * (value + GELU_CUBE * value * value * value))
        slope = 0.5 * (1.0 + inner) + 0.5 * value * (1.0 - inner * inner) * GELU_COEF * (
            1.0 + 3.0 * GELU_CUBE * value * value
        )
        result = (g_active * slope).astype(LOW)
        g_before[...] = result
        g_bias[...] = column_sum(result.astype(F32))
        store_blocks(blocks, dot_t(result, wu[...]))

    return kernel


def norm_back(grad, xhat, rstd, gain_ref):
    e = grad * gain_ref[...].astype(F32)
    mean_e = jnp.mean(e, axis=-1, keepdims=True)
    mean_ex = jnp.mean(e * xhat, axis=-1, keepdims=True)
    return rstd * (e - mean_e - xhat * mean_ex)


def make_middle_backward(parts):
    def kernel(grad_out, middle, *refs):
        terms, gain = refs[:parts], refs[parts]
        g_middle, g_merge, g_gain, g_shift, g_output, g_down = refs[parts + 1 :]
        grad = added(terms)
        xhat, rstd = normalized(middle[...])
        own = grad_out[...].astype(F32)
        rows = own + norm_back(grad, xhat, rstd, gain)
        g_middle[...] = rows
        low_rows = rows.astype(LOW)
        g_merge[...] = low_rows
        g_gain[...] = column_sum(grad * xhat)
        g_shift[...] = column_sum(grad)
        g_output[...] = column_sum(low_rows.astype(F32))
        g_down[...] = column_sum(own)

    return kernel


def make_first_backward(parts):
    def kernel(g_middle, hidden, *refs):
        terms, gain = refs[:parts], refs[parts]
        g_hidden, g_gain, g_shift = refs[parts + 1 :]
        grad = added(terms)
        xhat, rstd = normalized(hidden[...].astype(F32))
        g_hidden[...] = (g_middle[...] + norm_back(grad, xhat, rstd, gain)).astype(LOW)
        g_gain[...] = column_sum(grad * xhat)
        g_shift[...] = column_sum(grad)

    return kernel


def pick_columns_kernel(matrix, left, right, out):
    block = left.shape[0]
    step = left.shape[1]
    for m in range(out.shape[1] // step):
        first = dot(matrix[:, 2 * m * block : (2 * m + 1) * block], left[...])
        second = dot(matrix[:, (2 * m + 1) * block : (2 * m + 2) * block], right[...])
        out[:, m * step : (m + 1) * step] = (first + second).astype(LOW)


def make_spread_columns(parts):
    def kernel(*refs):
        pieces, place, out = refs[:parts], refs[parts], refs[parts + 1]
        size = place.shape[1]
        wide = place.shape[2]
        for m in range(out.shape[1] // wide):
            total = dot(pieces[0][:, m * size : (m + 1) * size], place[0])
            for k in range(1, parts):
                total = total + dot(pieces[k][:, m * size : (m + 1) * size], place[k])
            out[:, m * wide : (m + 1) * wide] = total

    return kernel


def swap(block):
    return lax.ppermute(block, "section", [(0, 1), (1, 0)])


def from_peers(blocks, axis, section=None):
    count = lax.axis_size(axis)
    received = []
    for k in range(1, count):
        if section is None:
            pairs = [(i, i ^ k) for i in range(count)]
            received.append(lax.ppermute(blocks[k], axis, pairs))
        else:
            pairs = [(section * count + i, section * count + (i ^ k)) for i in range(count)]
            received.append(lax.ppermute(blocks[k], ("section", axis), pairs))
    return [blocks[0]] + received


def gathered_blocks(block, axis, section=None):
    return from_peers([block] * lax.axis_size(axis), axis, section)


def body(
    tokens,
    doc_lengths,
    heads_weight,
    merge_weight,
    up_weight,
    down_weight,
    first_gain,
    first_shift,
    query_bias,
    value_bias,
    output_bias,
    second_gain,
    second_shift,
    up_bias,
    down_bias,
    cotangent,
):
    sections = lax.axis_size("section")
    shards = lax.axis_size("shard")
    reps = lax.axis_size("rep")
    assert sections == 2
    core = lax.axis_index("section")
    shard = lax.axis_index("shard")
    rep = lax.axis_index("rep")
    on_first = core == 0

    features = tokens.shape[1]
    slot_rows = tokens.shape[0] // doc_lengths.shape[0]
    slots = doc_lengths.shape[0] // sections
    n = slots * slot_rows
    all_rows = reps * n
    head_size = features // HEADS
    width = features // reps
    ff = up_weight.shape[2]
    ff_own = ff // reps
    depth = features // shards
    strided = HEADS % (shards * reps) == 0
    head_run = (HEADS // (shards * reps)) * head_size if strided else width

    def rows_of_core(array, which):
        return lax.dynamic_index_in_dim(
            array.reshape((sections, array.shape[0] // sections) + array.shape[1:]),
            which,
            0,
            keepdims=False,
        )

    vectors = (
        first_gain,
        first_shift,
        query_bias,
        value_bias,
        output_bias,
        second_gain,
        second_shift,
        down_bias,
        up_bias,
    )
    packed = jnp.concatenate([v.reshape(-1, depth) for v in vectors], axis=0)
    vector_rows = packed.shape[0]
    shard_order = gathered_blocks(packed, "shard")

    def in_order(pieces, index):
        count = len(pieces)
        result = []
        for j in range(count):
            total = pieces[0]
            for k in range(1, count):
                total = jnp.where(index == (j ^ k), pieces[k], total)
            result.append(total)
        return jnp.stack(result)

    own_vectors = in_order(shard_order, shard)
    other_vectors = swap(own_vectors)
    section_vectors = (
        jnp.where(on_first, own_vectors, other_vectors),
        jnp.where(on_first, other_vectors, own_vectors),
    )

    def vector(s, number):
        return section_vectors[s][:, number, :].reshape(1, features)

    def own_heads_part(flat):
        if strided:
            cut = flat.reshape(shards, reps, head_run)
            return lax.dynamic_index_in_dim(cut, rep, 1, keepdims=False).reshape(1, width)
        return lax.dynamic_index_in_dim(flat.reshape(reps, width), rep, 0, keepdims=False).reshape(
            1, width
        )

    def up_vector(s):
        flat = section_vectors[s][:, 8:, :].reshape(shards, reps, ff_own // shards)
        return lax.dynamic_index_in_dim(flat, rep, 1, keepdims=False).reshape(1, ff_own)

    def joint_vector(s):
        query = own_heads_part(vector(s, 2))
        value = own_heads_part(vector(s, 3))
        return jnp.concatenate([query, jnp.zeros_like(query), value], axis=1)

    if strided:
        lane = jnp.arange(reps * head_run, dtype=jnp.int32)[:, None]
        place = jnp.arange(2 * head_run, dtype=jnp.int32)[None, :]
        hit = lane == rep * head_run + place % head_run
        left = jnp.logical_and(hit, place < head_run).astype(LOW)
        right = jnp.logical_and(hit, place >= head_run).astype(LOW)
        heads_part = call(
            pick_columns_kernel, [sds((depth, 3 * width))], [heads_weight[0], left, right]
        )[0]
        merge_part = lax.dynamic_slice_in_dim(merge_weight[0], rep * head_run, head_run, 0)
    else:
        heads_part = lax.dynamic_index_in_dim(
            heads_weight.reshape(depth, 3, reps, width), rep, 2, keepdims=False
        ).reshape(depth, 3 * width)
        merge_part = merge_weight[0]
    up_part = lax.dynamic_index_in_dim(
        up_weight.reshape(depth, shards, reps, ff_own // shards), rep, 2, keepdims=False
    ).reshape(depth, ff_own)
    down_part = lax.dynamic_slice_in_dim(
        down_weight[0], rep * (ff_own // shards), ff_own // shards, 0
    )

    weights = []
    halves = []
    for part in (heads_part, merge_part, up_part, down_part):
        kept = rows_of_core(part, core)
        other = swap(rows_of_core(part, 1 - core))
        halves.append((jnp.where(on_first, kept, other), jnp.where(on_first, other, kept)))
    for s in range(sections):
        full = [
            lax.all_gather(pair[s], ("shard", "section"), axis=0, tiled=True) for pair in halves
        ]
        if not strided:
            full[1] = lax.dynamic_slice_in_dim(full[1], rep * width, width, 0)
        weights.append(full)

    own_lengths = rows_of_core(doc_lengths, core)
    lengths = jnp.concatenate(gathered_blocks(own_lengths, "rep"), axis=0)
    ends = jnp.cumsum(lengths, axis=1)
    position = jnp.arange(slot_rows, dtype=jnp.int32)
    segment = jnp.sum((position[None, :, None] >= ends[:, None, :]).astype(jnp.int32), axis=2)
    visible = jnp.logical_and(
        segment[:, :, None] == segment[:, None, :], position[None, None, :] <= position[None, :, None]
    ).astype(F32)
    slot_count = reps * slots

    own_tokens = rows_of_core(tokens, core)
    own_cotangent = rows_of_core(cotangent, core)
    block_shapes = [sds((n, features))] * reps
    attention_flops = 2 * all_rows * features * 4 * width
    mlp_flops = 4 * all_rows * features * ff_own

    hidden = own_tokens
    normed = call(
        norm_kernel, [sds((n, features))], [hidden, vector(0, 0), vector(0, 1)]
    )[0]
    saved = []
    outputs = []
    for s in range(sections):
        wh, wm, wu, wd = weights[s]
        results = call(
            make_attention_forward(reps, head_size),
            [
                sds((all_rows, features)),
                sds((all_rows, 3 * width)),
                sds((slot_count, (width // head_size) * slot_rows, slot_rows), F32),
                sds((all_rows, width)),
            ]
            + block_shapes,
            gathered_blocks(normed, "rep") + [wh, joint_vector(s), visible, wm],
            attention_flops,
        )
        normed_all, joint, probs, attended = results[:4]
        terms = from_peers(results[4:], "rep")
        middle, second = call(
            make_middle(reps),
            [sds((n, features), F32), sds((n, features))],
            [hidden] + terms + [vector(s, 4), vector(s, 5), vector(s, 6)],
        )
        results = call(
            make_mlp_forward(reps),
            [sds((all_rows, features)), sds((all_rows, ff_own), F32), sds((all_rows, ff_own))]
            + block_shapes,
            gathered_blocks(second, "rep") + [wu, up_vector(s), wd],
            mlp_flops,
        )
        second_all, before, active = results[:3]
        terms = from_peers(results[3:], "rep")
        saved.append((hidden, normed_all, joint, probs, attended, middle, second_all, before, active))
        if s + 1 < sections:
            hidden, normed = call(
                make_block_end(reps, True),
                [sds((n, features)), sds((n, features))],
                [middle] + terms + [vector(s, 7), vector(s + 1, 0), vector(s + 1, 1)],
            )
            outputs.append(hidden)
        else:
            outputs.append(
                call(
                    make_block_end(reps, False),
                    [sds((n, features))],
                    [middle] + terms + [vector(s, 7)],
                )[0]
            )

    grad_out = own_cotangent
    hidden_grads = [None] * sections
    vector_grads = [None] * sections
    weight_grads = [None] * sections

    def over_slots(left, right):
        product = t_dot(left, right).astype(LOW)
        return lax.psum_scatter(product, ("shard", "section"), scatter_dimension=0, tiled=True)

    for s in reversed(range(sections)):
        wh, wm, wu, wd = weights[s]
        hidden, normed_all, joint, probs, attended, middle, second_all, before, active = saved[s]
        row = sds((1, features), F32)
        results = call(
            make_mlp_backward(reps),
            [sds((all_rows, features)), sds((all_rows, ff_own)), sds((1, ff_own), F32)]
            + block_shapes,
            gathered_blocks(grad_out, "rep") + [wd, wu, before],
            mlp_flops,
        )
        down_all, before_all, up_sum = results[:3]
        terms = from_peers(results[3:], "rep")
        grad_down = over_slots(active, down_all)
        grad_up = over_slots(second_all, before_all)
        g_middle, g_merge, second_gain_sum, second_shift_sum, output_sum, down_sum = call(
            make_middle_backward(reps),
            [sds((n, features), F32), sds((n, features))] + [row] * 4,
            [grad_out, middle] + terms + [vector(s, 5)],
        )
        results = call(
            make_attention_backward(reps, head_size),
            [
                sds((all_rows, features)),
                sds((all_rows, 3 * width)),
                sds((1, width), F32),
                sds((1, width), F32),
            ]
            + block_shapes,
            gathered_blocks(g_merge, "rep") + [wm, wh, joint, probs],
            2 * attention_flops,
        )
        merge_all, joint_all, query_sum, value_sum = results[:4]
        terms = from_peers(results[4:], "rep")
        grad_heads = over_slots(normed_all, joint_all)
        if strided:
            grad_merge = over_slots(attended, merge_all)
        else:
            product = t_dot(attended, merge_all).astype(LOW)
            spread = lax.dynamic_update_slice_in_dim(
                jnp.zeros((features, features), LOW), product, rep * width, 0
            )
            grad_merge = lax.psum_scatter(
                spread, ("shard", "section"), scatter_dimension=0, tiled=True
            )
        grad_out, first_gain_sum, first_shift_sum = call(
            make_first_backward(reps),
            [sds((n, features)), row, row],
            [g_middle, hidden] + terms + [vector(s, 0)],
        )
        hidden_grads[s] = grad_out

        def placed_heads(part):
            if strided:
                wide = jnp.zeros((shards, reps, head_run), F32)
                part = part.reshape(shards, 1, head_run)
                return lax.dynamic_update_slice_in_dim(wide, part, rep, 1).reshape(shards, 1, depth)
            wide = jnp.zeros((reps, width), F32)
            return lax.dynamic_update_slice_in_dim(wide, part, rep, 0).reshape(shards, 1, depth)

        wide_up = lax.dynamic_update_slice_in_dim(
            jnp.zeros((shards, reps, ff_own // shards), F32),
            up_sum.reshape(shards, 1, ff_own // shards),
            rep,
            1,
        ).reshape(shards, -1, depth)
        vector_grads[s] = jnp.concatenate(
            [
                first_gain_sum.reshape(shards, 1, depth),
                first_shift_sum.reshape(shards, 1, depth),
                placed_heads(query_sum),
                placed_heads(value_sum),
                output_sum.reshape(shards, 1, depth),
                second_gain_sum.reshape(shards, 1, depth),
                second_shift_sum.reshape(shards, 1, depth),
                down_sum.reshape(shards, 1, depth),
                wide_up,
            ],
            axis=1,
        )
        weight_grads[s] = (grad_heads, grad_merge, grad_up, grad_down)

    own_sum = jnp.where(on_first, vector_grads[0], vector_grads[1])
    other_sum = jnp.where(on_first, vector_grads[1], vector_grads[0])
    own_sum = own_sum + swap(other_sum)
    pieces = from_peers(
        [
            lax.dynamic_index_in_dim(own_sum, shard ^ k, 0, keepdims=False)
            for k in range(shards)
        ],
        "shard",
    )
    total = sum(pieces[1:], pieces[0])
    pieces = gathered_blocks(total, "rep")
    total = sum(pieces[1:], pieces[0])
    singles = [total[number].reshape(1, depth) for number in range(8)]
    grad_up_bias = total[8:].reshape(1, -1)

    def owned(number):
        parts = []
        for s in range(sections):
            mine = weight_grads[s][number]
            theirs = lax.ppermute(mine, "section", [(1 - s, s)])
            parts.append(jnp.concatenate([mine, theirs] if s == 0 else [theirs, mine], axis=0))
        return parts

    def over_reps(number):
        parts = owned(number)
        lists = [gathered_blocks(parts[s], "rep", s) for s in range(sections)]
        return [jnp.where(on_first, a, b) for a, b in zip(*lists)]

    heads_pieces = over_reps(0)
    if strided:
        lane = jnp.arange(head_run, dtype=jnp.int32)[:, None]
        place = jnp.arange(reps * head_run, dtype=jnp.int32)[None, :]
        places = jnp.stack(
            [(place == (rep ^ k) * head_run + lane).astype(LOW) for k in range(reps)]
        )
        grad_heads = call(
            make_spread_columns(reps),
            [sds((depth, 3 * features), F32)],
            heads_pieces + [places],
        )[0][None]
        merge_pieces = over_reps(1)
        grad_merge = jnp.zeros((reps, head_run, features), F32)
        for k, piece in enumerate(merge_pieces):
            grad_merge = lax.dynamic_update_slice_in_dim(
                grad_merge, piece.astype(F32)[None], rep ^ k, 0
            )
        grad_merge = grad_merge.reshape(1, depth, features)
    else:
        grad_heads = jnp.zeros((depth, 3, reps, width), F32)
        for k, piece in enumerate(heads_pieces):
            grad_heads = lax.dynamic_update_slice_in_dim(
                grad_heads, piece.astype(F32).reshape(depth, 3, 1, width), rep ^ k, 2
            )
        grad_heads = grad_heads.reshape(1, depth, 3 * features)
        parts = owned(1)
        grad_merge = lax.psum(jnp.where(on_first, parts[0], parts[1]), "rep").astype(F32)[None]

    grad_up = jnp.zeros((depth, shards, reps, ff_own // shards), F32)
    for k, piece in enumerate(over_reps(2)):
        grad_up = lax.dynamic_update_slice_in_dim(
            grad_up, piece.astype(F32).reshape(depth, shards, 1, ff_own // shards), rep ^ k, 2
        )
    grad_up = grad_up.reshape(1, depth, ff)
    grad_down = jnp.zeros((reps, ff_own // shards, features), F32)
    for k, piece in enumerate(over_reps(3)):
        grad_down = lax.dynamic_update_slice_in_dim(
            grad_down, piece.astype(F32)[None], rep ^ k, 0
        )
    grad_down = grad_down.reshape(1, ff // shards, features)

    def by_section(pair):
        own = jnp.where(on_first, pair[0], pair[1])
        other = swap(jnp.where(on_first, pair[1], pair[0]))
        return jnp.concatenate(
            [jnp.where(on_first, own, other), jnp.where(on_first, other, own)], axis=0
        )[None]

    activations = by_section(outputs)
    input_grads = by_section(hidden_grads)
    (
        grad_first_gain,
        grad_first_shift,
        grad_query,
        grad_value,
        grad_output,
        grad_second_gain,
        grad_second_shift,
        grad_down_bias,
    ) = singles
    return (
        activations,
        input_grads,
        grad_heads,
        grad_merge,
        grad_up,
        grad_down,
        grad_first_gain,
        grad_first_shift,
        grad_query,
        grad_value,
        grad_output,
        grad_second_gain,
        grad_second_shift,
        grad_up_bias,
        grad_down_bias,
    )


def solution(mesh):
    rows = P(("shard", "rep"), None)
    matrix = P("section", "shard", None)
    line = P("section", "shard")
    return jax.shard_map(
        body,
        mesh=mesh,
        in_specs=(rows, rows) + (matrix,) * 4 + (line,) * 9 + (rows,),
        out_specs=(P("section", ("shard", "rep"), None),) * 2 + (matrix,) * 4 + (line,) * 9,
        check_vma=False,
    )
```

time: 1440 us -> 711 us (0.49)
  waiting for transfers between devices: 1050 us -> 264 us
  starting transfers between devices: 9.49 us -> 143 us
  matrix products: 131 us -> 25 us
  local copies, waits for them, and re-layouts: 68 us -> 150 us
  blocking collectives: 110 us -> 33.2 us
  Pallas kernels: 0 us -> 45.6 us
  other arithmetic: 43.2 us -> 23.9 us
    all_gather x4 -> x6, waiting for transfers between devices: 354 us -> 32.9 us  [body(): lax.all_gather(pair[s], ('shard', 'section'), axis=0, tiled=True)]
    reduce_scatter x4 -> x8, waiting for transfers between devices: 396 us -> 119 us  [over_slots(): lax.psum_scatter(product, ('shard', 'section'), scatter_dimension=0, tile...]
    unnamed x27 -> x14, waiting for transfers between devices: 181 us -> 1.25 us
    ppermute x4 -> x100, starting transfers between devices: 8.12 us -> 143 us  [the longest x60 75.3 us: from_peers(): received.append(lax.ppermute(blocks[k], axis, pairs))]
    psum x1 -> x0, waiting for transfers between devices: 119 us -> none  [body(): lax.psum(group_parts[0].astype(jnp.bfloat16), 'rep').astype(jnp.float32)]
    ppermute x4 -> x100, waiting for transfers between devices: 3.15 us -> 111 us  [the longest x60 89.2 us: from_peers(): received.append(lax.ppermute(blocks[k], axis, pairs))]
    dot_general x49 -> x8, matrix products: 131 us -> 25 us  [t_dot(): lax.dot_general(left, right, (((0,), (0,)), ((), ())), preferred_element_...]
    dynamic_update_slice x0 -> x10, local copies, waits for them, and re-layouts: none -> 91.2 us  [the longest x4 91 us: body(): lax.dynamic_update_slice_in_dim(grad_up, piece.astype(F32).reshape(depth,...]
  transfers between devices with their start and end apart: 22 -> 114, of which waited for: 21 -> 49; matrix products, arithmetic and copies ran while one was open for 6% -> 26% of each run, Pallas kernels for 0% -> 5%
where the time goes in v1:
time: 711 us; the launch traced here: 701 us
  waiting for transfers between devices  264 us (37%)
  local copies, waits for them, and re-layouts  150 us (21%)
  starting transfers between devices  143 us (20%)
  Pallas kernels  45.6 us (6%)
  blocking collectives  33.2 us (5%)
  matrix products  25 us (4%)
  other arithmetic  23.9 us (3%)
  between operations  15.9 us (2%)
    reduce_scatter x8, waiting for transfers between devices, over_slots(): lax.psum_scatter(product, ('shard', 'section'), scatter_dimension=0, tile...  119 us
    dynamic_update_slice x4, local copies, waits for them, and re-layouts, body(): lax.dynamic_update_slice_in_dim(grad_up, piece.astype(F32).reshape(depth,...  91 us
    ppermute x60, waiting for transfers between devices, from_peers(): received.append(lax.ppermute(blocks[k], axis, pairs))  89.2 us
    ppermute x60, starting transfers between devices, from_peers(): received.append(lax.ppermute(blocks[k], axis, pairs))  75.3 us
    ppermute x24, starting transfers between devices, from_peers(): received.append(lax.ppermute(blocks[k], ('section', axis), pairs))  54.2 us
    pallas_call x19, Pallas kernels, call(): pl.pallas_call(kernel, out_shape=outs, in_specs=[vmem] * len(args), out_s...  45.6 us
    all_gather x2, blocking collectives, body(): lax.all_gather(pair[s], ('shard', 'section'), axis=0, tiled=True)  33.2 us
    all_gather x6, waiting for transfers between devices, body(): lax.all_gather(pair[s], ('shard', 'section'), axis=0, tiled=True)  32.9 us
  transfers between devices with their start and end apart: 114, of which 49 were waited for; matrix products, arithmetic and copies ran while one was open for 26% of the time, Pallas kernels for 5%

profile of v1, /device:TPU:0, one launch (start us, length us, event | category | flops | bytes accessed | tf_op | source)
XLA Modules:
  0.0 700.8 jit_solution(3348913160407349201)
XLA Ops:
  11.9 4.5 reshape.555
  16.4 4.9 dynamic-slice_reduce_fusion
  28.5 4.8 collective-permute-start
  48.3 17.9 %all_gather.25.refs_7_.refs_4_ = bf16[256,1024]{1,0:T(8,128)(2,1)S(1)} all-gather(bf16[32,1024]{1,0:T(8,128)(2,1)S(1)} %get-tuple-element.198), channel_id=1, replica_groups=mesh['section'=2,'shard'=4,'rep'=4] {'shard','section'}, dimensions={0}, use_global_device_ids=true | all-gather | bytes 589824 | tf_op jit(solution)/shard_map/all_gather | solution.py:448
  66.2 4.3 shard_map.273
  74.9 4.2 collective-permute-done.12.refs_1_
  79.1 4.9 collective-permute-done.13.refs_2_
  87.9 4.3 collective-permute-done.15.refs_1_
  92.2 3.7 collective-permute-done.16.refs_2_
  95.9 10.0 %all-gather.11.cloned.1.call-done.refs_6_.refs_4_ = bf16[1024,1024]{1,0:T(8,128)(2,1)} async-done(((bf16[128,1024]{1,0:T(8,128)(2,1)}), bf16[1024,1024]{1,0:T(8,128)(2,1)}) %all-gather.11.cloned.1.call-update) | async-done | bytes 2097168 | tf_op jit(solution)/shard_map/all_gather | solution.py:448
  105.9 4.7 shard_map.275
  115.0 4.2 collective-permute-done.20.refs_1_
  119.2 4.7 collective-permute-done.21.refs_2_
  127.8 15.3 %all_gather.29.refs_7_.refs_4_ = bf16[256,1024]{1,0:T(8,128)(2,1)S(1)} all-gather(bf16[32,1024]{1,0:T(8,128)(2,1)S(1)} %get-tuple-element.197), channel_id=1, replica_groups=mesh['section'=2,'shard'=4,'rep'=4] {'shard','section'}, dimensions={0}, use_global_device_ids=true | all-gather | bytes 589824 | tf_op jit(solution)/shard_map/all_gather | solution.py:448
  143.2 4.2 shard_map.277
  151.8 4.2 collective-permute-done.26.refs_1_
  171.3 22.9 %all-gather.17.cloned.1.call-done.refs_6_.refs_4_ = bf16[1024,1024]{1,0:T(8,128)(2,1)} async-done(((bf16[128,1024]{1,0:T(8,128)(2,1)}), bf16[1024,1024]{1,0:T(8,128)(2,1)}) %all-gather.17.cloned.1.call-update) | async-done | bytes 2097168 | tf_op jit(solution)/shard_map/all_gather | solution.py:448
  196.0 4.9 shard_map.279
  204.9 5.3 shard_map.281
  214.6 4.2 collective-permute-done.39.refs_1_
  218.8 4.7 collective-permute-done.40.refs_2_
  227.6 4.3 collective-permute-done.42.refs_1_
  231.9 3.5 collective-permute-done.43.refs_2_
  235.5 4.4 shard_map.283
  259.2 5.3 shard_map.285
  271.4 4.1 collective-permute-done.53.refs_3_
  284.4 5.1 shard_map.287
  292.4 3.5 convolution_convert_fusion.4
  296.0 3.7 convolution_convert_fusion.2
  299.8 4.0 convolution_convert_fusion
  307.3 4.0 convolution_convert_fusion.3
  317.4 3.6 collective-permute-done.33.refs_2_
  331.9 3.8 collective-permute-done.59.refs_3_
  342.1 3.8 convolution_convert_fusion.1
  359.0 6.2 collective-permute-done.69
  380.8 13.6 %reduce-scatter.19.cloned.1.call-done = bf16[128,1024]{1,0:T(8,128)(2,1)} async-done(((bf16[1024,1024]{1,0:T(8,128)(2,1)}), bf16[128,1024]{1,0:T(8,128)(2,1)}) %reduce-scatter.19.cloned.1.call-update) | async-done | bytes 262160 | tf_op jit(solution)/shard_map/reduce_scatter | solution.py:530
  402.2 29.1 %reduce-scatter.23.cloned.1.call-done = bf16[128,1024]{1,0:T(8,128)(2,1)} async-done(((bf16[1024,1024]{1,0:T(8,128)(2,1)}), bf16[128,1024]{1,0:T(8,128)(2,1)}) %reduce-scatter.23.cloned.1.call-update) | async-done | bytes 262160 | tf_op jit(solution)/shard_map/reduce_scatter | solution.py:530
  432.7 33.5 %reduce-scatter.9.cloned.1.call-done = bf16[128,768]{1,0:T(8,128)(2,1)} async-done(((bf16[1024,768]{1,0:T(8,128)(2,1)}), bf16[128,768]{1,0:T(8,128)(2,1)}) %reduce-scatter.9.cloned.1.call-update) | async-done | bytes 196624 | tf_op jit(solution)/shard_map/reduce_scatter | solution.py:530
  485.6 4.1 collective-permute-start.67
  490.8 12.0 %reduce-scatter.17.cloned.1.call-done = bf16[128,1024]{1,0:T(8,128)(2,1)} async-done(((bf16[1024,1024]{1,0:T(8,128)(2,1)}), bf16[128,1024]{1,0:T(8,128)(2,1)}) %reduce-scatter.17.cloned.1.call-update) | async-done | bytes 262160 | tf_op jit(solution)/shard_map/reduce_scatter | solution.py:530
  509.0 31.1 %reduce-scatter.21.cloned.1.call-done = bf16[128,1024]{1,0:T(8,128)(2,1)} async-done(((bf16[1024,1024]{1,0:T(8,128)(2,1)}), bf16[128,1024]{1,0:T(8,128)(2,1)}) %reduce-scatter.21.cloned.1.call-update) | async-done | bytes 262160 | tf_op jit(solution)/shard_map/reduce_scatter | solution.py:530
  545.8 3.5 shard_map.289
  555.0 22.7 %dynamic_update_slice.58 = f32[256,4,4,256]{3,2,1,0:T(4,128)} dynamic-update-slice(f32[256,4,4,256]{3,2,1,0:T(4,128)} %broadcast_in_dim.76, f32[256,4,1,256]{3,2,1,0:T(1,128)S(1)} %copy.174, s32[]{:T(128)} %constant.106.clone.1, s32[]{:T(128)} %constant.106.clone.1, s32[]{:T(128)S(6)} %select_n.374, s32[]{:T(128)} %constant.106.clone.1) | dynamic-update-slice | bytes 2097156 | tf_op jit(solution)/shard_map/dynamic_update_slice | solution.py:674
  606.3 22.8 %dynamic_update_slice.59 = f32[256,4,4,256]{3,2,1,0:T(4,128)} dynamic-update-slice(f32[256,4,4,256]{3,2,1,0:T(4,128)} %dynamic_update_slice.58, f32[256,4,1,256]{3,2,1,0:T(1,128)S(1)} %reshape.606, s32[]{:T(128)} %constant.106.clone.1, s32[]{:T(128)} %constant.106.clone.1, s32[]{:T(128)S(6)} %select_n.404, s32[]{:T(128)} %constant.106.clone.1) | dynamic-update-slice | bytes 2097156 | tf_op jit(solution)/shard_map/dynamic_update_slice | solution.py:674
  629.1 22.7 %dynamic_update_slice.60 = f32[256,4,4,256]{3,2,1,0:T(4,128)} dynamic-update-slice(f32[256,4,4,256]{3,2,1,0:T(4,128)} %dynamic_update_slice.59, f32[256,4,1,256]{3,2,1,0:T(1,128)S(1)} %reshape.607, s32[]{:T(128)} %constant.106.clone.1, s32[]{:T(128)} %constant.106.clone.1, s32[]{:T(128)S(6)} %select_n.406, s32[]{:T(128)} %constant.106.clone.1) | dynamic-update-slice | bytes 2097156 | tf_op jit(solution)/shard_map/dynamic_update_slice | solution.py:674
  651.8 22.7 %dynamic_update_slice.61 = f32[256,4,4,256]{3,2,1,0:T(4,128)} dynamic-update-slice(f32[256,4,4,256]{3,2,1,0:T(4,128)} %dynamic_update_slice.60, f32[256,4,1,256]{3,2,1,0:T(1,128)S(1)} %reshape.608, s32[]{:T(128)} %constant.106.clone.1, s32[]{:T(128)} %constant.106.clone.1, s32[]{:T(128)S(6)} %select_n.408, s32[]{:T(128)} %constant.106.clone.1) | dynamic-update-slice | bytes 2097156 | tf_op jit(solution)/shard_map/dynamic_update_slice | solution.py:674
  674.6 5.9 reshape.569
  687.5 5.2 collective-permute-done.91
  (481 shorter events, 253.6 us)
Async XLA Ops:
  7.2 59.0 %all-gather.7.cloned.1.call-start = ((), (), s32[]{:S(2)}) async-start(), calls=%async_computation.8 | async-start | bytes 1769472 | tf_op jit(solution)/shard_map/all_gather | solution.py:448
  11.8 84.1 %all-gather.9.cloned.1.call-start = ((), (), s32[]{:S(2)}) async-start(), calls=%async_computation.9 | async-start | bytes 2359296 | tf_op jit(solution)/shard_map/all_gather | solution.py:448
  24.4 81.4 %all-gather.11.cloned.1.call-start = ((), (), s32[]{:S(2)}) async-start(), calls=%async_computation.10 | async-start | bytes 2359296 | tf_op jit(solution)/shard_map/all_gather | solution.py:448
  27.1 116.1 %all-gather.13.cloned.1.call-start = ((), (), s32[]{:S(2)}) async-start(), calls=%async_computation.11 | async-start | bytes 1769472 | tf_op jit(solution)/shard_map/all_gather | solution.py:448
  27.7 143.7 %all-gather.15.cloned.1.call-start = ((), (), s32[]{:S(2)}) async-start(), calls=%async_computation.12 | async-start | bytes 2359296 | tf_op jit(solution)/shard_map/all_gather | solution.py:448
  28.2 165.9 %all-gather.17.cloned.1.call-start = ((), (), s32[]{:S(2)}) async-start(), calls=%async_computation.13 | async-start | bytes 2359296 | tf_op jit(solution)/shard_map/all_gather | solution.py:448
  28.5 13.8 %collective-permute-start = (bf16[12,256]{1,0:T(8,128)(2,1)S(1)}, bf16[12,256]{1,0:T(8,128)(2,1)S(1)}, u32[]{:S(2)}, u32[]{:S(2)}) collective-permute-start(bf16[12,256]{1,0:T(8,128)(2,1)S(1)} %concatenate.126), channel_id=1, source_target_pairs={{0,12},{4,8},{8,4},{12,0},{1,13},{5,9},{9,5},{13,1},{2,14},{6,10},... | collective-permute-start | bytes 18440 | tf_op jit(solution)/shard_map/ppermute | solution.py:307
  38.1 311.5 %reduce-scatter.15.cloned.1.call-start = ((), (), s32[]{:S(2)}) async-start(), calls=%async_computation.17 | async-start | bytes 589824 | tf_op jit(solution)/shard_map/reduce_scatter | solution.py:530
  43.9 22.3 %collective-permute-start.4 = (bf16[96,1024]{1,0:T(8,128)(2,1)S(1)}, bf16[96,1024]{1,0:T(8,128)(2,1)S(1)}, u32[]{:S(2)}, u32[]{:S(2)}) collective-permute-start(bf16[96,1024]{1,0:T(8,128)(2,1)S(1)} %shard_map.271.refs_0_), channel_id=1, source_target_pairs={{0,1},{1,0},{2,3},{3,2},{4,5},{5,4},{6,7},{7,6},{8,9},{9,8},{10,11... | collective-permute-start | bytes 589832 | tf_op jit(solution)/shard_map/ppermute | solution.py:307
  45.7 20.5 %collective-permute-start.5 = (bf16[96,1024]{1,0:T(8,128)(2,1)S(1)}, bf16[96,1024]{1,0:T(8,128)(2,1)S(1)}, u32[]{:S(2)}, u32[]{:S(2)}) collective-permute-start(bf16[96,1024]{1,0:T(8,128)(2,1)S(1)} %shard_map.271.refs_0_), channel_id=1, source_target_pairs={{0,2},{1,3},{2,0},{3,1},{4,6},{5,7},{6,4},{7,5},{8,10},{9,11},{10,... | collective-permute-start | bytes 589832 | tf_op jit(solution)/shard_map/ppermute | solution.py:307
  47.2 19.0 %collective-permute-start.6 = (bf16[96,1024]{1,0:T(8,128)(2,1)S(1)}, bf16[96,1024]{1,0:T(8,128)(2,1)S(1)}, u32[]{:S(2)}, u32[]{:S(2)}) collective-permute-start(bf16[96,1024]{1,0:T(8,128)(2,1)S(1)} %shard_map.271.refs_0_), channel_id=1, source_target_pairs={{0,3},{1,2},{2,1},{3,0},{4,7},{5,6},{6,5},{7,4},{8,11},{9,10},{10,... | collective-permute-start | bytes 589832 | tf_op jit(solution)/shard_map/ppermute | solution.py:307
  124.3 18.9 %collective-permute-start.23 = (bf16[96,1024]{1,0:T(8,128)(2,1)S(1)}, bf16[96,1024]{1,0:T(8,128)(2,1)S(1)}, u32[]{:S(2)}, u32[]{:S(2)}) collective-permute-start(bf16[96,1024]{1,0:T(8,128)(2,1)S(1)} %get-tuple-element.110.refs_0_), channel_id=1, source_target_pairs={{0,1},{1,0},{2,3},{3,2},{4,5},{5,4},{6,7},{7,6},{8,9},{9,8},{10,11... | collective-permute-start | bytes 589832 | tf_op jit(solution)/shard_map/ppermute | solution.py:307
  125.5 17.7 %collective-permute-start.24 = (bf16[96,1024]{1,0:T(8,128)(2,1)S(1)}, bf16[96,1024]{1,0:T(8,128)(2,1)S(1)}, u32[]{:S(2)}, u32[]{:S(2)}) collective-permute-start(bf16[96,1024]{1,0:T(8,128)(2,1)S(1)} %get-tuple-element.110.refs_0_), channel_id=1, source_target_pairs={{0,2},{1,3},{2,0},{3,1},{4,6},{5,7},{6,4},{7,5},{8,10},{9,11},{10,... | collective-permute-start | bytes 589832 | tf_op jit(solution)/shard_map/ppermute | solution.py:307
  126.4 16.8 %collective-permute-start.25 = (bf16[96,1024]{1,0:T(8,128)(2,1)S(1)}, bf16[96,1024]{1,0:T(8,128)(2,1)S(1)}, u32[]{:S(2)}, u32[]{:S(2)}) collective-permute-start(bf16[96,1024]{1,0:T(8,128)(2,1)S(1)} %get-tuple-element.110.refs_0_), channel_id=1, source_target_pairs={{0,3},{1,2},{2,1},{3,0},{4,7},{5,6},{6,5},{7,4},{8,11},{9,10},{10,... | collective-permute-start | bytes 589832 | tf_op jit(solution)/shard_map/ppermute | solution.py:307
  161.8 32.3 %collective-permute-start.30 = (bf16[96,1024]{1,0:T(8,128)(2,1)S(1)}, bf16[96,1024]{1,0:T(8,128)(2,1)}, u32[]{:S(2)}, u32[]{:S(2)}) collective-permute-start(bf16[96,1024]{1,0:T(8,128)(2,1)S(1)} %get-tuple-element.116.refs_0_), channel_id=1, source_target_pairs={{0,2},{1,3},{2,0},{3,1},{4,6},{5,7},{6,4},{7,5},{8,10},{9,11},{10,... | collective-permute-start | bytes 589832 | tf_op jit(solution)/shard_map/ppermute | solution.py:307
  163.3 30.9 %collective-permute-start.31 = (bf16[96,1024]{1,0:T(8,128)(2,1)S(1)}, bf16[96,1024]{1,0:T(8,128)(2,1)}, u32[]{:S(2)}, u32[]{:S(2)}) collective-permute-start(bf16[96,1024]{1,0:T(8,128)(2,1)S(1)} %get-tuple-element.116.refs_0_), channel_id=1, source_target_pairs={{0,3},{1,2},{2,1},{3,0},{4,7},{5,6},{6,5},{7,4},{8,11},{9,10},{10,... | collective-permute-start | bytes 589832 | tf_op jit(solution)/shard_map/ppermute | solution.py:307
  165.5 39.3 %collective-permute-start.36 = (bf16[96,1024]{1,0:T(8,128)(2,1)S(1)}, bf16[96,1024]{1,0:T(8,128)(2,1)S(1)}, u32[]{:S(2)}, u32[]{:S(2)}) collective-permute-start(bf16[96,1024]{1,0:T(8,128)(2,1)S(1)} %dynamic-slice_bitcast_fusion.2.refs_0_.grad_out), channel_id=1, source_target_pairs={{0,1},{1,0},{2,3},{3,2},{4,5},{5,4},{6,7},{7,6},{8,9},{9,8},{10,11... | collective-permute-start | bytes 589832 | tf_op jit(solution)/shard_map/ppermute | solution.py:307
  166.3 38.5 %collective-permute-start.37 = (bf16[96,1024]{1,0:T(8,128)(2,1)S(1)}, bf16[96,1024]{1,0:T(8,128)(2,1)S(1)}, u32[]{:S(2)}, u32[]{:S(2)}) collective-permute-start(bf16[96,1024]{1,0:T(8,128)(2,1)S(1)} %dynamic-slice_bitcast_fusion.2.refs_0_.grad_out), channel_id=1, source_target_pairs={{0,2},{1,3},{2,0},{3,1},{4,6},{5,7},{6,4},{7,5},{8,10},{9,11},{10,... | collective-permute-start | bytes 589832 | tf_op jit(solution)/shard_map/ppermute | solution.py:307
  169.6 35.3 %collective-permute-start.38 = (bf16[96,1024]{1,0:T(8,128)(2,1)S(1)}, bf16[96,1024]{1,0:T(8,128)(2,1)S(1)}, u32[]{:S(2)}, u32[]{:S(2)}) collective-permute-start(bf16[96,1024]{1,0:T(8,128)(2,1)S(1)} %dynamic-slice_bitcast_fusion.2.refs_0_.grad_out), channel_id=1, source_target_pairs={{0,3},{1,2},{2,1},{3,0},{4,7},{5,6},{6,5},{7,4},{8,11},{9,10},{10,... | collective-permute-start | bytes 589832 | tf_op jit(solution)/shard_map/ppermute | solution.py:307
  255.2 101.6 %reduce-scatter.13.cloned.1.call-start = ((), (), s32[]{:S(2)}) async-start(), calls=%async_computation.16 | async-start | bytes 589824 | tf_op jit(solution)/shard_map/reduce_scatter | solution.py:530
  292.3 84.0 %reduce-scatter.11.cloned.1.call-start = ((), (), s32[]{:S(2)}) async-start(), calls=%async_computation.15 | async-start | bytes 1769472 | tf_op jit(solution)/shard_map/reduce_scatter | solution.py:530
  295.9 98.5 %reduce-scatter.19.cloned.1.call-start = ((), (), s32[]{:S(2)}) async-start(), calls=%async_computation.19 | async-start | bytes 2359296 | tf_op jit(solution)/shard_map/reduce_scatter | solution.py:530
  299.7 131.6 %reduce-scatter.23.cloned.1.call-start = ((), (), s32[]{:S(2)}) async-start(), calls=%async_computation.21 | async-start | bytes 2359296 | tf_op jit(solution)/shard_map/reduce_scatter | solution.py:530
  303.9 162.4 %reduce-scatter.9.cloned.1.call-start = ((), (), s32[]{:S(2)}) async-start(), calls=%async_computation.14 | async-start | bytes 1769472 | tf_op jit(solution)/shard_map/reduce_scatter | solution.py:530
  307.2 195.7 %reduce-scatter.17.cloned.1.call-start = ((), (), s32[]{:S(2)}) async-start(), calls=%async_computation.18 | async-start | bytes 2359296 | tf_op jit(solution)/shard_map/reduce_scatter | solution.py:530
  311.3 228.7 %reduce-scatter.21.cloned.1.call-start = ((), (), s32[]{:S(2)}) async-start(), calls=%async_computation.20 | async-start | bytes 2359296 | tf_op jit(solution)/shard_map/reduce_scatter | solution.py:530
  354.7 18.3 %collective-permute-start.72 = (bf16[64,1024]{1,0:T(8,128)(2,1)S(1)}, bf16[64,1024]{1,0:T(8,128)(2,1)S(1)}, u32[]{:S(2)}, u32[]{:S(2)}) collective-permute-start(bf16[64,1024]{1,0:T(8,128)(2,1)S(1)} %constant_dynamic-update-slice_fusion.6), channel_id=1, source_target_pairs={{16,17},{17,16},{18,19},{19,18},{20,21},{21,20},{22,23},{23,22},{2... | collective-permute-start | bytes 393224 | tf_op jit(solution)/shard_map/ppermute | solution.py:310
  355.4 20.8 %collective-permute-start.74 = (bf16[64,1024]{1,0:T(8,128)(2,1)S(1)}, bf16[64,1024]{1,0:T(8,128)(2,1)S(1)}, u32[]{:S(2)}, u32[]{:S(2)}) collective-permute-start(bf16[64,1024]{1,0:T(8,128)(2,1)S(1)} %constant_dynamic-update-slice_fusion.6), channel_id=1, source_target_pairs={{16,18},{17,19},{18,16},{19,17},{20,22},{21,23},{22,20},{23,21},{2... | collective-permute-start | bytes 393224 | tf_op jit(solution)/shard_map/ppermute | solution.py:310
  356.1 21.5 %collective-permute-start.76 = (bf16[64,1024]{1,0:T(8,128)(2,1)S(1)}, bf16[64,1024]{1,0:T(8,128)(2,1)S(1)}, u32[]{:S(2)}, u32[]{:S(2)}) collective-permute-start(bf16[64,1024]{1,0:T(8,128)(2,1)S(1)} %constant_dynamic-update-slice_fusion.6), channel_id=1, source_target_pairs={{16,19},{17,18},{18,17},{19,16},{20,23},{21,22},{22,21},{23,20},{2... | collective-permute-start | bytes 393224 | tf_op jit(solution)/shard_map/ppermute | solution.py:310
  376.3 19.4 %collective-permute-start.62 = (bf16[128,768]{1,0:T(8,128)(2,1)}, bf16[128,768]{1,0:T(8,128)(2,1)S(1)}, u32[]{:S(2)}, u32[]{:S(2)}) collective-permute-start(bf16[128,768]{1,0:T(8,128)(2,1)} %reduce-scatter.11.cloned.1.call-done), channel_id=1, source_target_pairs={{0,16},{1,17},{2,18},{3,19},{4,20},{5,21},{6,22},{7,23},{8,24},{9,... | collective-permute-start | bytes 589832 | tf_op jit(solution)/shard_map/ppermute | solution.py:634
  394.4 73.4 %collective-permute-start.78 = (bf16[128,1024]{1,0:T(8,128)(2,1)}, bf16[128,1024]{1,0:T(8,128)(2,1)S(1)}, u32[]{:S(2)}, u32[]{:S(2)}) collective-permute-start(bf16[128,1024]{1,0:T(8,128)(2,1)} %reduce-scatter.19.cloned.1.call-done), channel_id=1, source_target_pairs={{0,16},{1,17},{2,18},{3,19},{4,20},{5,21},{6,22},{7,23},{8,24},{9,... | collective-permute-start | bytes 786440 | tf_op jit(solution)/shard_map/ppermute | solution.py:634
  396.7 84.9 %collective-permute-start.64 = (bf16[256,768]{1,0:T(8,128)(2,1)S(1)}, bf16[256,768]{1,0:T(8,128)(2,1)}, u32[]{:S(2)}, u32[]{:S(2)}) collective-permute-start(bf16[256,768]{1,0:T(8,128)(2,1)S(1)} %constant_dynamic-update-slice_fusion.2), channel_id=1, source_target_pairs={{16,17},{17,16},{18,19},{19,18},{20,21},{21,20},{22,23},{23,22},{2... | collective-permute-start | bytes 1179656 | tf_op jit(solution)/shard_map/ppermute | solution.py:310
  398.1 87.5 %collective-permute-start.66 = (bf16[256,768]{1,0:T(8,128)(2,1)S(1)}, bf16[256,768]{1,0:T(8,128)(2,1)}, u32[]{:S(2)}, u32[]{:S(2)}) collective-permute-start(bf16[256,768]{1,0:T(8,128)(2,1)S(1)} %constant_dynamic-update-slice_fusion.2), channel_id=1, source_target_pairs={{16,18},{17,19},{18,16},{19,17},{20,22},{21,23},{22,20},{23,21},{2... | collective-permute-start | bytes 1179656 | tf_op jit(solution)/shard_map/ppermute | solution.py:310
  399.5 109.5 %collective-permute-start.68 = (bf16[256,768]{1,0:T(8,128)(2,1)S(1)}, bf16[256,768]{1,0:T(8,128)(2,1)}, u32[]{:S(2)}, u32[]{:S(2)}) collective-permute-start(bf16[256,768]{1,0:T(8,128)(2,1)S(1)} %constant_dynamic-update-slice_fusion.2), channel_id=1, source_target_pairs={{16,19},{17,18},{18,17},{19,16},{20,23},{21,22},{22,21},{23,20},{2... | collective-permute-start | bytes 1179656 | tf_op jit(solution)/shard_map/ppermute | solution.py:310
  431.3 43.9 %collective-permute-start.86 = (bf16[128,1024]{1,0:T(8,128)(2,1)}, bf16[128,1024]{1,0:T(8,128)(2,1)S(1)}, u32[]{:S(2)}, u32[]{:S(2)}) collective-permute-start(bf16[128,1024]{1,0:T(8,128)(2,1)} %reduce-scatter.23.cloned.1.call-done), channel_id=1, source_target_pairs={{0,16},{1,17},{2,18},{3,19},{4,20},{5,21},{6,22},{7,23},{8,24},{9,... | collective-permute-start | bytes 786440 | tf_op jit(solution)/shard_map/ppermute | solution.py:634
  481.5 101.0 %collective-permute-start.80 = (bf16[256,1024]{1,0:T(8,128)(2,1)}, bf16[256,1024]{1,0:T(8,128)(2,1)}, u32[]{:S(2)}, u32[]{:S(2)}) collective-permute-start(bf16[256,1024]{1,0:T(8,128)(2,1)} %copy-done.42), channel_id=1, source_target_pairs={{16,17},{17,16},{18,19},{19,18},{20,21},{21,20},{22,23},{23,22},{2... | collective-permute-start | bytes 1572872 | tf_op jit(solution)/shard_map/ppermute | solution.py:310
  483.1 106.6 %collective-permute-start.82 = (bf16[256,1024]{1,0:T(8,128)(2,1)}, bf16[256,1024]{1,0:T(8,128)(2,1)}, u32[]{:S(2)}, u32[]{:S(2)}) collective-permute-start(bf16[256,1024]{1,0:T(8,128)(2,1)} %copy-done.42), channel_id=1, source_target_pairs={{16,18},{17,19},{18,16},{19,17},{20,22},{21,23},{22,20},{23,21},{2... | collective-permute-start | bytes 1572872 | tf_op jit(solution)/shard_map/ppermute | solution.py:310
  485.6 55.8 %collective-permute-start.67 = (bf16[256,768]{1,0:T(8,128)(2,1)}, bf16[256,768]{1,0:T(8,128)(2,1)}, u32[]{:S(2)}, u32[]{:S(2)}) collective-permute-start(bf16[256,768]{1,0:T(8,128)(2,1)} %constant_dynamic-update-slice_fusion), channel_id=1, source_target_pairs={{0,3},{1,2},{2,1},{3,0},{4,7},{5,6},{6,5},{7,4},{8,11},{9,10},{10,... | collective-permute-start | bytes 1179656 | tf_op jit(solution)/shard_map/ppermute | solution.py:310
  506.8 90.1 %collective-permute-start.84 = (bf16[256,1024]{1,0:T(8,128)(2,1)}, bf16[256,1024]{1,0:T(8,128)(2,1)}, u32[]{:S(2)}, u32[]{:S(2)}) collective-permute-start(bf16[256,1024]{1,0:T(8,128)(2,1)} %copy-done.42), channel_id=1, source_target_pairs={{16,19},{17,18},{18,17},{19,16},{20,23},{21,22},{22,21},{23,20},{2... | collective-permute-start | bytes 1572872 | tf_op jit(solution)/shard_map/ppermute | solution.py:310
  540.1 37.6 %collective-permute-start.85 = (bf16[128,1024]{1,0:T(8,128)(2,1)}, bf16[128,1024]{1,0:T(8,128)(2,1)S(1)}, u32[]{:S(2)}, u32[]{:S(2)}) collective-permute-start(bf16[128,1024]{1,0:T(8,128)(2,1)} %reduce-scatter.21.cloned.1.call-done), channel_id=1, source_target_pairs={{16,0},{17,1},{18,2},{19,3},{20,4},{21,5},{22,6},{23,7},{24,8},{25... | collective-permute-start | bytes 786440 | tf_op jit(solution)/shard_map/ppermute | solution.py:634
  541.4 43.1 %collective-permute-start.79 = (bf16[256,1024]{1,0:T(8,128)(2,1)}, bf16[256,1024]{1,0:T(8,128)(2,1)}, u32[]{:S(2)}, u32[]{:S(2)}) collective-permute-start(bf16[256,1024]{1,0:T(8,128)(2,1)} %constant_dynamic-update-slice_fusion.8), channel_id=1, source_target_pairs={{0,1},{1,0},{2,3},{3,2},{4,5},{5,4},{6,7},{7,6},{8,9},{9,8},{10,11... | collective-permute-start | bytes 1572872 | tf_op jit(solution)/shard_map/ppermute | solution.py:310
  577.7 13.5 %collective-permute-start.81 = (bf16[256,1024]{1,0:T(8,128)(2,1)}, bf16[256,1024]{1,0:T(8,128)(2,1)}, u32[]{:S(2)}, u32[]{:S(2)}) collective-permute-start(bf16[256,1024]{1,0:T(8,128)(2,1)} %constant_dynamic-update-slice_fusion.8), channel_id=1, source_target_pairs={{0,2},{1,3},{2,0},{3,1},{4,6},{5,7},{6,4},{7,5},{8,10},{9,11},{10,... | collective-permute-start | bytes 1572872 | tf_op jit(solution)/shard_map/ppermute | solution.py:310
  582.5 98.0 %collective-permute-start.88 = (bf16[256,1024]{1,0:T(8,128)(2,1)}, bf16[256,1024]{1,0:T(8,128)(2,1)}, u32[]{:S(2)}, u32[]{:S(2)}) collective-permute-start(bf16[256,1024]{1,0:T(8,128)(2,1)} %constant_dynamic-update-slice_fusion.14), channel_id=1, source_target_pairs={{16,17},{17,16},{18,19},{19,18},{20,21},{21,20},{22,23},{23,22},{2... | collective-permute-start | bytes 1572872 | tf_op jit(solution)/shard_map/ppermute | solution.py:310
  584.5 13.9 %collective-permute-start.83 = (bf16[256,1024]{1,0:T(8,128)(2,1)}, bf16[256,1024]{1,0:T(8,128)(2,1)}, u32[]{:S(2)}, u32[]{:S(2)}) collective-permute-start(bf16[256,1024]{1,0:T(8,128)(2,1)} %constant_dynamic-update-slice_fusion.8), channel_id=1, source_target_pairs={{0,3},{1,2},{2,1},{3,0},{4,7},{5,6},{6,5},{7,4},{8,11},{9,10},{10,... | collective-permute-start | bytes 1572872 | tf_op jit(solution)/shard_map/ppermute | solution.py:310
  589.7 95.6 %collective-permute-start.90 = (bf16[256,1024]{1,0:T(8,128)(2,1)}, bf16[256,1024]{1,0:T(8,128)(2,1)}, u32[]{:S(2)}, u32[]{:S(2)}) collective-permute-start(bf16[256,1024]{1,0:T(8,128)(2,1)} %constant_dynamic-update-slice_fusion.14), channel_id=1, source_target_pairs={{16,18},{17,19},{18,16},{19,17},{20,22},{21,23},{22,20},{23,21},{2... | collective-permute-start | bytes 1572872 | tf_op jit(solution)/shard_map/ppermute | solution.py:310
  591.2 91.8 %collective-permute-start.87 = (bf16[256,1024]{1,0:T(8,128)(2,1)}, bf16[256,1024]{1,0:T(8,128)(2,1)}, u32[]{:S(2)}, u32[]{:S(2)}) collective-permute-start(bf16[256,1024]{1,0:T(8,128)(2,1)} %constant_dynamic-update-slice_fusion.12), channel_id=1, source_target_pairs={{0,1},{1,0},{2,3},{3,2},{4,5},{5,4},{6,7},{7,6},{8,9},{9,8},{10,11... | collective-permute-start | bytes 1572872 | tf_op jit(solution)/shard_map/ppermute | solution.py:310
  596.9 90.5 %collective-permute-start.92 = (bf16[256,1024]{1,0:T(8,128)(2,1)}, bf16[256,1024]{1,0:T(8,128)(2,1)}, u32[]{:S(2)}, u32[]{:S(2)}) collective-permute-start(bf16[256,1024]{1,0:T(8,128)(2,1)} %constant_dynamic-update-slice_fusion.14), channel_id=1, source_target_pairs={{16,19},{17,18},{18,17},{19,16},{20,23},{21,22},{22,21},{23,20},{2... | collective-permute-start | bytes 1572872 | tf_op jit(solution)/shard_map/ppermute | solution.py:310
  598.4 86.8 %collective-permute-start.89 = (bf16[256,1024]{1,0:T(8,128)(2,1)}, bf16[256,1024]{1,0:T(8,128)(2,1)}, u32[]{:S(2)}, u32[]{:S(2)}) collective-permute-start(bf16[256,1024]{1,0:T(8,128)(2,1)} %constant_dynamic-update-slice_fusion.12), channel_id=1, source_target_pairs={{0,2},{1,3},{2,0},{3,1},{4,6},{5,7},{6,4},{7,5},{8,10},{9,11},{10,... | collective-permute-start | bytes 1572872 | tf_op jit(solution)/shard_map/ppermute | solution.py:310
  (120 other events, 1114.6 us)
Sparse Core Ops, SparseCore 0:
  12.0 28.7 all-gather.6
  42.9 32.1 all-gather.8
  77.3 28.5 all-gather.10
  108.0 24.5 all-gather.12
  134.6 28.9 all-gather.14
  165.5 28.5 all-gather.16
  255.4 29.2 reduce-scatter.14
  292.5 29.8 reduce-scatter.12
  324.6 32.7 reduce-scatter.10
  360.1 34.2 reduce-scatter.18
  396.7 34.5 reduce-scatter.22
  433.5 32.7 reduce-scatter.8
  469.1 33.6 reduce-scatter.16
  505.5 34.4 reduce-scatter.20

commit v2 on v1

--- a/solution.py
+++ b/solution.py
@@ -8,6 +8,9 @@
 from jax.sharding import PartitionSpec as P
 
 HEADS = 16
+TIE_DOWN = 3
+TIE_UP = 4
+COPY_DOWN = 5
 NORM_EPS = 1e-05
 GELU_COEF = 0.7978845608028654
 GELU_CUBE = 0.044715
@@ -27,7 +30,7 @@
     return lax.dot_general(left, right, (((0,), (0,)), ((), ())), preferred_element_type=F32)
 
 
-def call(kernel, outs, args, flops=0):
+def call(kernel, outs, args, flops=0, scalars=None):
     nbytes = sum(a.size * a.dtype.itemsize for a in args) + sum(
         math.prod(o.shape) * jnp.dtype(o.dtype).itemsize for o in outs
     )
@@ -35,11 +38,12 @@
     return pl.pallas_call(
         kernel,
         out_shape=outs,
-        in_specs=[vmem] * len(args),
+        in_specs=[pl.BlockSpec(memory_space=pltpu.SMEM)] * (scalars is not None)
+        + [vmem] * len(args),
         out_specs=[vmem] * len(outs),
-        compiler_params=pltpu.CompilerParams(vmem_limit_bytes=50 * 2**20),
+        compiler_params=pltpu.CompilerParams(vmem_limit_bytes=40 * 2**20),
         cost_estimate=pl.CostEstimate(flops=flops, bytes_accessed=nbytes, transcendentals=0),
-    )(*args)
+    )(*(([] if scalars is None else [scalars]) + list(args)))
 
 
 def sds(shape, dtype=LOW):
@@ -294,6 +298,171 @@
     return kernel
 
 
+def at_block(index, size):
+    return pl.ds(pl.multiple_of(index * size, size), size)
+
+
+def prepare_attention_kernel(where, heads, merge, left, right, kept, sent):
+    core, rep = where[0], where[1]
+    block, step = left.shape
+    run = step // 2
+    half = kept.shape[0]
+    width = kept.shape[1] // 4
+    packed = []
+    for m in range(3 * width // step):
+        first = dot(heads[:, 2 * m * block : (2 * m + 1) * block], left[...])
+        second = dot(heads[:, (2 * m + 1) * block : (2 * m + 2) * block], right[...])
+        packed.append((first + second).astype(LOW))
+    own = merge[at_block(rep, run), :]
+    packed.append(
+        jnp.concatenate(
+            [own[:, j * width : (j + 1) * width] for j in range(2 * half // run)], axis=0
+        )
+    )
+    rows = jnp.concatenate(packed, axis=1)
+    first = core == 0
+    kept[...] = jnp.where(first, rows[:half], rows[half:])
+    sent[...] = jnp.where(first, rows[half:], rows[:half])
+
+
+def prepare_mlp_kernel(where, up, down, kept, sent):
+    core, rep = where[0], where[1]
+    half = kept.shape[0] // 2
+    ff_own = kept.shape[1]
+    run = 2 * half
+    reps = up.shape[1] // ff_own
+    for target, which in ((kept, core), (sent, 1 - core)):
+        rows = at_block(which, half)
+        for m in range(ff_own // run):
+            target[:half, m * run : (m + 1) * run] = up[rows, at_block(m * reps + rep, run)]
+        target[half:, :] = down[at_block(2 * rep + which, half), :]
+
+
+def make_assemble_attention(shards):
+    def kernel(where, *refs):
+        core, shard = where[0], where[2]
+        heads, merge = refs[2 * shards :]
+        half = refs[0].shape[0]
+        width = merge.shape[0]
+        run = width // shards
+        for number, ref in enumerate(refs[: 2 * shards]):
+            source = lax.rem(shard - number % shards + shards, shards)
+            which = core if number < shards else 1 - core
+            heads[at_block(2 * source + which, half), :] = ref[:, : 3 * width]
+            for j in range(half // run):
+                merge[at_block(source, run), at_block(which * (half // run) + j, width)] = ref[
+                    j * run : (j + 1) * run, 3 * width :
+                ]
+
+    return kernel
+
+
+def make_assemble_mlp(shards):
+    def kernel(where, *refs):
+        core, shard = where[0], where[2]
+        up, down = refs[2 * shards :]
+        half = refs[0].shape[0] // 2
+        for number, ref in enumerate(refs[: 2 * shards]):
+            source = lax.rem(shard - number % shards + shards, shards)
+            which = core if number < shards else 1 - core
+            rows = at_block(2 * source + which, half)
+            up[rows, :] = ref[:half, :]
+            down[rows, :] = ref[half:, :]
+
+    return kernel
+
+
+def split_by_core(core, product, kept, sent, shards):
+    half = product.shape[0] // (2 * shards)
+    first = core == 0
+    for b in range(shards):
+        one = product[2 * b * half : (2 * b + 1) * half]
+        two = product[(2 * b + 1) * half : (2 * b + 2) * half]
+        kept[b * half : (b + 1) * half, : one.shape[1]] = jnp.where(first, one, two)
+        sent[b * half : (b + 1) * half, : one.shape[1]] = jnp.where(first, two, one)
+
+
+def make_weight_gradient(shards):
+    def kernel(where, left, right, kept, sent):
+        split_by_core(where[0], t_dot(left[...], right[...]).astype(LOW), kept, sent, shards)
+
+    return kernel
+
+
+def make_attention_gradient(shards):
+    def kernel(where, normed, joint, attended, merge, kept, sent):
+        core = where[0]
+        split_by_core(core, t_dot(normed[...], joint[...]).astype(LOW), kept, sent, shards)
+        product = t_dot(attended[...], merge[...]).astype(LOW)
+        width = product.shape[0]
+        run = width // shards
+        half = kept.shape[0] // shards
+        count = half // run
+        first = core == 0
+        for b in range(shards):
+            rows = product[b * run : (b + 1) * run]
+            for j in range(count):
+                one = rows[:, j * width : (j + 1) * width]
+                two = rows[:, (count + j) * width : (count + j + 1) * width]
+                at = slice(b * half + j * run, b * half + (j + 1) * run)
+                kept[at, 3 * width :] = jnp.where(first, one, two)
+                sent[at, 3 * width :] = jnp.where(first, two, one)
+
+    return kernel
+
+
+def chosen(core, refs, number, count):
+    return jnp.where(core == 0, refs[number][...], refs[count + number][...])
+
+
+def make_place_attention(parts):
+    def kernel(where, *refs):
+        core, rep = where[0], where[1]
+        place, heads, merge = refs[2 * parts :]
+        run = place.shape[1]
+        wide = place.shape[2]
+        width = heads.shape[1] // (3 * parts)
+        pieces = [chosen(core, refs, k, parts) for k in range(parts)]
+        for m in range(heads.shape[1] // wide):
+            total = dot(pieces[0][:, m * run : (m + 1) * run], place[0])
+            for k in range(1, parts):
+                total = total + dot(pieces[k][:, m * run : (m + 1) * run], place[k])
+            heads[:, m * wide : (m + 1) * wide] = total
+        for k in range(parts):
+            for j in range(pieces[k].shape[0] // run):
+                merge[at_block(jnp.bitwise_xor(rep, k), run), j * width : (j + 1) * width] = pieces[
+                    k
+                ][j * run : (j + 1) * run, 3 * width :].astype(F32)
+
+    return kernel
+
+
+def make_place_up(parts):
+    def kernel(where, *refs):
+        core, rep = where[0], where[1]
+        out = refs[2 * parts]
+        run = out.shape[0]
+        for k in range(parts):
+            piece = chosen(core, refs, k, parts).astype(F32)
+            for m in range(piece.shape[1] // run):
+                out[:, at_block(m * parts + jnp.bitwise_xor(rep, k), run)] = piece[
+                    :, m * run : (m + 1) * run
+                ]
+
+    return kernel
+
+
+def make_place_down(parts):
+    def kernel(where, *refs):
+        core, rep = where[0], where[1]
+        out = refs[2 * parts]
+        for k in range(parts):
+            piece = chosen(core, refs, k, parts).astype(F32)
+            out[at_block(jnp.bitwise_xor(rep, k), piece.shape[0]), :] = piece
+
+    return kernel
+
+
 def swap(block):
     return lax.ppermute(block, "section", [(0, 1), (1, 0)])
 
@@ -309,6 +478,60 @@
             pairs = [(section * count + i, section * count + (i ^ k)) for i in range(count)]
             received.append(lax.ppermute(blocks[k], ("section", axis), pairs))
     return [blocks[0]] + received
+
+
+def after(value, other):
+    return lax.optimization_barrier((value, other))[0]
+
+
+def ring_gather(block):
+    count = lax.axis_size("shard")
+    blocks = [block]
+    for _ in range(count - 1):
+        blocks.append(
+            lax.ppermute(blocks[-1], "shard", [(i, (i + 1) % count) for i in range(count)])
+        )
+    return blocks + [swap(b) for b in blocks]
+
+
+class GradientSum:
+    def __init__(self, pair, section, tie=None, copy=None):
+        self.section, self.tie, self.copy, self.age = section, tie, copy, 0
+        self.state, self.stage = list(pair), 0
+
+    def advance(self):
+        self.age += 1
+        if self.age in (1, self.tie, self.copy):
+            self.next_stage()
+            return True
+        return False
+
+    def next_stage(self):
+        self.stage += 1
+        s = self.section
+        if self.stage == 1:
+            kept, arrived = self.state[0], swap(self.state[1])
+            self.state = (kept.astype(F32) + arrived.astype(F32)).astype(LOW)
+        elif self.stage == 2:
+            self.state = lax.psum_scatter(self.state, "shard", scatter_dimension=0, tiled=True)
+        elif self.stage == 3:
+            theirs = lax.ppermute(self.state, "section", [(1 - s, s)])
+            order = [self.state, theirs] if s == 0 else [theirs, self.state]
+            self.state = gathered_blocks(jnp.concatenate(order, axis=0), "rep", s)
+
+    def finish(self):
+        while self.stage < 3:
+            self.next_stage()
+        return self.state
+
+
+def window(waiting, tasks, new=()):
+    tied = [task for task in tasks if task.advance()] + list(new)
+    tasks.extend(new)
+    waiting, states = lax.optimization_barrier((waiting, [task.state for task in tied]))
+    for task, state in zip(tied, states):
+        task.state = state
+    return waiting
 
 
 def gathered_blocks(block, axis, section=None):
@@ -354,6 +577,9 @@
     depth = features // shards
     strided = HEADS % (shards * reps) == 0
     head_run = (HEADS // (shards * reps)) * head_size if strided else width
+    fast = strided and depth == reps * head_run and (ff_own // shards) == depth
+    fast = fast and ff_own == features and depth % 256 == 0 and width == depth
+    where = jnp.stack([core, rep, shard]).astype(jnp.int32)
 
     def rows_of_core(array, which):
         return lax.dynamic_index_in_dim(
@@ -415,41 +641,80 @@
         value = own_heads_part(vector(s, 3))
         return jnp.concatenate([query, jnp.zeros_like(query), value], axis=1)
 
-    if strided:
+    weights = []
+    if fast:
         lane = jnp.arange(reps * head_run, dtype=jnp.int32)[:, None]
-        place = jnp.arange(2 * head_run, dtype=jnp.int32)[None, :]
-        hit = lane == rep * head_run + place % head_run
-        left = jnp.logical_and(hit, place < head_run).astype(LOW)
-        right = jnp.logical_and(hit, place >= head_run).astype(LOW)
-        heads_part = call(
-            pick_columns_kernel, [sds((depth, 3 * width))], [heads_weight[0], left, right]
-        )[0]
-        merge_part = lax.dynamic_slice_in_dim(merge_weight[0], rep * head_run, head_run, 0)
+        column = jnp.arange(2 * head_run, dtype=jnp.int32)[None, :]
+        hit = lane == rep * head_run + column % head_run
+        left = jnp.logical_and(hit, column < head_run).astype(LOW)
+        right = jnp.logical_and(hit, column >= head_run).astype(LOW)
+        half = sds((depth // 2, 4 * width))
+        kept_a, sent_a = call(
+            prepare_attention_kernel,
+            [half, half],
+            [heads_weight[0], merge_weight[0], left, right],
+            scalars=where,
+        )
+        whole = sds((depth, ff_own))
+        other_a = swap(sent_a)
+        kept_b, sent_b = call(
+            prepare_mlp_kernel,
+            [whole, whole],
+            [up_weight[0], down_weight[0]],
+            scalars=after(where, other_a),
+        )
+        other_b = swap(sent_b)
+
+    def attention_weights(s, then):
+        mine = on_first if s == 0 else jnp.logical_not(on_first)
+        blocks = ring_gather(after(jnp.where(mine, kept_a, other_a), then))
+        outs = [sds((features, 3 * width)), sds((width, features))]
+        return call(make_assemble_attention(shards), outs, blocks, scalars=where), blocks
+
+    def mlp_weights(s, then):
+        mine = on_first if s == 0 else jnp.logical_not(on_first)
+        blocks = ring_gather(after(jnp.where(mine, kept_b, other_b), then))
+        outs = [sds((features, ff_own)), sds((ff_own, features))]
+        return call(make_assemble_mlp(shards), outs, blocks, scalars=where), blocks
+
+    if fast:
+        first_pair, blocks_a = attention_weights(0, other_a)
+        weights.append(list(first_pair))
     else:
-        heads_part = lax.dynamic_index_in_dim(
-            heads_weight.reshape(depth, 3, reps, width), rep, 2, keepdims=False
-        ).reshape(depth, 3 * width)
-        merge_part = merge_weight[0]
-    up_part = lax.dynamic_index_in_dim(
-        up_weight.reshape(depth, shards, reps, ff_own // shards), rep, 2, keepdims=False
-    ).reshape(depth, ff_own)
-    down_part = lax.dynamic_slice_in_dim(
-        down_weight[0], rep * (ff_own // shards), ff_own // shards, 0
-    )
-
-    weights = []
-    halves = []
-    for part in (heads_part, merge_part, up_part, down_part):
-        kept = rows_of_core(part, core)
-        other = swap(rows_of_core(part, 1 - core))
-        halves.append((jnp.where(on_first, kept, other), jnp.where(on_first, other, kept)))
-    for s in range(sections):
-        full = [
-            lax.all_gather(pair[s], ("shard", "section"), axis=0, tiled=True) for pair in halves
-        ]
-        if not strided:
-            full[1] = lax.dynamic_slice_in_dim(full[1], rep * width, width, 0)
-        weights.append(full)
+        if strided:
+            lane = jnp.arange(reps * head_run, dtype=jnp.int32)[:, None]
+            place = jnp.arange(2 * head_run, dtype=jnp.int32)[None, :]
+            hit = lane == rep * head_run + place % head_run
+            left = jnp.logical_and(hit, place < head_run).astype(LOW)
+            right = jnp.logical_and(hit, place >= head_run).astype(LOW)
+            heads_part = call(
+                pick_columns_kernel, [sds((depth, 3 * width))], [heads_weight[0], left, right]
+            )[0]
+            merge_part = lax.dynamic_slice_in_dim(merge_weight[0], rep * head_run, head_run, 0)
+        else:
+            heads_part = lax.dynamic_index_in_dim(
+                heads_weight.reshape(depth, 3, reps, width), rep, 2, keepdims=False
+            ).reshape(depth, 3 * width)
+            merge_part = merge_weight[0]
+        up_part = lax.dynamic_index_in_dim(
+            up_weight.reshape(depth, shards, reps, ff_own // shards), rep, 2, keepdims=False
+        ).reshape(depth, ff_own)
+        down_part = lax.dynamic_slice_in_dim(
+            down_weight[0], rep * (ff_own // shards), ff_own // shards, 0
+        )
+
+        halves = []
+        for part in (heads_part, merge_part, up_part, down_part):
+            kept = rows_of_core(part, core)
+            other = swap(rows_of_core(part, 1 - core))
+            halves.append((jnp.where(on_first, kept, other), jnp.where(on_first, other, kept)))
+        for s in range(sections):
+            full = [
+                lax.all_gather(pair[s], ("shard", "section"), axis=0, tiled=True) for pair in halves
+            ]
+            if not strided:
+                full[1] = lax.dynamic_slice_in_dim(full[1], rep * width, width, 0)
+            weights.append(full)
 
     own_lengths = rows_of_core(doc_lengths, core)
     lengths = jnp.concatenate(gathered_blocks(own_lengths, "rep"), axis=0)
@@ -474,6 +739,10 @@
     saved = []
     outputs = []
     for s in range(sections):
+        normed_blocks = gathered_blocks(normed, "rep")
+        if fast:
+            second_pair, _ = mlp_weights(s, other_b if s == 0 else blocks_a[shards - 1])
+            weights[s] += list(second_pair)
         wh, wm, wu, wd = weights[s]
         results = call(
             make_attention_forward(reps, head_size),
@@ -484,11 +753,14 @@
                 sds((all_rows, width)),
             ]
             + block_shapes,
-            gathered_blocks(normed, "rep") + [wh, joint_vector(s), visible, wm],
+            normed_blocks + [wh, joint_vector(s), visible, wm],
             attention_flops,
         )
         normed_all, joint, probs, attended = results[:4]
         terms = from_peers(results[4:], "rep")
+        if fast and s + 1 < sections:
+            first_pair, _ = attention_weights(s + 1, blocks_a[shards - 1])
+            weights.append(list(first_pair))
         middle, second = call(
             make_middle(reps),
             [sds((n, features), F32), sds((n, features))],
@@ -524,6 +796,7 @@
     hidden_grads = [None] * sections
     vector_grads = [None] * sections
     weight_grads = [None] * sections
+    tasks = []
 
     def over_slots(left, right):
         product = t_dot(left, right).astype(LOW)
@@ -533,22 +806,45 @@
         wh, wm, wu, wd = weights[s]
         hidden, normed_all, joint, probs, attended, middle, second_all, before, active = saved[s]
         row = sds((1, features), F32)
+        out_blocks = gathered_blocks(grad_out, "rep")
+        if tasks:
+            out_blocks = window(out_blocks, tasks)
         results = call(
             make_mlp_backward(reps),
             [sds((all_rows, features)), sds((all_rows, ff_own)), sds((1, ff_own), F32)]
             + block_shapes,
-            gathered_blocks(grad_out, "rep") + [wd, wu, before],
+            out_blocks + [wd, wu, before],
             mlp_flops,
         )
         down_all, before_all, up_sum = results[:3]
         terms = from_peers(results[3:], "rep")
-        grad_down = over_slots(active, down_all)
-        grad_up = over_slots(second_all, before_all)
+        if fast:
+            piece = sds((features // 2, features))
+            flops = 2 * all_rows * features * features
+            down_pair = call(
+                make_weight_gradient(shards), [piece, piece], [active, down_all], flops, where
+            )
+            grad_down = GradientSum(down_pair, s, TIE_DOWN, COPY_DOWN)
+            terms = window(terms, tasks, [grad_down])
+        else:
+            grad_down = over_slots(active, down_all)
+            grad_up = over_slots(second_all, before_all)
         g_middle, g_merge, second_gain_sum, second_shift_sum, output_sum, down_sum = call(
             make_middle_backward(reps),
             [sds((n, features), F32), sds((n, features))] + [row] * 4,
             [grad_out, middle] + terms + [vector(s, 5)],
         )
+        merge_blocks = gathered_blocks(g_merge, "rep")
+        if fast:
+            up_pair = call(
+                make_weight_gradient(shards),
+                [piece, piece],
+                [second_all, before_all],
+                flops,
+                after(where, g_merge),
+            )
+            grad_up = GradientSum(up_pair, s, TIE_UP)
+            merge_blocks = window(merge_blocks, tasks, [grad_up])
         results = call(
             make_attention_backward(reps, head_size),
             [
@@ -558,15 +854,26 @@
                 sds((1, width), F32),
             ]
             + block_shapes,
-            gathered_blocks(g_merge, "rep") + [wm, wh, joint, probs],
+            merge_blocks + [wm, wh, joint, probs],
             2 * attention_flops,
         )
         merge_all, joint_all, query_sum, value_sum = results[:4]
         terms = from_peers(results[4:], "rep")
-        grad_heads = over_slots(normed_all, joint_all)
-        if strided:
+        if fast:
+            both_pair = call(
+                make_attention_gradient(shards),
+                [piece, piece],
+                [normed_all, joint_all, attended, merge_all],
+                flops,
+                where,
+            )
+            grad_heads, grad_merge = GradientSum(both_pair, s), None
+            terms = window(terms, tasks, [grad_heads])
+        elif strided:
+            grad_heads = over_slots(normed_all, joint_all)
             grad_merge = over_slots(attended, merge_all)
         else:
+            grad_heads = over_slots(normed_all, joint_all)
             product = t_dot(attended, merge_all).astype(LOW)
             spread = lax.dynamic_update_slice_in_dim(
                 jnp.zeros((features, features), LOW), product, rep * width, 0
@@ -640,47 +947,74 @@
         lists = [gathered_blocks(parts[s], "rep", s) for s in range(sections)]
         return [jnp.where(on_first, a, b) for a, b in zip(*lists)]
 
-    heads_pieces = over_reps(0)
-    if strided:
+    if fast:
+
+        def both_sections(number):
+            return [p for s in range(sections) for p in weight_grads[s][number].finish()]
+
+        grad_up = call(
+            make_place_up(reps), [sds((depth, ff), F32)], both_sections(2), scalars=where
+        )[0][None]
+        grad_down = call(
+            make_place_down(reps),
+            [sds((ff // shards, features), F32)],
+            both_sections(3),
+            scalars=where,
+        )[0][None]
         lane = jnp.arange(head_run, dtype=jnp.int32)[:, None]
-        place = jnp.arange(reps * head_run, dtype=jnp.int32)[None, :]
+        column = jnp.arange(reps * head_run, dtype=jnp.int32)[None, :]
         places = jnp.stack(
-            [(place == (rep ^ k) * head_run + lane).astype(LOW) for k in range(reps)]
-        )
-        grad_heads = call(
-            make_spread_columns(reps),
-            [sds((depth, 3 * features), F32)],
-            heads_pieces + [places],
-        )[0][None]
-        merge_pieces = over_reps(1)
-        grad_merge = jnp.zeros((reps, head_run, features), F32)
-        for k, piece in enumerate(merge_pieces):
-            grad_merge = lax.dynamic_update_slice_in_dim(
-                grad_merge, piece.astype(F32)[None], rep ^ k, 0
+            [(column == (rep ^ k) * head_run + lane).astype(LOW) for k in range(reps)]
+        )
+        grad_heads, grad_merge = call(
+            make_place_attention(reps),
+            [sds((depth, 3 * features), F32), sds((depth, features), F32)],
+            both_sections(0) + [places],
+            scalars=where,
+        )
+        grad_heads, grad_merge = grad_heads[None], grad_merge[None]
+    else:
+        heads_pieces = over_reps(0)
+        if strided:
+            lane = jnp.arange(head_run, dtype=jnp.int32)[:, None]
+            place = jnp.arange(reps * head_run, dtype=jnp.int32)[None, :]
+            places = jnp.stack(
+                [(place == (rep ^ k) * head_run + lane).astype(LOW) for k in range(reps)]
             )
-        grad_merge = grad_merge.reshape(1, depth, features)
-    else:
-        grad_heads = jnp.zeros((depth, 3, reps, width), F32)
-        for k, piece in enumerate(heads_pieces):
-            grad_heads = lax.dynamic_update_slice_in_dim(
-                grad_heads, piece.astype(F32).reshape(depth, 3, 1, width), rep ^ k, 2
+            grad_heads = call(
+                make_spread_columns(reps),
+                [sds((depth, 3 * features), F32)],
+                heads_pieces + [places],
+            )[0][None]
+            merge_pieces = over_reps(1)
+            grad_merge = jnp.zeros((reps, head_run, features), F32)
+            for k, piece in enumerate(merge_pieces):
+                grad_merge = lax.dynamic_update_slice_in_dim(
+                    grad_merge, piece.astype(F32)[None], rep ^ k, 0
+                )
+            grad_merge = grad_merge.reshape(1, depth, features)
+        else:
+            grad_heads = jnp.zeros((depth, 3, reps, width), F32)
+            for k, piece in enumerate(heads_pieces):
+                grad_heads = lax.dynamic_update_slice_in_dim(
+                    grad_heads, piece.astype(F32).reshape(depth, 3, 1, width), rep ^ k, 2
+                )
+            grad_heads = grad_heads.reshape(1, depth, 3 * features)
+            parts = owned(1)
+            grad_merge = lax.psum(jnp.where(on_first, parts[0], parts[1]), "rep").astype(F32)[None]
+
+        grad_up = jnp.zeros((depth, shards, reps, ff_own // shards), F32)
+        for k, piece in enumerate(over_reps(2)):
+            grad_up = lax.dynamic_update_slice_in_dim(
+                grad_up, piece.astype(F32).reshape(depth, shards, 1, ff_own // shards), rep ^ k, 2
             )
-        grad_heads = grad_heads.reshape(1, depth, 3 * features)
-        parts = owned(1)
-        grad_merge = lax.psum(jnp.where(on_first, parts[0], parts[1]), "rep").astype(F32)[None]
-
-    grad_up = jnp.zeros((depth, shards, reps, ff_own // shards), F32)
-    for k, piece in enumerate(over_reps(2)):
-        grad_up = lax.dynamic_update_slice_in_dim(
-            grad_up, piece.astype(F32).reshape(depth, shards, 1, ff_own // shards), rep ^ k, 2
-        )
-    grad_up = grad_up.reshape(1, depth, ff)
-    grad_down = jnp.zeros((reps, ff_own // shards, features), F32)
-    for k, piece in enumerate(over_reps(3)):
-        grad_down = lax.dynamic_update_slice_in_dim(
-            grad_down, piece.astype(F32)[None], rep ^ k, 0
-        )
-    grad_down = grad_down.reshape(1, ff // shards, features)
+        grad_up = grad_up.reshape(1, depth, ff)
+        grad_down = jnp.zeros((reps, ff_own // shards, features), F32)
+        for k, piece in enumerate(over_reps(3)):
+            grad_down = lax.dynamic_update_slice_in_dim(
+                grad_down, piece.astype(F32)[None], rep ^ k, 0
+            )
+        grad_down = grad_down.reshape(1, ff // shards, features)
 
     def by_section(pair):
         own = jnp.where(on_first, pair[0], pair[1])

time: 711 us -> 479 us (0.67)
  local copies, waits for them, and re-layouts: 150 us -> 57.6 us
  waiting for transfers between devices: 264 us -> 175 us
  blocking collectives: 33.2 us -> 0 us
  matrix products: 25 us -> 0 us
  Pallas kernels: 45.6 us -> 60.3 us
    reduce_scatter x8 -> x6, waiting for transfers between devices: 119 us -> 11.4 us  [next_stage(): lax.psum_scatter(self.state, 'shard', scatter_dimension=0, tiled=True)]
    dynamic_update_slice x4 -> x0, local copies, waits for them, and re-layouts: 91 us -> none  [body(): lax.dynamic_update_slice_in_dim(grad_up, piece.astype(F32).reshape(depth,...]
    ppermute x8 -> x18, waiting for transfers between devices: 7.42 us -> 56.3 us  [the longest x12 54.4 us: ring_gather(): lax.ppermute(blocks[-1], 'shard', [(i, (i + 1) % count) for i in range(co...]
    all_gather x2 -> x0, blocking collectives: 33.2 us -> none  [body(): lax.all_gather(pair[s], ('shard', 'section'), axis=0, tiled=True)]
    all_gather x6 -> x0, waiting for transfers between devices: 32.9 us -> none  [body(): lax.all_gather(pair[s], ('shard', 'section'), axis=0, tiled=True)]
    unnamed x118 -> x280, local copies, waits for them, and re-layouts: 20.1 us -> 51.6 us
    dot_general x8 -> x0, matrix products: 25 us -> none  [t_dot(): lax.dot_general(left, right, (((0,), (0,)), ((), ())), preferred_element_...]
    reshape x5 -> x0, local copies, waits for them, and re-layouts: 15.4 us -> none  [the longest x1 5.91 us: body(): grad_up = grad_up.reshape(1, depth, ff)]
  transfers between devices with their start and end apart: 114 -> 130, of which waited for: 49 -> 49; matrix products, arithmetic and copies ran while one was open for 26% -> 6% of each run, Pallas kernels for 5% -> 11%
where the time goes in v2:
time: 479 us; the launch traced here: 470 us
  waiting for transfers between devices  175 us (37%)
  starting transfers between devices  140 us (29%)
  Pallas kernels  60.3 us (13%)
  local copies, waits for them, and re-layouts  57.6 us (12%)
  other arithmetic  20.1 us (4%)
  between operations  16.5 us (3%)
    ppermute x60, waiting for transfers between devices, from_peers(): received.append(lax.ppermute(blocks[k], axis, pairs))  90.3 us
    ppermute x60, starting transfers between devices, from_peers(): received.append(lax.ppermute(blocks[k], axis, pairs))  75.8 us
    pallas_call x32, Pallas kernels, call(): pl.pallas_call(kernel, out_shape=outs, in_specs=[pl.BlockSpec(memory_spac...  60.3 us
    ppermute x12, waiting for transfers between devices, ring_gather(): lax.ppermute(blocks[-1], 'shard', [(i, (i + 1) % count) for i in range(co...  54.4 us
    unnamed x280, local copies, waits for them, and re-layouts  51.6 us
    ppermute x18, starting transfers between devices, from_peers(): received.append(lax.ppermute(blocks[k], ('section', axis), pairs))  40 us
    ppermute x18, waiting for transfers between devices, from_peers(): received.append(lax.ppermute(blocks[k], ('section', axis), pairs))  16.8 us
    reduce_scatter x6, waiting for transfers between devices, next_stage(): lax.psum_scatter(self.state, 'shard', scatter_dimension=0, tiled=True)  11.4 us
  transfers between devices with their start and end apart: 130, of which 49 were waited for; matrix products, arithmetic and copies ran while one was open for 6% of the time, Pallas kernels for 11%

profile of v2, /device:TPU:0, one launch (start us, length us, event | category | flops | bytes accessed | tf_op | source)
XLA Modules:
  0.0 469.9 jit_solution(4919238157754036977)
XLA Ops:
  12.5 4.7 collective-permute-start
  23.2 9.2 %collective-permute-done.8.refs_1_ = bf16[128,1024]{1,0:T(8,128)(2,1)S(1)} collective-permute-done((bf16[128,1024]{1,0:T(8,128)(2,1)S(1)}, bf16[128,1024]{1,0:T(8,128)(2,1)S(1)}, u32[]{:S(2)}, u32[]{:S(2)}) %collective-permute-start.8) | collective-permute-done | bytes 262176 | tf_op jit(solution)/shard_map/ppermute | solution.py:492
  47.7 15.1 %collective-permute-done.10.refs_3_ = bf16[128,1024]{1,0:T(8,128)(2,1)S(1)} collective-permute-done((bf16[128,1024]{1,0:T(8,128)(2,1)}, bf16[128,1024]{1,0:T(8,128)(2,1)S(1)}, u32[]{:S(2)}, u32[]{:S(2)}) %collective-permute-start.10) | collective-permute-done | bytes 262176 | tf_op jit(solution)/shard_map/ppermute | solution.py:492
  70.5 8.6 %collective-permute-done.26.refs_2_ = bf16[256,1024]{1,0:T(8,128)(2,1)} collective-permute-done((bf16[256,1024]{1,0:T(8,128)(2,1)S(1)}, bf16[256,1024]{1,0:T(8,128)(2,1)}, u32[]{:S(2)}, u32[]{:S(2)}) %collective-permute-start.26) | collective-permute-done | bytes 524320 | tf_op jit(solution)/shard_map/ppermute | solution.py:492
  86.0 4.0 shard_map.274
  93.9 7.6 %collective-permute-done.38.refs_1_ = bf16[128,1024]{1,0:T(8,128)(2,1)S(1)} collective-permute-done((bf16[128,1024]{1,0:T(8,128)(2,1)S(1)}, bf16[128,1024]{1,0:T(8,128)(2,1)S(1)}, u32[]{:S(2)}, u32[]{:S(2)}) %collective-permute-start.38) | collective-permute-done | bytes 262176 | tf_op jit(solution)/shard_map/ppermute | solution.py:492
  103.6 6.2 %collective-permute-done.20.refs_3_ = bf16[96,1024]{1,0:T(8,128)(2,1)S(1)} collective-permute-done((bf16[96,1024]{1,0:T(8,128)(2,1)S(1)}, bf16[96,1024]{1,0:T(8,128)(2,1)S(1)}, u32[]{:S(2)}, u32[]{:S(2)}) %collective-permute-start.20) | collective-permute-done | bytes 196640 | tf_op jit(solution)/shard_map/ppermute | solution.py:476
  112.0 7.0 %collective-permute-done.39.refs_2_ = bf16[128,1024]{1,0:T(8,128)(2,1)S(1)} collective-permute-done((bf16[128,1024]{1,0:T(8,128)(2,1)S(1)}, bf16[128,1024]{1,0:T(8,128)(2,1)S(1)}, u32[]{:S(2)}, u32[]{:S(2)}) %collective-permute-start.39) | collective-permute-done | bytes 262176 | tf_op jit(solution)/shard_map/ppermute | solution.py:492
  124.9 3.5 collective-permute-done.22.refs_2_
  134.7 5.4 %collective-permute-done.40.refs_3_ = bf16[128,1024]{1,0:T(8,128)(2,1)S(1)} collective-permute-done((bf16[128,1024]{1,0:T(8,128)(2,1)S(1)}, bf16[128,1024]{1,0:T(8,128)(2,1)S(1)}, u32[]{:S(2)}, u32[]{:S(2)}) %collective-permute-start.40) | collective-permute-done | bytes 262176 | tf_op jit(solution)/shard_map/ppermute | solution.py:492
  142.1 6.3 %collective-permute-done.34.refs_3_ = bf16[96,1024]{1,0:T(8,128)(2,1)S(1)} collective-permute-done((bf16[96,1024]{1,0:T(8,128)(2,1)S(1)}, bf16[96,1024]{1,0:T(8,128)(2,1)S(1)}, u32[]{:S(2)}, u32[]{:S(2)}) %collective-permute-start.34) | collective-permute-done | bytes 196640 | tf_op jit(solution)/shard_map/ppermute | solution.py:476
  153.2 3.6 collective-permute-done.35.refs_1_
  156.8 3.5 collective-permute-done.36.refs_2_
  166.8 3.0 collective-permute-done.45.refs_1_
  173.6 5.4 %collective-permute-done.47.refs_3_ = bf16[96,1024]{1,0:T(8,128)(2,1)S(1)} collective-permute-done((bf16[96,1024]{1,0:T(8,128)(2,1)S(1)}, bf16[96,1024]{1,0:T(8,128)(2,1)S(1)}, u32[]{:S(2)}, u32[]{:S(2)}) %collective-permute-start.47) | collective-permute-done | bytes 196640 | tf_op jit(solution)/shard_map/ppermute | solution.py:476
  198.2 2.6 shard_map.286
  219.7 3.6 collective-permute-done.69.refs_2_
  229.1 4.7 shard_map.290
  242.5 3.8 collective-permute-done.73.refs_2_
  253.1 2.8 collective-permute-done.76.refs_1_
  256.0 4.5 collective-permute-done.77.refs_2_
  263.6 2.6 shard_map.293
  271.6 2.5 collective-permute-done.80.refs_1_
  274.1 3.2 collective-permute-done.81.refs_2_
  293.4 2.9 collective-permute-done.83.refs_1_
  301.0 3.8 collective-permute-done.84.refs_2_
  305.2 4.5 collective-permute-start.94
  313.7 4.6 shard_map.297
  326.4 3.9 collective-permute-done.92.refs_2_
  334.7 3.7 collective-permute-done.58.refs_1_
  338.5 4.7 collective-permute-done.59.refs_2_
  344.1 2.6 add_convert_fusion
  359.4 3.7 collective-permute-start.120
  376.8 2.8 collective-permute-start.114
  382.9 11.3 %reduce-scatter.11.cloned.1.call-done = bf16[128,1024]{1,0:T(8,128)(2,1)} async-done(((bf16[512,1024]{1,0:T(8,128)(2,1)}), bf16[128,1024]{1,0:T(8,128)(2,1)}) %reduce-scatter.11.cloned.1.call-update) | async-done | bytes 262160 | tf_op jit(solution)/shard_map/reduce_scatter | solution.py:516
  401.8 3.4 collective-permute-start.115
  405.1 3.4 collective-permute-start.116
  408.5 2.5 collective-permute-start.106
  411.0 3.4 collective-permute-start.107
  414.4 3.4 collective-permute-start.108
  420.1 5.2 %collective-permute-done.115.refs_2_ = bf16[256,1024]{1,0:T(8,128)(2,1)S(1)} collective-permute-done((bf16[256,1024]{1,0:T(8,128)(2,1)S(1)}, bf16[256,1024]{1,0:T(8,128)(2,1)S(1)}, u32[]{:S(2)}, u32[]{:S(2)}) %collective-permute-start.115) | collective-permute-done | bytes 524320 | tf_op jit(solution)/shard_map/ppermute | solution.py:479
  427.5 3.4 collective-permute-start.98
  430.9 10.1 %collective-permute-done.107.refs_2_ = bf16[256,1024]{1,0:T(8,128)(2,1)S(1)} collective-permute-done((bf16[256,1024]{1,0:T(8,128)(2,1)S(1)}, bf16[256,1024]{1,0:T(8,128)(2,1)S(1)}, u32[]{:S(2)}, u32[]{:S(2)}) %collective-permute-start.107) | collective-permute-done | bytes 524320 | tf_op jit(solution)/shard_map/ppermute | solution.py:479
  440.9 3.4 collective-permute-start.99
  444.3 3.7 collective-permute-start.100
  449.4 3.8 shard_map.302
  453.2 3.7 shard_map.301
  457.6 5.0 %shard_map.300 = (f32[256,3072]{1,0:T(8,128)}, f32[256,1024]{1,0:T(8,128)}) custom-call(s32[3]{0:T(128)S(1)} %pad_add_fusion.1.where, bf16[256,1024]{1,0:T(8,128)(2,1)S(1)} %constant_dynamic-update-slice_fusion.2.refs_0_, bf16[256,1024]{1,0:T(8,128)(2,1)S(1)} %collective-permute-done.98.refs_1_, bf16[256,1024]{1,0:T(8,128)(2,1)S(1)} %collective-permute-done.99.refs_2_, ...), custom_call_target="tpu_custom_call" | custom-call | bytes 8519680 | tf_op jit(solution)/shard_map/pallas_call | solution.py:38
  (628 shorter events, 227.6 us)
Async XLA Ops:
  7.2 253.3 %reduce-scatter.7.cloned.1.call-start = ((), (), s32[]{:S(2)}) async-start(), calls=%async_computation.6 | async-start | bytes 1310720 | tf_op jit(solution)/shard_map/reduce_scatter | solution.py:516
  12.5 33.7 %collective-permute-start = (bf16[12,256]{1,0:T(8,128)(2,1)S(1)}, bf16[12,256]{1,0:T(8,128)(2,1)S(1)}, u32[]{:S(2)}, u32[]{:S(2)}) collective-permute-start(bf16[12,256]{1,0:T(8,128)(2,1)S(1)} %concatenate.42), channel_id=1, source_target_pairs={{0,12},{4,8},{8,4},{12,0},{1,13},{5,9},{9,5},{13,1},{2,14},{6,10},... | collective-permute-start | bytes 18440 | tf_op jit(solution)/shard_map/ppermute | solution.py:476
  17.2 29.0 %collective-permute-start.1 = (bf16[12,256]{1,0:T(8,128)(2,1)S(1)}, bf16[12,256]{1,0:T(8,128)(2,1)S(1)}, u32[]{:S(2)}, u32[]{:S(2)}) collective-permute-start(bf16[12,256]{1,0:T(8,128)(2,1)S(1)} %concatenate.42), channel_id=1, source_target_pairs={{0,8},{4,12},{8,0},{12,4},{1,9},{5,13},{9,1},{13,5},{2,10},{6,14},... | collective-permute-start | bytes 18440 | tf_op jit(solution)/shard_map/ppermute | solution.py:476
  17.2 29.0 %collective-permute-start.2 = (bf16[12,256]{1,0:T(8,128)(2,1)S(1)}, bf16[12,256]{1,0:T(8,128)(2,1)S(1)}, u32[]{:S(2)}, u32[]{:S(2)}) collective-permute-start(bf16[12,256]{1,0:T(8,128)(2,1)S(1)} %concatenate.42), channel_id=1, source_target_pairs={{0,4},{4,0},{8,12},{12,8},{1,5},{5,1},{9,13},{13,9},{2,6},{6,2},{1... | collective-permute-start | bytes 18440 | tf_op jit(solution)/shard_map/ppermute | solution.py:476
  44.0 18.8 %collective-permute-start.25 = (bf16[256,1024]{1,0:T(8,128)(2,1)S(1)}, bf16[256,1024]{1,0:T(8,128)(2,1)S(1)}, u32[]{:S(2)}, u32[]{:S(2)}) collective-permute-start(bf16[256,1024]{1,0:T(8,128)(2,1)S(1)} %get-tuple-element.197.refs_0_), channel_id=1, source_target_pairs={{0,4},{4,8},{8,12},{12,0},{1,5},{5,9},{9,13},{13,1},{2,6},{6,10},{... | collective-permute-start | bytes 1572872 | tf_op jit(solution)/shard_map/ppermute | solution.py:492
  44.5 18.3 %collective-permute-start.10 = (bf16[128,1024]{1,0:T(8,128)(2,1)}, bf16[128,1024]{1,0:T(8,128)(2,1)S(1)}, u32[]{:S(2)}, u32[]{:S(2)}) collective-permute-start(bf16[128,1024]{1,0:T(8,128)(2,1)} %collective-permute-done.9.refs_2_), channel_id=1, source_target_pairs={{0,4},{4,8},{8,12},{12,0},{1,5},{5,9},{9,13},{13,1},{2,6},{6,10},{... | collective-permute-start | bytes 786440 | tf_op jit(solution)/shard_map/ppermute | solution.py:492
  46.4 16.8 %collective-permute-start.11 = (bf16[128,1024]{1,0:T(8,128)(2,1)S(1)}, bf16[128,1024]{1,0:T(8,128)(2,1)S(1)}, u32[]{:S(2)}, u32[]{:S(2)}) collective-permute-start(bf16[128,1024]{1,0:T(8,128)(2,1)S(1)} %get-tuple-element.185.refs_0_), channel_id=1, source_target_pairs={{0,16},{16,0},{1,17},{17,1},{2,18},{18,2},{3,19},{19,3},{4,20},{20... | collective-permute-start | bytes 786440 | tf_op jit(solution)/shard_map/ppermute | solution.py:467
  47.0 17.6 %collective-permute-start.12 = (bf16[128,1024]{1,0:T(8,128)(2,1)S(1)}, bf16[128,1024]{1,0:T(8,128)(2,1)S(1)}, u32[]{:S(2)}, u32[]{:S(2)}) collective-permute-start(bf16[128,1024]{1,0:T(8,128)(2,1)S(1)} %collective-permute-done.8.refs_1_), channel_id=1, source_target_pairs={{0,16},{16,0},{1,17},{17,1},{2,18},{18,2},{3,19},{19,3},{4,20},{20... | collective-permute-start | bytes 786440 | tf_op jit(solution)/shard_map/ppermute | solution.py:467
  47.6 19.3 %collective-permute-start.13 = (bf16[128,1024]{1,0:T(8,128)(2,1)}, bf16[128,1024]{1,0:T(8,128)(2,1)S(1)}, u32[]{:S(2)}, u32[]{:S(2)}) collective-permute-start(bf16[128,1024]{1,0:T(8,128)(2,1)} %collective-permute-done.9.refs_2_), channel_id=1, source_target_pairs={{0,16},{16,0},{1,17},{17,1},{2,18},{18,2},{3,19},{19,3},{4,20},{20... | collective-permute-start | bytes 786440 | tf_op jit(solution)/shard_map/ppermute | solution.py:467
  62.8 16.2 %collective-permute-start.26 = (bf16[256,1024]{1,0:T(8,128)(2,1)S(1)}, bf16[256,1024]{1,0:T(8,128)(2,1)}, u32[]{:S(2)}, u32[]{:S(2)}) collective-permute-start(bf16[256,1024]{1,0:T(8,128)(2,1)S(1)} %collective-permute-done.25.refs_1_), channel_id=1, source_target_pairs={{0,4},{4,8},{8,12},{12,0},{1,5},{5,9},{9,13},{13,1},{2,6},{6,10},{... | collective-permute-start | bytes 1572872 | tf_op jit(solution)/shard_map/ppermute | solution.py:492
  64.0 22.0 %collective-permute-start.4 = (bf16[96,1024]{1,0:T(8,128)(2,1)S(1)}, bf16[96,1024]{1,0:T(8,128)(2,1)}, u32[]{:S(2)}, u32[]{:S(2)}) collective-permute-start(bf16[96,1024]{1,0:T(8,128)(2,1)S(1)} %shard_map.271.refs_0_), channel_id=1, source_target_pairs={{0,1},{1,0},{2,3},{3,2},{4,5},{5,4},{6,7},{7,6},{8,9},{9,8},{10,11... | collective-permute-start | bytes 589832 | tf_op jit(solution)/shard_map/ppermute | solution.py:476
  65.3 20.7 %collective-permute-start.5 = (bf16[96,1024]{1,0:T(8,128)(2,1)S(1)}, bf16[96,1024]{1,0:T(8,128)(2,1)}, u32[]{:S(2)}, u32[]{:S(2)}) collective-permute-start(bf16[96,1024]{1,0:T(8,128)(2,1)S(1)} %shard_map.271.refs_0_), channel_id=1, source_target_pairs={{0,2},{1,3},{2,0},{3,1},{4,6},{5,7},{6,4},{7,5},{8,10},{9,11},{10,... | collective-permute-start | bytes 589832 | tf_op jit(solution)/shard_map/ppermute | solution.py:476
  67.5 18.5 %collective-permute-start.6 = (bf16[96,1024]{1,0:T(8,128)(2,1)S(1)}, bf16[96,1024]{1,0:T(8,128)(2,1)}, u32[]{:S(2)}, u32[]{:S(2)}) collective-permute-start(bf16[96,1024]{1,0:T(8,128)(2,1)S(1)} %shard_map.271.refs_0_), channel_id=1, source_target_pairs={{0,3},{1,2},{2,1},{3,0},{4,7},{5,6},{6,5},{7,4},{8,11},{9,10},{10,... | collective-permute-start | bytes 589832 | tf_op jit(solution)/shard_map/ppermute | solution.py:476
  69.6 24.4 %collective-permute-start.28 = (bf16[256,1024]{1,0:T(8,128)(2,1)S(1)}, bf16[256,1024]{1,0:T(8,128)(2,1)}, u32[]{:S(2)}, u32[]{:S(2)}) collective-permute-start(bf16[256,1024]{1,0:T(8,128)(2,1)S(1)} %get-tuple-element.197.refs_0_), channel_id=1, source_target_pairs={{0,16},{16,0},{1,17},{17,1},{2,18},{18,2},{3,19},{19,3},{4,20},{20... | collective-permute-start | bytes 1572872 | tf_op jit(solution)/shard_map/ppermute | solution.py:467
  79.0 24.6 %collective-permute-start.27 = (bf16[256,1024]{1,0:T(8,128)(2,1)}, bf16[256,1024]{1,0:T(8,128)(2,1)S(1)}, u32[]{:S(2)}, u32[]{:S(2)}) collective-permute-start(bf16[256,1024]{1,0:T(8,128)(2,1)} %collective-permute-done.26.refs_2_), channel_id=1, source_target_pairs={{0,4},{4,8},{8,12},{12,0},{1,5},{5,9},{9,13},{13,1},{2,6},{6,10},{... | collective-permute-start | bytes 1572872 | tf_op jit(solution)/shard_map/ppermute | solution.py:492
  93.9 17.4 %collective-permute-start.51 = (bf16[256,1024]{1,0:T(8,128)(2,1)S(1)}, bf16[256,1024]{1,0:T(8,128)(2,1)S(1)}, u32[]{:S(2)}, u32[]{:S(2)}) collective-permute-start(bf16[256,1024]{1,0:T(8,128)(2,1)S(1)} %get-tuple-element.215.refs_0_), channel_id=1, source_target_pairs={{0,4},{4,8},{8,12},{12,0},{1,5},{5,9},{9,13},{13,1},{2,6},{6,10},{... | collective-permute-start | bytes 1572872 | tf_op jit(solution)/shard_map/ppermute | solution.py:492
  101.5 18.2 %collective-permute-start.29 = (bf16[256,1024]{1,0:T(8,128)(2,1)S(1)}, bf16[256,1024]{1,0:T(8,128)(2,1)S(1)}, u32[]{:S(2)}, u32[]{:S(2)}) collective-permute-start(bf16[256,1024]{1,0:T(8,128)(2,1)S(1)} %collective-permute-done.25.refs_1_), channel_id=1, source_target_pairs={{0,16},{16,0},{1,17},{17,1},{2,18},{18,2},{3,19},{19,3},{4,20},{20... | collective-permute-start | bytes 1572872 | tf_op jit(solution)/shard_map/ppermute | solution.py:467
  101.5 19.6 %collective-permute-start.30 = (bf16[256,1024]{1,0:T(8,128)(2,1)}, bf16[256,1024]{1,0:T(8,128)(2,1)S(1)}, u32[]{:S(2)}, u32[]{:S(2)}) collective-permute-start(bf16[256,1024]{1,0:T(8,128)(2,1)} %collective-permute-done.26.refs_2_), channel_id=1, source_target_pairs={{0,16},{16,0},{1,17},{17,1},{2,18},{18,2},{3,19},{19,3},{4,20},{20... | collective-permute-start | bytes 1572872 | tf_op jit(solution)/shard_map/ppermute | solution.py:467
  103.6 17.6 %collective-permute-start.31 = (bf16[256,1024]{1,0:T(8,128)(2,1)S(1)}, bf16[256,1024]{1,0:T(8,128)(2,1)S(1)}, u32[]{:S(2)}, u32[]{:S(2)}) collective-permute-start(bf16[256,1024]{1,0:T(8,128)(2,1)S(1)} %collective-permute-done.27.refs_3_), channel_id=1, source_target_pairs={{0,16},{16,0},{1,17},{17,1},{2,18},{18,2},{3,19},{19,3},{4,20},{20... | collective-permute-start | bytes 1572872 | tf_op jit(solution)/shard_map/ppermute | solution.py:467
  121.1 19.0 %collective-permute-start.52 = (bf16[256,1024]{1,0:T(8,128)(2,1)S(1)}, bf16[256,1024]{1,0:T(8,128)(2,1)S(1)}, u32[]{:S(2)}, u32[]{:S(2)}) collective-permute-start(bf16[256,1024]{1,0:T(8,128)(2,1)S(1)} %collective-permute-done.51.refs_1_), channel_id=1, source_target_pairs={{0,4},{4,8},{8,12},{12,0},{1,5},{5,9},{9,13},{13,1},{2,6},{6,10},{... | collective-permute-start | bytes 1572872 | tf_op jit(solution)/shard_map/ppermute | solution.py:492
  121.2 18.9 %collective-permute-start.40 = (bf16[128,1024]{1,0:T(8,128)(2,1)S(1)}, bf16[128,1024]{1,0:T(8,128)(2,1)S(1)}, u32[]{:S(2)}, u32[]{:S(2)}) collective-permute-start(bf16[128,1024]{1,0:T(8,128)(2,1)S(1)} %collective-permute-done.39.refs_2_), channel_id=1, source_target_pairs={{0,4},{4,8},{8,12},{12,0},{1,5},{5,9},{9,13},{13,1},{2,6},{6,10},{... | collective-permute-start | bytes 786440 | tf_op jit(solution)/shard_map/ppermute | solution.py:492
  148.4 18.4 %collective-permute-start.53 = (bf16[256,1024]{1,0:T(8,128)(2,1)S(1)}, bf16[256,1024]{1,0:T(8,128)(2,1)S(1)}, u32[]{:S(2)}, u32[]{:S(2)}) collective-permute-start(bf16[256,1024]{1,0:T(8,128)(2,1)S(1)} %collective-permute-done.52.refs_2_), channel_id=1, source_target_pairs={{0,4},{4,8},{8,12},{12,0},{1,5},{5,9},{9,13},{13,1},{2,6},{6,10},{... | collective-permute-start | bytes 1572872 | tf_op jit(solution)/shard_map/ppermute | solution.py:492
  164.8 16.6 %collective-permute-start.55 = (bf16[256,1024]{1,0:T(8,128)(2,1)S(1)}, bf16[256,1024]{1,0:T(8,128)(2,1)S(1)}, u32[]{:S(2)}, u32[]{:S(2)}) collective-permute-start(bf16[256,1024]{1,0:T(8,128)(2,1)S(1)} %collective-permute-done.51.refs_1_), channel_id=1, source_target_pairs={{0,16},{16,0},{1,17},{17,1},{2,18},{18,2},{3,19},{19,3},{4,20},{20... | collective-permute-start | bytes 1572872 | tf_op jit(solution)/shard_map/ppermute | solution.py:467
  166.8 16.8 %collective-permute-start.56 = (bf16[256,1024]{1,0:T(8,128)(2,1)S(1)}, bf16[256,1024]{1,0:T(8,128)(2,1)S(1)}, u32[]{:S(2)}, u32[]{:S(2)}) collective-permute-start(bf16[256,1024]{1,0:T(8,128)(2,1)S(1)} %collective-permute-done.52.refs_2_), channel_id=1, source_target_pairs={{0,16},{16,0},{1,17},{17,1},{2,18},{18,2},{3,19},{19,3},{4,20},{20... | collective-permute-start | bytes 1572872 | tf_op jit(solution)/shard_map/ppermute | solution.py:467
  223.3 81.6 %reduce-scatter.9.cloned.1.call-start = ((), (), s32[]{:S(2)}) async-start(), calls=%async_computation.7 | async-start | bytes 1310720 | tf_op jit(solution)/shard_map/reduce_scatter | solution.py:516
  223.6 17.6 %collective-permute-start.75 = (bf16[512,1024]{1,0:T(8,128)(2,1)}, bf16[512,1024]{1,0:T(8,128)(2,1)S(1)}, u32[]{:S(2)}, u32[]{:S(2)}) collective-permute-start(bf16[512,1024]{1,0:T(8,128)(2,1)} %copy-done.84), channel_id=1, source_target_pairs={{0,16},{16,0},{1,17},{17,1},{2,18},{18,2},{3,19},{19,3},{4,20},{20... | collective-permute-start | bytes 3145736 | tf_op jit(solution)/shard_map/ppermute | solution.py:467
  246.4 110.6 %reduce-scatter.13.cloned.1.call-start = ((), (), s32[]{:S(2)}) async-start(), calls=%async_computation.9 | async-start | bytes 1310720 | tf_op jit(solution)/shard_map/reduce_scatter | solution.py:516
  260.6 110.7 %reduce-scatter.17.cloned.1.call-start = ((), (), s32[]{:S(2)}) async-start(), calls=%async_computation.11 | async-start | bytes 1310720 | tf_op jit(solution)/shard_map/reduce_scatter | solution.py:516
  277.4 20.6 %collective-permute-start.90 = (bf16[512,1024]{1,0:T(8,128)(2,1)S(1)}, bf16[512,1024]{1,0:T(8,128)(2,1)S(1)}, u32[]{:S(2)}, u32[]{:S(2)}) collective-permute-start(bf16[512,1024]{1,0:T(8,128)(2,1)S(1)} %get-tuple-element.292), channel_id=1, source_target_pairs={{0,16},{16,0},{1,17},{17,1},{2,18},{18,2},{3,19},{19,3},{4,20},{20... | collective-permute-start | bytes 3145736 | tf_op jit(solution)/shard_map/ppermute | solution.py:467
  281.0 23.8 %collective-permute-start.87 = (bf16[256,1024]{1,0:T(8,128)(2,1)S(1)}, bf16[256,1024]{1,0:T(8,128)(2,1)}, u32[]{:S(2)}, u32[]{:S(2)}) collective-permute-start(bf16[256,1024]{1,0:T(8,128)(2,1)S(1)} %constant_dynamic-update-slice_fusion.refs_4_), channel_id=1, source_target_pairs={{16,17},{17,16},{18,19},{19,18},{20,21},{21,20},{22,23},{23,22},{2... | collective-permute-start | bytes 1572872 | tf_op jit(solution)/shard_map/ppermute | solution.py:479
  282.5 22.4 %collective-permute-start.88 = (bf16[256,1024]{1,0:T(8,128)(2,1)S(1)}, bf16[256,1024]{1,0:T(8,128)(2,1)}, u32[]{:S(2)}, u32[]{:S(2)}) collective-permute-start(bf16[256,1024]{1,0:T(8,128)(2,1)S(1)} %constant_dynamic-update-slice_fusion.refs_4_), channel_id=1, source_target_pairs={{16,18},{17,19},{18,16},{19,17},{20,22},{21,23},{22,20},{23,21},{2... | collective-permute-start | bytes 1572872 | tf_op jit(solution)/shard_map/ppermute | solution.py:479
  283.9 20.9 %collective-permute-start.89 = (bf16[256,1024]{1,0:T(8,128)(2,1)S(1)}, bf16[256,1024]{1,0:T(8,128)(2,1)}, u32[]{:S(2)}, u32[]{:S(2)}) collective-permute-start(bf16[256,1024]{1,0:T(8,128)(2,1)S(1)} %constant_dynamic-update-slice_fusion.refs_4_), channel_id=1, source_target_pairs={{16,19},{17,18},{18,17},{19,16},{20,23},{21,22},{22,21},{23,20},{2... | collective-permute-start | bytes 1572872 | tf_op jit(solution)/shard_map/ppermute | solution.py:479
  304.9 76.7 %reduce-scatter.15.cloned.1.call-start = ((), (), s32[]{:S(2)}) async-start(), calls=%async_computation.10 | async-start | bytes 1310720 | tf_op jit(solution)/shard_map/reduce_scatter | solution.py:516
  305.2 19.5 %collective-permute-start.94 = (bf16[512,1024]{1,0:T(8,128)(2,1)}, bf16[512,1024]{1,0:T(8,128)(2,1)S(1)}, u32[]{:S(2)}, u32[]{:S(2)}) collective-permute-start(bf16[512,1024]{1,0:T(8,128)(2,1)} %copy-done.83), channel_id=1, source_target_pairs={{0,16},{16,0},{1,17},{17,1},{2,18},{18,2},{3,19},{19,3},{4,20},{20... | collective-permute-start | bytes 3145736 | tf_op jit(solution)/shard_map/ppermute | solution.py:467
  330.3 64.0 %reduce-scatter.11.cloned.1.call-start = ((), (), s32[]{:S(2)}) async-start(), calls=%async_computation.8 | async-start | bytes 1310720 | tf_op jit(solution)/shard_map/reduce_scatter | solution.py:516
  375.3 33.2 %collective-permute-start.102 = (bf16[256,1024]{1,0:T(8,128)(2,1)S(1)}, bf16[256,1024]{1,0:T(8,128)(2,1)}, u32[]{:S(2)}, u32[]{:S(2)}) collective-permute-start(bf16[256,1024]{1,0:T(8,128)(2,1)S(1)} %constant_dynamic-update-slice_fusion.4.refs_4_), channel_id=1, source_target_pairs={{16,17},{17,16},{18,19},{19,18},{20,21},{21,20},{22,23},{23,22},{2... | collective-permute-start | bytes 1572872 | tf_op jit(solution)/shard_map/ppermute | solution.py:479
  376.8 34.2 %collective-permute-start.114 = (bf16[256,1024]{1,0:T(8,128)(2,1)S(1)}, bf16[256,1024]{1,0:T(8,128)(2,1)}, u32[]{:S(2)}, u32[]{:S(2)}) collective-permute-start(bf16[256,1024]{1,0:T(8,128)(2,1)S(1)} %constant_dynamic-update-slice_fusion.10.refs_0_), channel_id=1, source_target_pairs={{0,1},{1,0},{2,3},{3,2},{4,5},{5,4},{6,7},{7,6},{8,9},{9,8},{10,11... | collective-permute-start | bytes 1572872 | tf_op jit(solution)/shard_map/ppermute | solution.py:479
  381.6 16.1 %collective-permute-start.105 = (bf16[128,1024]{1,0:T(8,128)(2,1)}, bf16[128,1024]{1,0:T(8,128)(2,1)}, u32[]{:S(2)}, u32[]{:S(2)}) collective-permute-start(bf16[128,1024]{1,0:T(8,128)(2,1)} %reduce-scatter.15.cloned.1.call-done), channel_id=1, source_target_pairs={{16,0},{17,1},{18,2},{19,3},{20,4},{21,5},{22,6},{23,7},{24,8},{25... | collective-permute-start | bytes 786440 | tf_op jit(solution)/shard_map/ppermute | solution.py:518
  394.2 20.2 %collective-permute-start.97 = (bf16[128,1024]{1,0:T(8,128)(2,1)}, bf16[128,1024]{1,0:T(8,128)(2,1)S(1)}, u32[]{:S(2)}, u32[]{:S(2)}) collective-permute-start(bf16[128,1024]{1,0:T(8,128)(2,1)} %reduce-scatter.11.cloned.1.call-done), channel_id=1, source_target_pairs={{16,0},{17,1},{18,2},{19,3},{20,4},{21,5},{22,6},{23,7},{24,8},{25... | collective-permute-start | bytes 786440 | tf_op jit(solution)/shard_map/ppermute | solution.py:518
  401.8 23.5 %collective-permute-start.115 = (bf16[256,1024]{1,0:T(8,128)(2,1)S(1)}, bf16[256,1024]{1,0:T(8,128)(2,1)S(1)}, u32[]{:S(2)}, u32[]{:S(2)}) collective-permute-start(bf16[256,1024]{1,0:T(8,128)(2,1)S(1)} %constant_dynamic-update-slice_fusion.10.refs_0_), channel_id=1, source_target_pairs={{0,2},{1,3},{2,0},{3,1},{4,6},{5,7},{6,4},{7,5},{8,10},{9,11},{10,... | collective-permute-start | bytes 1572872 | tf_op jit(solution)/shard_map/ppermute | solution.py:479
  405.1 20.9 %collective-permute-start.116 = (bf16[256,1024]{1,0:T(8,128)(2,1)S(1)}, bf16[256,1024]{1,0:T(8,128)(2,1)S(1)}, u32[]{:S(2)}, u32[]{:S(2)}) collective-permute-start(bf16[256,1024]{1,0:T(8,128)(2,1)S(1)} %constant_dynamic-update-slice_fusion.10.refs_0_), channel_id=1, source_target_pairs={{0,3},{1,2},{2,1},{3,0},{4,7},{5,6},{6,5},{7,4},{8,11},{9,10},{10,... | collective-permute-start | bytes 1572872 | tf_op jit(solution)/shard_map/ppermute | solution.py:479
  408.5 19.0 %collective-permute-start.106 = (bf16[256,1024]{1,0:T(8,128)(2,1)S(1)}, bf16[256,1024]{1,0:T(8,128)(2,1)S(1)}, u32[]{:S(2)}, u32[]{:S(2)}) collective-permute-start(bf16[256,1024]{1,0:T(8,128)(2,1)S(1)} %constant_dynamic-update-slice_fusion.6.refs_0_), channel_id=1, source_target_pairs={{0,1},{1,0},{2,3},{3,2},{4,5},{5,4},{6,7},{7,6},{8,9},{9,8},{10,11... | collective-permute-start | bytes 1572872 | tf_op jit(solution)/shard_map/ppermute | solution.py:479
  411.0 29.9 %collective-permute-start.107 = (bf16[256,1024]{1,0:T(8,128)(2,1)S(1)}, bf16[256,1024]{1,0:T(8,128)(2,1)S(1)}, u32[]{:S(2)}, u32[]{:S(2)}) collective-permute-start(bf16[256,1024]{1,0:T(8,128)(2,1)S(1)} %constant_dynamic-update-slice_fusion.6.refs_0_), channel_id=1, source_target_pairs={{0,2},{1,3},{2,0},{3,1},{4,6},{5,7},{6,4},{7,5},{8,10},{9,11},{10,... | collective-permute-start | bytes 1572872 | tf_op jit(solution)/shard_map/ppermute | solution.py:479
  414.4 29.9 %collective-permute-start.108 = (bf16[256,1024]{1,0:T(8,128)(2,1)S(1)}, bf16[256,1024]{1,0:T(8,128)(2,1)S(1)}, u32[]{:S(2)}, u32[]{:S(2)}) collective-permute-start(bf16[256,1024]{1,0:T(8,128)(2,1)S(1)} %constant_dynamic-update-slice_fusion.6.refs_0_), channel_id=1, source_target_pairs={{0,3},{1,2},{2,1},{3,0},{4,7},{5,6},{6,5},{7,4},{8,11},{9,10},{10,... | collective-permute-start | bytes 1572872 | tf_op jit(solution)/shard_map/ppermute | solution.py:479
  425.3 31.6 %collective-permute-start.103 = (bf16[256,1024]{1,0:T(8,128)(2,1)S(1)}, bf16[256,1024]{1,0:T(8,128)(2,1)S(1)}, u32[]{:S(2)}, u32[]{:S(2)}) collective-permute-start(bf16[256,1024]{1,0:T(8,128)(2,1)S(1)} %constant_dynamic-update-slice_fusion.4.refs_4_), channel_id=1, source_target_pairs={{16,18},{17,19},{18,16},{19,17},{20,22},{21,23},{22,20},{23,21},{2... | collective-permute-start | bytes 1572872 | tf_op jit(solution)/shard_map/ppermute | solution.py:479
  426.0 30.9 %collective-permute-start.104 = (bf16[256,1024]{1,0:T(8,128)(2,1)S(1)}, bf16[256,1024]{1,0:T(8,128)(2,1)S(1)}, u32[]{:S(2)}, u32[]{:S(2)}) collective-permute-start(bf16[256,1024]{1,0:T(8,128)(2,1)S(1)} %constant_dynamic-update-slice_fusion.4.refs_4_), channel_id=1, source_target_pairs={{16,19},{17,18},{18,17},{19,16},{20,23},{21,22},{22,21},{23,20},{2... | collective-permute-start | bytes 1572872 | tf_op jit(solution)/shard_map/ppermute | solution.py:479
  427.5 29.4 %collective-permute-start.98 = (bf16[256,1024]{1,0:T(8,128)(2,1)S(1)}, bf16[256,1024]{1,0:T(8,128)(2,1)S(1)}, u32[]{:S(2)}, u32[]{:S(2)}) collective-permute-start(bf16[256,1024]{1,0:T(8,128)(2,1)S(1)} %constant_dynamic-update-slice_fusion.2.refs_0_), channel_id=1, source_target_pairs={{0,1},{1,0},{2,3},{3,2},{4,5},{5,4},{6,7},{7,6},{8,9},{9,8},{10,11... | collective-permute-start | bytes 1572872 | tf_op jit(solution)/shard_map/ppermute | solution.py:479
  440.9 16.7 %collective-permute-start.99 = (bf16[256,1024]{1,0:T(8,128)(2,1)S(1)}, bf16[256,1024]{1,0:T(8,128)(2,1)S(1)}, u32[]{:S(2)}, u32[]{:S(2)}) collective-permute-start(bf16[256,1024]{1,0:T(8,128)(2,1)S(1)} %constant_dynamic-update-slice_fusion.2.refs_0_), channel_id=1, source_target_pairs={{0,2},{1,3},{2,0},{3,1},{4,6},{5,7},{6,4},{7,5},{8,10},{9,11},{10,... | collective-permute-start | bytes 1572872 | tf_op jit(solution)/shard_map/ppermute | solution.py:479
  (218 other events, 1999.5 us)
Sparse Core Ops, SparseCore 0:
  223.4 27.4 reduce-scatter.6
  253.3 25.7 reduce-scatter.8
  282.0 25.7 reduce-scatter.12
  310.1 26.2 reduce-scatter.16
  339.1 25.9 reduce-scatter.14
  367.9 26.2 reduce-scatter.10

commit v3 on v2

--- a/solution.py
+++ b/solution.py
@@ -8,9 +8,7 @@
 from jax.sharding import PartitionSpec as P
 
 HEADS = 16
-TIE_DOWN = 3
-TIE_UP = 4
-COPY_DOWN = 5
+TIE_MLP = 4
 NORM_EPS = 1e-05
 GELU_COEF = 0.7978845608028654
 GELU_CUBE = 0.044715
@@ -372,19 +370,26 @@
     return kernel
 
 
-def split_by_core(core, product, kept, sent, shards):
+def split_by_core(core, product, kept, sent, shards, offset=0):
     half = product.shape[0] // (2 * shards)
+    stride = kept.shape[0] // shards
     first = core == 0
     for b in range(shards):
         one = product[2 * b * half : (2 * b + 1) * half]
         two = product[(2 * b + 1) * half : (2 * b + 2) * half]
-        kept[b * half : (b + 1) * half, : one.shape[1]] = jnp.where(first, one, two)
-        sent[b * half : (b + 1) * half, : one.shape[1]] = jnp.where(first, two, one)
-
-
-def make_weight_gradient(shards):
-    def kernel(where, left, right, kept, sent):
-        split_by_core(where[0], t_dot(left[...], right[...]).astype(LOW), kept, sent, shards)
+        at = slice(b * stride + offset, b * stride + offset + half)
+        kept[at, : one.shape[1]] = jnp.where(first, one, two)
+        sent[at, : one.shape[1]] = jnp.where(first, two, one)
+
+
+def make_mlp_gradient(shards):
+    def kernel(where, active, down, second, before, kept, sent):
+        core = where[0]
+        half = kept.shape[0] // shards // 2
+        product = t_dot(active[...], down[...]).astype(LOW)
+        split_by_core(core, product, kept, sent, shards, 0)
+        product = t_dot(second[...], before[...]).astype(LOW)
+        split_by_core(core, product, kept, sent, shards, half)
 
     return kernel
 
@@ -437,28 +442,22 @@
     return kernel
 
 
-def make_place_up(parts):
+def make_place_mlp(parts):
     def kernel(where, *refs):
         core, rep = where[0], where[1]
-        out = refs[2 * parts]
-        run = out.shape[0]
+        up, down = refs[2 * parts :]
+        run = up.shape[0]
+        half = run // 2
         for k in range(parts):
             piece = chosen(core, refs, k, parts).astype(F32)
-            for m in range(piece.shape[1] // run):
-                out[:, at_block(m * parts + jnp.bitwise_xor(rep, k), run)] = piece[
-                    :, m * run : (m + 1) * run
-                ]
-
-    return kernel
-
-
-def make_place_down(parts):
-    def kernel(where, *refs):
-        core, rep = where[0], where[1]
-        out = refs[2 * parts]
-        for k in range(parts):
-            piece = chosen(core, refs, k, parts).astype(F32)
-            out[at_block(jnp.bitwise_xor(rep, k), piece.shape[0]), :] = piece
+            peer = jnp.bitwise_xor(rep, k)
+            for c in range(2):
+                start = 2 * c * half
+                down[at_block(2 * peer + c, half), :] = piece[start : start + half]
+                for m in range(piece.shape[1] // run):
+                    up[c * half : (c + 1) * half, at_block(m * parts + peer, run)] = piece[
+                        start + half : start + 2 * half, m * run : (m + 1) * run
+                    ]
 
     return kernel
 
@@ -495,7 +494,8 @@
 
 
 class GradientSum:
-    def __init__(self, pair, section, tie=None, copy=None):
+    def __init__(self, pair, section, tie=None, copy=None, direct=False):
+        self.direct = direct
         self.section, self.tie, self.copy, self.age = section, tie, copy, 0
         self.state, self.stage = list(pair), 0
 
@@ -512,15 +512,29 @@
         if self.stage == 1:
             kept, arrived = self.state[0], swap(self.state[1])
             self.state = (kept.astype(F32) + arrived.astype(F32)).astype(LOW)
+        elif self.stage == 2 and self.direct:
+            count, shard = lax.axis_size("shard"), lax.axis_index("shard")
+            size = self.state.shape[0] // count
+            pieces = from_peers(
+                [
+                    lax.dynamic_slice_in_dim(self.state, (shard ^ k) * size, size, 0)
+                    for k in range(count)
+                ],
+                "shard",
+            )
+            pieces = [p.astype(F32) for p in pieces]
+            self.state = sum(pieces[1:], pieces[0]).astype(LOW)
         elif self.stage == 2:
             self.state = lax.psum_scatter(self.state, "shard", scatter_dimension=0, tiled=True)
         elif self.stage == 3:
             theirs = lax.ppermute(self.state, "section", [(1 - s, s)])
             order = [self.state, theirs] if s == 0 else [theirs, self.state]
-            self.state = gathered_blocks(jnp.concatenate(order, axis=0), "rep", s)
+            self.state = jnp.concatenate(order, axis=0)
+        elif self.stage == 4:
+            self.state = gathered_blocks(self.state, "rep", s)
 
     def finish(self):
-        while self.stage < 3:
+        while self.stage < 4:
             self.next_stage()
         return self.state
 
@@ -821,11 +835,7 @@
         if fast:
             piece = sds((features // 2, features))
             flops = 2 * all_rows * features * features
-            down_pair = call(
-                make_weight_gradient(shards), [piece, piece], [active, down_all], flops, where
-            )
-            grad_down = GradientSum(down_pair, s, TIE_DOWN, COPY_DOWN)
-            terms = window(terms, tasks, [grad_down])
+            terms = window(terms, tasks)
         else:
             grad_down = over_slots(active, down_all)
             grad_up = over_slots(second_all, before_all)
@@ -836,14 +846,15 @@
         )
         merge_blocks = gathered_blocks(g_merge, "rep")
         if fast:
-            up_pair = call(
-                make_weight_gradient(shards),
-                [piece, piece],
-                [second_all, before_all],
-                flops,
+            wide = sds((features, features))
+            mlp_pair = call(
+                make_mlp_gradient(shards),
+                [wide, wide],
+                [active, down_all, second_all, before_all],
+                2 * flops,
                 after(where, g_merge),
             )
-            grad_up = GradientSum(up_pair, s, TIE_UP)
+            grad_up, grad_down = GradientSum(mlp_pair, s, TIE_MLP, TIE_MLP + 1), None
             merge_blocks = window(merge_blocks, tasks, [grad_up])
         results = call(
             make_attention_backward(reps, head_size),
@@ -867,7 +878,7 @@
                 flops,
                 where,
             )
-            grad_heads, grad_merge = GradientSum(both_pair, s), None
+            grad_heads, grad_merge = GradientSum(both_pair, s, direct=s == 0), None
             terms = window(terms, tasks, [grad_heads])
         elif strided:
             grad_heads = over_slots(normed_all, joint_all)
@@ -887,6 +898,8 @@
             [g_middle, hidden] + terms + [vector(s, 0)],
         )
         hidden_grads[s] = grad_out
+        if fast and s == 0:
+            first_gain_sum, first_shift_sum = window([first_gain_sum, first_shift_sum], tasks)
 
         def placed_heads(part):
             if strided:
@@ -952,15 +965,22 @@
         def both_sections(number):
             return [p for s in range(sections) for p in weight_grads[s][number].finish()]
 
-        grad_up = call(
-            make_place_up(reps), [sds((depth, ff), F32)], both_sections(2), scalars=where
-        )[0][None]
-        grad_down = call(
-            make_place_down(reps),
-            [sds((ff // shards, features), F32)],
-            both_sections(3),
+        for s in reversed(range(sections)):
+            for number in (2, 0):
+                task = weight_grads[s][number]
+                while task.stage < 2:
+                    task.next_stage()
+                if s + 1 < sections:
+                    task.state = after(task.state, earlier)
+                task.finish()
+            earlier = [weight_grads[s][number].state for number in (2, 0)]
+        grad_up, grad_down = call(
+            make_place_mlp(reps),
+            [sds((depth, ff), F32), sds((ff // shards, features), F32)],
+            both_sections(2),
             scalars=where,
-        )[0][None]
+        )
+        grad_up, grad_down = grad_up[None], grad_down[None]
         lane = jnp.arange(head_run, dtype=jnp.int32)[:, None]
         column = jnp.arange(reps * head_run, dtype=jnp.int32)[None, :]
         places = jnp.stack(

time: 479 us -> 478 us (level)
  other arithmetic: 20.1 us -> 25.4 us
  starting transfers between devices: 140 us -> 135 us
    ppermute x60 -> x63, waiting for transfers between devices: 90.3 us -> 115 us  [from_peers(): received.append(lax.ppermute(blocks[k], axis, pairs))]
    ppermute x18 -> x12, starting transfers between devices: 40 us -> 27.3 us  [from_peers(): received.append(lax.ppermute(blocks[k], ('section', axis), pairs))]
    reduce_scatter x6 -> x3, waiting for transfers between devices: 11.4 us -> 0.88 us  [next_stage(): lax.psum_scatter(self.state, 'shard', scatter_dimension=0, tiled=True)]
    ppermute x60 -> x63, starting transfers between devices: 75.8 us -> 85.6 us  [from_peers(): received.append(lax.ppermute(blocks[k], axis, pairs))]
    ppermute x18 -> x12, waiting for transfers between devices: 16.8 us -> 9.02 us  [from_peers(): received.append(lax.ppermute(blocks[k], ('section', axis), pairs))]
    unnamed x280 -> x243, local copies, waits for them, and re-layouts: 51.6 us -> 44.5 us
    pallas_call x32 -> x29, Pallas kernels: 60.3 us -> 55.7 us  [call(): pl.pallas_call(kernel, out_shape=outs, in_specs=[pl.BlockSpec(memory_spac...]
    ppermute x6 -> x4, starting transfers between devices: 11.1 us -> 7.14 us  [next_stage(): theirs = lax.ppermute(self.state, 'section', [(1 - s, s)])]
  transfers between devices with their start and end apart: 130 -> 120, of which waited for: 49 -> 45; matrix products, arithmetic and copies ran while one was open for 6% -> 9% of each run, Pallas kernels for 11% -> 10%
where the time goes in v3:
time: 478 us; the launch traced here: 468 us
  waiting for transfers between devices  177 us (37%)
  starting transfers between devices  135 us (28%)
  local copies, waits for them, and re-layouts  59.6 us (12%)
  Pallas kernels  55.7 us (12%)
  other arithmetic  25.4 us (5%)
  between operations  15.9 us (3%)
    ppermute x63, waiting for transfers between devices, from_peers(): received.append(lax.ppermute(blocks[k], axis, pairs))  115 us
    ppermute x63, starting transfers between devices, from_peers(): received.append(lax.ppermute(blocks[k], axis, pairs))  85.6 us
    pallas_call x29, Pallas kernels, call(): pl.pallas_call(kernel, out_shape=outs, in_specs=[pl.BlockSpec(memory_spac...  55.7 us
    ppermute x12, waiting for transfers between devices, ring_gather(): lax.ppermute(blocks[-1], 'shard', [(i, (i + 1) % count) for i in range(co...  51.8 us
    unnamed x243, local copies, waits for them, and re-layouts  44.5 us
    ppermute x12, starting transfers between devices, from_peers(): received.append(lax.ppermute(blocks[k], ('section', axis), pairs))  27.3 us
    ppermute x26, starting transfers between devices, swap(): return lax.ppermute(block, 'section', [(0, 1), (1, 0)])  11.9 us
    convert_element_type x4, other arithmetic, next_stage(): self.state = (kept.astype(F32) + arrived.astype(F32)).astype(LOW)  10.2 us
  transfers between devices with their start and end apart: 120, of which 45 were waited for; matrix products, arithmetic and copies ran while one was open for 9% of the time, Pallas kernels for 10%

profile of v3, /device:TPU:0, one launch (start us, length us, event | category | flops | bytes accessed | tf_op | source)
XLA Modules:
  0.0 468.3 jit_solution(16216556892649813721)
XLA Ops:
  12.5 4.7 collective-permute-start
  23.8 8.8 %collective-permute-done.8.refs_1_ = bf16[128,1024]{1,0:T(8,128)(2,1)} collective-permute-done((bf16[128,1024]{1,0:T(8,128)(2,1)S(1)}, bf16[128,1024]{1,0:T(8,128)(2,1)}, u32[]{:S(2)}, u32[]{:S(2)}) %collective-permute-start.8) | collective-permute-done | bytes 262176 | tf_op jit(solution)/shard_map/ppermute | solution.py:491
  32.5 2.4 collective-permute-start.17
  46.8 15.3 %collective-permute-done.10.refs_3_ = bf16[128,1024]{1,0:T(8,128)(2,1)S(1)} collective-permute-done((bf16[128,1024]{1,0:T(8,128)(2,1)}, bf16[128,1024]{1,0:T(8,128)(2,1)S(1)}, u32[]{:S(2)}, u32[]{:S(2)}) %collective-permute-start.10) | collective-permute-done | bytes 262176 | tf_op jit(solution)/shard_map/ppermute | solution.py:491
  71.1 7.2 %collective-permute-done.26.refs_2_ = bf16[256,1024]{1,0:T(8,128)(2,1)} collective-permute-done((bf16[256,1024]{1,0:T(8,128)(2,1)S(1)}, bf16[256,1024]{1,0:T(8,128)(2,1)}, u32[]{:S(2)}, u32[]{:S(2)}) %collective-permute-start.26) | collective-permute-done | bytes 524320 | tf_op jit(solution)/shard_map/ppermute | solution.py:491
  86.1 3.4 shard_map.274
  94.6 6.2 %collective-permute-done.38.refs_1_ = bf16[128,1024]{1,0:T(8,128)(2,1)S(1)} collective-permute-done((bf16[128,1024]{1,0:T(8,128)(2,1)S(1)}, bf16[128,1024]{1,0:T(8,128)(2,1)S(1)}, u32[]{:S(2)}, u32[]{:S(2)}) %collective-permute-start.38) | collective-permute-done | bytes 262176 | tf_op jit(solution)/shard_map/ppermute | solution.py:491
  103.7 5.4 %collective-permute-done.20.refs_3_ = bf16[96,1024]{1,0:T(8,128)(2,1)S(1)} collective-permute-done((bf16[96,1024]{1,0:T(8,128)(2,1)S(1)}, bf16[96,1024]{1,0:T(8,128)(2,1)S(1)}, u32[]{:S(2)}, u32[]{:S(2)}) %collective-permute-start.20) | collective-permute-done | bytes 196640 | tf_op jit(solution)/shard_map/ppermute | solution.py:475
  112.1 6.2 %collective-permute-done.39.refs_2_ = bf16[128,1024]{1,0:T(8,128)(2,1)S(1)} collective-permute-done((bf16[128,1024]{1,0:T(8,128)(2,1)S(1)}, bf16[128,1024]{1,0:T(8,128)(2,1)S(1)}, u32[]{:S(2)}, u32[]{:S(2)}) %collective-permute-start.39) | collective-permute-done | bytes 262176 | tf_op jit(solution)/shard_map/ppermute | solution.py:491
  123.6 4.1 collective-permute-done.22.refs_2_
  133.9 6.3 %collective-permute-done.40.refs_3_ = bf16[128,1024]{1,0:T(8,128)(2,1)S(1)} collective-permute-done((bf16[128,1024]{1,0:T(8,128)(2,1)S(1)}, bf16[128,1024]{1,0:T(8,128)(2,1)S(1)}, u32[]{:S(2)}, u32[]{:S(2)}) %collective-permute-start.40) | collective-permute-done | bytes 262176 | tf_op jit(solution)/shard_map/ppermute | solution.py:491
  142.2 6.3 %collective-permute-done.34.refs_3_ = bf16[96,1024]{1,0:T(8,128)(2,1)S(1)} collective-permute-done((bf16[96,1024]{1,0:T(8,128)(2,1)S(1)}, bf16[96,1024]{1,0:T(8,128)(2,1)S(1)}, u32[]{:S(2)}, u32[]{:S(2)}) %collective-permute-start.34) | collective-permute-done | bytes 196640 | tf_op jit(solution)/shard_map/ppermute | solution.py:475
  153.3 3.6 collective-permute-done.35.refs_1_
  165.4 2.8 collective-permute-done.45.refs_1_
  172.2 5.4 %collective-permute-done.47.refs_3_ = bf16[96,1024]{1,0:T(8,128)(2,1)S(1)} collective-permute-done((bf16[96,1024]{1,0:T(8,128)(2,1)S(1)}, bf16[96,1024]{1,0:T(8,128)(2,1)S(1)}, u32[]{:S(2)}, u32[]{:S(2)}) %collective-permute-start.47) | collective-permute-done | bytes 196640 | tf_op jit(solution)/shard_map/ppermute | solution.py:475
  191.1 2.9 shard_map.284
  196.7 2.6 shard_map.286
  213.2 2.9 shard_map.288
  218.2 3.7 shard_map.289
  230.6 4.2 collective-permute-done.72.refs_2_
  243.3 2.8 collective-permute-done.75.refs_1_
  246.1 4.4 collective-permute-done.76.refs_2_
  255.2 3.8 shard_map.292
  262.5 4.3 collective-permute-done.79.refs_1_
  267.3 2.9 collective-permute-done.81.refs_3_
  276.1 2.9 shard_map.294
  284.0 2.7 collective-permute-start.88
  290.8 3.5 shard_map.295
  301.7 3.9 add_convert_fusion
  314.5 2.7 collective-permute-done.59.refs_2_
  328.2 2.7 concatenate.47
  348.4 2.6 add_convert_fusion.2
  351.1 8.4 %collective-permute-start.110 = (f32[4,12,256]{2,1,0:T(8,128)S(1)}, f32[4,12,256]{2,1,0:T(8,128)S(1)}, u32[]{:S(2)}, u32[]{:S(2)}) collective-permute-start(f32[4,12,256]{2,1,0:T(8,128)S(1)} %broadcast_select_fusion.12), channel_id=1, source_target_pairs={{0,16},{16,0},{1,17},{17,1},{2,18},{18,2},{3,19},{19,3},{4,20},{20... | collective-permute-start | bytes 147464 | tf_op jit(solution)/shard_map/ppermute | solution.py:466
  360.7 3.5 collective-permute-start.94
  365.2 6.7 %collective-permute-done.94 = bf16[128,1024]{1,0:T(8,128)(2,1)S(1)} collective-permute-done((bf16[128,1024]{1,0:T(8,128)(2,1)S(1)}, bf16[128,1024]{1,0:T(8,128)(2,1)S(1)}, u32[]{:S(2)}, u32[]{:S(2)}) %collective-permute-start.94) | collective-permute-done | bytes 262176 | tf_op jit(solution)/shard_map/ppermute | solution.py:475
  371.8 3.4 collective-permute-start.113
  375.3 9.0 %collective-permute-done.93 = bf16[128,1024]{1,0:T(8,128)(2,1)S(1)} collective-permute-done((bf16[128,1024]{1,0:T(8,128)(2,1)S(1)}, bf16[128,1024]{1,0:T(8,128)(2,1)S(1)}, u32[]{:S(2)}, u32[]{:S(2)}) %collective-permute-start.93) | collective-permute-done | bytes 262176 | tf_op jit(solution)/shard_map/ppermute | solution.py:475
  384.3 3.2 collective-permute-start.111
  394.9 3.1 collective-permute-start.103
  399.1 2.8 collective-permute-start.107
  401.9 3.1 collective-permute-start.108
  404.9 3.4 collective-permute-start.109
  410.9 19.0 %collective-permute-done.115 = f32[12,256]{1,0:T(8,128)S(1)} collective-permute-done((f32[12,256]{1,0:T(8,128)S(1)}, f32[12,256]{1,0:T(8,128)S(1)}, u32[]{:S(2)}, u32[]{:S(2)}) %collective-permute-start.115) | collective-permute-done | bytes 12320 | tf_op jit(solution)/shard_map/ppermute | solution.py:475
  433.7 3.1 collective-permute-start.104
  436.8 3.4 collective-permute-start.105
  441.4 9.0 %collective-permute-done.104.refs_2_ = bf16[256,1024]{1,0:T(8,128)(2,1)S(1)} collective-permute-done((bf16[256,1024]{1,0:T(8,128)(2,1)S(1)}, bf16[256,1024]{1,0:T(8,128)(2,1)S(1)}, u32[]{:S(2)}, u32[]{:S(2)}) %collective-permute-start.104) | collective-permute-done | bytes 524320 | tf_op jit(solution)/shard_map/ppermute | solution.py:478
  450.4 5.3 %shard_map.298 = (f32[256,3072]{1,0:T(8,128)}, f32[256,1024]{1,0:T(8,128)}) custom-call(s32[3]{0:T(128)S(1)} %pad_add_fusion.1.where, bf16[256,1024]{1,0:T(8,128)(2,1)S(1)} %constant_dynamic-update-slice_fusion.2.refs_0_, bf16[256,1024]{1,0:T(8,128)(2,1)S(1)} %collective-permute-done.103.refs_1_, bf16[256,1024]{1,0:T(8,128)(2,1)S(1)} %collective-permute-done.104.refs_2_, ...), custom_call_target="tpu_custom_call" | custom-call | bytes 8519680 | tf_op jit(solution)/shard_map/pallas_call | solution.py:36
  455.7 5.6 %shard_map.299 = (f32[256,4096]{1,0:T(8,128)}, f32[1024,1024]{1,0:T(8,128)}) custom-call(s32[3]{0:T(128)S(1)} %pad_add_fusion.1.where, bf16[512,1024]{1,0:T(8,128)(2,1)S(1)} %constant_dynamic-update-slice_fusion.4.refs_0_, bf16[512,1024]{1,0:T(8,128)(2,1)S(1)} %collective-permute-done.107.refs_1_, bf16[512,1024]{1,0:T(8,128)(2,1)S(1)} %collective-permute-done.108.refs_2_, ...), custom_call_target="tpu_custom_call" | custom-call | bytes 16777216 | tf_op jit(solution)/shard_map/pallas_call | solution.py:36
  (563 shorter events, 217.0 us)
Async XLA Ops:
  7.2 276.8 %reduce-scatter.4.cloned.1.call-start = ((), (), s32[]{:S(2)}) async-start(), calls=%async_computation.3 | async-start | bytes 2621440 | tf_op jit(solution)/shard_map/reduce_scatter | solution.py:528
  12.5 32.8 %collective-permute-start = (bf16[12,256]{1,0:T(8,128)(2,1)S(1)}, bf16[12,256]{1,0:T(8,128)(2,1)S(1)}, u32[]{:S(2)}, u32[]{:S(2)}) collective-permute-start(bf16[12,256]{1,0:T(8,128)(2,1)S(1)} %concatenate.36), channel_id=1, source_target_pairs={{0,12},{4,8},{8,4},{12,0},{1,13},{5,9},{9,5},{13,1},{2,14},{6,10},... | collective-permute-start | bytes 18440 | tf_op jit(solution)/shard_map/ppermute | solution.py:475
  17.2 28.1 %collective-permute-start.1 = (bf16[12,256]{1,0:T(8,128)(2,1)S(1)}, bf16[12,256]{1,0:T(8,128)(2,1)S(1)}, u32[]{:S(2)}, u32[]{:S(2)}) collective-permute-start(bf16[12,256]{1,0:T(8,128)(2,1)S(1)} %concatenate.36), channel_id=1, source_target_pairs={{0,8},{4,12},{8,0},{12,4},{1,9},{5,13},{9,1},{13,5},{2,10},{6,14},... | collective-permute-start | bytes 18440 | tf_op jit(solution)/shard_map/ppermute | solution.py:475
  17.2 28.1 %collective-permute-start.2 = (bf16[12,256]{1,0:T(8,128)(2,1)S(1)}, bf16[12,256]{1,0:T(8,128)(2,1)S(1)}, u32[]{:S(2)}, u32[]{:S(2)}) collective-permute-start(bf16[12,256]{1,0:T(8,128)(2,1)S(1)} %concatenate.36), channel_id=1, source_target_pairs={{0,4},{4,0},{8,12},{12,8},{1,5},{5,1},{9,13},{13,9},{2,6},{6,2},{1... | collective-permute-start | bytes 18440 | tf_op jit(solution)/shard_map/ppermute | solution.py:475
  44.1 18.1 %collective-permute-start.25 = (bf16[256,1024]{1,0:T(8,128)(2,1)S(1)}, bf16[256,1024]{1,0:T(8,128)(2,1)S(1)}, u32[]{:S(2)}, u32[]{:S(2)}) collective-permute-start(bf16[256,1024]{1,0:T(8,128)(2,1)S(1)} %get-tuple-element.190.refs_0_), channel_id=1, source_target_pairs={{0,4},{4,8},{8,12},{12,0},{1,5},{5,9},{9,13},{13,1},{2,6},{6,10},{... | collective-permute-start | bytes 1572872 | tf_op jit(solution)/shard_map/ppermute | solution.py:491
  44.8 17.3 %collective-permute-start.10 = (bf16[128,1024]{1,0:T(8,128)(2,1)}, bf16[128,1024]{1,0:T(8,128)(2,1)S(1)}, u32[]{:S(2)}, u32[]{:S(2)}) collective-permute-start(bf16[128,1024]{1,0:T(8,128)(2,1)} %collective-permute-done.9.refs_2_), channel_id=1, source_target_pairs={{0,4},{4,8},{8,12},{12,0},{1,5},{5,9},{9,13},{13,1},{2,6},{6,10},{... | collective-permute-start | bytes 786440 | tf_op jit(solution)/shard_map/ppermute | solution.py:491
  45.5 17.7 %collective-permute-start.11 = (bf16[128,1024]{1,0:T(8,128)(2,1)S(1)}, bf16[128,1024]{1,0:T(8,128)(2,1)S(1)}, u32[]{:S(2)}, u32[]{:S(2)}) collective-permute-start(bf16[128,1024]{1,0:T(8,128)(2,1)S(1)} %get-tuple-element.178.refs_0_), channel_id=1, source_target_pairs={{0,16},{16,0},{1,17},{17,1},{2,18},{18,2},{3,19},{19,3},{4,20},{20... | collective-permute-start | bytes 786440 | tf_op jit(solution)/shard_map/ppermute | solution.py:466
  46.1 19.3 %collective-permute-start.12 = (bf16[128,1024]{1,0:T(8,128)(2,1)}, bf16[128,1024]{1,0:T(8,128)(2,1)S(1)}, u32[]{:S(2)}, u32[]{:S(2)}) collective-permute-start(bf16[128,1024]{1,0:T(8,128)(2,1)} %collective-permute-done.8.refs_1_), channel_id=1, source_target_pairs={{0,16},{16,0},{1,17},{17,1},{2,18},{18,2},{3,19},{19,3},{4,20},{20... | collective-permute-start | bytes 786440 | tf_op jit(solution)/shard_map/ppermute | solution.py:466
  46.6 21.0 %collective-permute-start.13 = (bf16[128,1024]{1,0:T(8,128)(2,1)}, bf16[128,1024]{1,0:T(8,128)(2,1)S(1)}, u32[]{:S(2)}, u32[]{:S(2)}) collective-permute-start(bf16[128,1024]{1,0:T(8,128)(2,1)} %collective-permute-done.9.refs_2_), channel_id=1, source_target_pairs={{0,16},{16,0},{1,17},{17,1},{2,18},{18,2},{3,19},{19,3},{4,20},{20... | collective-permute-start | bytes 786440 | tf_op jit(solution)/shard_map/ppermute | solution.py:466
  62.1 16.2 %collective-permute-start.26 = (bf16[256,1024]{1,0:T(8,128)(2,1)S(1)}, bf16[256,1024]{1,0:T(8,128)(2,1)}, u32[]{:S(2)}, u32[]{:S(2)}) collective-permute-start(bf16[256,1024]{1,0:T(8,128)(2,1)S(1)} %collective-permute-done.25.refs_1_), channel_id=1, source_target_pairs={{0,4},{4,8},{8,12},{12,0},{1,5},{5,9},{9,13},{13,1},{2,6},{6,10},{... | collective-permute-start | bytes 1572872 | tf_op jit(solution)/shard_map/ppermute | solution.py:491
  63.9 22.1 %collective-permute-start.4 = (bf16[96,1024]{1,0:T(8,128)(2,1)S(1)}, bf16[96,1024]{1,0:T(8,128)(2,1)}, u32[]{:S(2)}, u32[]{:S(2)}) collective-permute-start(bf16[96,1024]{1,0:T(8,128)(2,1)S(1)} %shard_map.271.refs_0_), channel_id=1, source_target_pairs={{0,1},{1,0},{2,3},{3,2},{4,5},{5,4},{6,7},{7,6},{8,9},{9,8},{10,11... | collective-permute-start | bytes 589832 | tf_op jit(solution)/shard_map/ppermute | solution.py:475
  66.0 20.1 %collective-permute-start.5 = (bf16[96,1024]{1,0:T(8,128)(2,1)S(1)}, bf16[96,1024]{1,0:T(8,128)(2,1)}, u32[]{:S(2)}, u32[]{:S(2)}) collective-permute-start(bf16[96,1024]{1,0:T(8,128)(2,1)S(1)} %shard_map.271.refs_0_), channel_id=1, source_target_pairs={{0,2},{1,3},{2,0},{3,1},{4,6},{5,7},{6,4},{7,5},{8,10},{9,11},{10,... | collective-permute-start | bytes 589832 | tf_op jit(solution)/shard_map/ppermute | solution.py:475
  68.3 17.9 %collective-permute-start.6 = (bf16[96,1024]{1,0:T(8,128)(2,1)S(1)}, bf16[96,1024]{1,0:T(8,128)(2,1)}, u32[]{:S(2)}, u32[]{:S(2)}) collective-permute-start(bf16[96,1024]{1,0:T(8,128)(2,1)S(1)} %shard_map.271.refs_0_), channel_id=1, source_target_pairs={{0,3},{1,2},{2,1},{3,0},{4,7},{5,6},{6,5},{7,4},{8,11},{9,10},{10,... | collective-permute-start | bytes 589832 | tf_op jit(solution)/shard_map/ppermute | solution.py:475
  69.5 24.6 %collective-permute-start.28 = (bf16[256,1024]{1,0:T(8,128)(2,1)S(1)}, bf16[256,1024]{1,0:T(8,128)(2,1)}, u32[]{:S(2)}, u32[]{:S(2)}) collective-permute-start(bf16[256,1024]{1,0:T(8,128)(2,1)S(1)} %get-tuple-element.190.refs_0_), channel_id=1, source_target_pairs={{0,16},{16,0},{1,17},{17,1},{2,18},{18,2},{3,19},{19,3},{4,20},{20... | collective-permute-start | bytes 1572872 | tf_op jit(solution)/shard_map/ppermute | solution.py:466
  78.4 25.4 %collective-permute-start.27 = (bf16[256,1024]{1,0:T(8,128)(2,1)}, bf16[256,1024]{1,0:T(8,128)(2,1)S(1)}, u32[]{:S(2)}, u32[]{:S(2)}) collective-permute-start(bf16[256,1024]{1,0:T(8,128)(2,1)} %collective-permute-done.26.refs_2_), channel_id=1, source_target_pairs={{0,4},{4,8},{8,12},{12,0},{1,5},{5,9},{9,13},{13,1},{2,6},{6,10},{... | collective-permute-start | bytes 1572872 | tf_op jit(solution)/shard_map/ppermute | solution.py:491
  94.2 16.5 %collective-permute-start.51 = (bf16[256,1024]{1,0:T(8,128)(2,1)S(1)}, bf16[256,1024]{1,0:T(8,128)(2,1)S(1)}, u32[]{:S(2)}, u32[]{:S(2)}) collective-permute-start(bf16[256,1024]{1,0:T(8,128)(2,1)S(1)} %get-tuple-element.208.refs_0_), channel_id=1, source_target_pairs={{0,4},{4,8},{8,12},{12,0},{1,5},{5,9},{9,13},{13,1},{2,6},{6,10},{... | collective-permute-start | bytes 1572872 | tf_op jit(solution)/shard_map/ppermute | solution.py:491
  100.8 19.0 %collective-permute-start.29 = (bf16[256,1024]{1,0:T(8,128)(2,1)S(1)}, bf16[256,1024]{1,0:T(8,128)(2,1)S(1)}, u32[]{:S(2)}, u32[]{:S(2)}) collective-permute-start(bf16[256,1024]{1,0:T(8,128)(2,1)S(1)} %copy-done.25), channel_id=1, source_target_pairs={{0,16},{16,0},{1,17},{17,1},{2,18},{18,2},{3,19},{19,3},{4,20},{20... | collective-permute-start | bytes 1572872 | tf_op jit(solution)/shard_map/ppermute | solution.py:466
  100.8 20.4 %collective-permute-start.30 = (bf16[256,1024]{1,0:T(8,128)(2,1)}, bf16[256,1024]{1,0:T(8,128)(2,1)S(1)}, u32[]{:S(2)}, u32[]{:S(2)}) collective-permute-start(bf16[256,1024]{1,0:T(8,128)(2,1)} %collective-permute-done.26.refs_2_), channel_id=1, source_target_pairs={{0,16},{16,0},{1,17},{17,1},{2,18},{18,2},{3,19},{19,3},{4,20},{20... | collective-permute-start | bytes 1572872 | tf_op jit(solution)/shard_map/ppermute | solution.py:466
  103.7 18.3 %collective-permute-start.31 = (bf16[256,1024]{1,0:T(8,128)(2,1)S(1)}, bf16[256,1024]{1,0:T(8,128)(2,1)S(1)}, u32[]{:S(2)}, u32[]{:S(2)}) collective-permute-start(bf16[256,1024]{1,0:T(8,128)(2,1)S(1)} %collective-permute-done.27.refs_3_), channel_id=1, source_target_pairs={{0,16},{16,0},{1,17},{17,1},{2,18},{18,2},{3,19},{19,3},{4,20},{20... | collective-permute-start | bytes 1572872 | tf_op jit(solution)/shard_map/ppermute | solution.py:466
  121.2 19.0 %collective-permute-start.52 = (bf16[256,1024]{1,0:T(8,128)(2,1)S(1)}, bf16[256,1024]{1,0:T(8,128)(2,1)S(1)}, u32[]{:S(2)}, u32[]{:S(2)}) collective-permute-start(bf16[256,1024]{1,0:T(8,128)(2,1)S(1)} %collective-permute-done.51.refs_1_), channel_id=1, source_target_pairs={{0,4},{4,8},{8,12},{12,0},{1,5},{5,9},{9,13},{13,1},{2,6},{6,10},{... | collective-permute-start | bytes 1572872 | tf_op jit(solution)/shard_map/ppermute | solution.py:491
  122.0 18.2 %collective-permute-start.40 = (bf16[128,1024]{1,0:T(8,128)(2,1)S(1)}, bf16[128,1024]{1,0:T(8,128)(2,1)S(1)}, u32[]{:S(2)}, u32[]{:S(2)}) collective-permute-start(bf16[128,1024]{1,0:T(8,128)(2,1)S(1)} %collective-permute-done.39.refs_2_), channel_id=1, source_target_pairs={{0,4},{4,8},{8,12},{12,0},{1,5},{5,9},{9,13},{13,1},{2,6},{6,10},{... | collective-permute-start | bytes 786440 | tf_op jit(solution)/shard_map/ppermute | solution.py:491
  132.4 16.6 %collective-permute-start.41 = (bf16[128,1024]{1,0:T(8,128)(2,1)S(1)}, bf16[128,1024]{1,0:T(8,128)(2,1)S(1)}, u32[]{:S(2)}, u32[]{:S(2)}) collective-permute-start(bf16[128,1024]{1,0:T(8,128)(2,1)S(1)} %get-tuple-element.199.refs_0_), channel_id=1, source_target_pairs={{0,16},{16,0},{1,17},{17,1},{2,18},{18,2},{3,19},{19,3},{4,20},{20... | collective-permute-start | bytes 786440 | tf_op jit(solution)/shard_map/ppermute | solution.py:466
  148.5 16.9 %collective-permute-start.53 = (bf16[256,1024]{1,0:T(8,128)(2,1)S(1)}, bf16[256,1024]{1,0:T(8,128)(2,1)S(1)}, u32[]{:S(2)}, u32[]{:S(2)}) collective-permute-start(bf16[256,1024]{1,0:T(8,128)(2,1)S(1)} %collective-permute-done.52.refs_2_), channel_id=1, source_target_pairs={{0,4},{4,8},{8,12},{12,0},{1,5},{5,9},{9,13},{13,1},{2,6},{6,10},{... | collective-permute-start | bytes 1572872 | tf_op jit(solution)/shard_map/ppermute | solution.py:491
  163.4 15.8 %collective-permute-start.54 = (bf16[256,1024]{1,0:T(8,128)(2,1)S(1)}, bf16[256,1024]{1,0:T(8,128)(2,1)S(1)}, u32[]{:S(2)}, u32[]{:S(2)}) collective-permute-start(bf16[256,1024]{1,0:T(8,128)(2,1)S(1)} %get-tuple-element.208.refs_0_), channel_id=1, source_target_pairs={{0,16},{16,0},{1,17},{17,1},{2,18},{18,2},{3,19},{19,3},{4,20},{20... | collective-permute-start | bytes 1572872 | tf_op jit(solution)/shard_map/ppermute | solution.py:466
  163.4 16.6 %collective-permute-start.55 = (bf16[256,1024]{1,0:T(8,128)(2,1)S(1)}, bf16[256,1024]{1,0:T(8,128)(2,1)S(1)}, u32[]{:S(2)}, u32[]{:S(2)}) collective-permute-start(bf16[256,1024]{1,0:T(8,128)(2,1)S(1)} %collective-permute-done.51.refs_1_), channel_id=1, source_target_pairs={{0,16},{16,0},{1,17},{17,1},{2,18},{18,2},{3,19},{19,3},{4,20},{20... | collective-permute-start | bytes 1572872 | tf_op jit(solution)/shard_map/ppermute | solution.py:466
  165.4 16.8 %collective-permute-start.56 = (bf16[256,1024]{1,0:T(8,128)(2,1)S(1)}, bf16[256,1024]{1,0:T(8,128)(2,1)S(1)}, u32[]{:S(2)}, u32[]{:S(2)}) collective-permute-start(bf16[256,1024]{1,0:T(8,128)(2,1)S(1)} %collective-permute-done.52.refs_2_), channel_id=1, source_target_pairs={{0,16},{16,0},{1,17},{17,1},{2,18},{18,2},{3,19},{19,3},{4,20},{20... | collective-permute-start | bytes 1572872 | tf_op jit(solution)/shard_map/ppermute | solution.py:466
  234.8 76.6 %reduce-scatter.6.cloned.1.call-start = ((), (), s32[]{:S(2)}) async-start(), calls=%async_computation.4 | async-start | bytes 1310720 | tf_op jit(solution)/shard_map/reduce_scatter | solution.py:528
  284.0 16.5 %collective-permute-start.89 = (bf16[1024,1024]{1,0:T(8,128)(2,1)}, bf16[1024,1024]{1,0:T(8,128)(2,1)}, u32[]{:S(2)}, u32[]{:S(2)}) collective-permute-start(bf16[1024,1024]{1,0:T(8,128)(2,1)} %copy-done.72), channel_id=1, source_target_pairs={{0,16},{16,0},{1,17},{17,1},{2,18},{18,2},{3,19},{19,3},{4,20},{20... | collective-permute-start | bytes 6291464 | tf_op jit(solution)/shard_map/ppermute | solution.py:466
  284.0 106.1 %reduce-scatter.8.cloned.1.call-start = ((), (), s32[]{:S(2)}) async-start(), calls=%async_computation.5 | async-start | bytes 2621440 | tf_op jit(solution)/shard_map/reduce_scatter | solution.py:528
  284.0 16.4 %collective-permute-start.88 = (bf16[256,1024]{1,0:T(8,128)(2,1)}, bf16[256,1024]{1,0:T(8,128)(2,1)S(1)}, u32[]{:S(2)}, u32[]{:S(2)}) collective-permute-start(bf16[256,1024]{1,0:T(8,128)(2,1)} %reduce-scatter.4.cloned.1.call-done), channel_id=1, source_target_pairs={{0,16},{1,17},{2,18},{3,19},{4,20},{5,21},{6,22},{7,23},{8,24},{9,... | collective-permute-start | bytes 1572872 | tf_op jit(solution)/shard_map/ppermute | solution.py:530
  317.4 29.3 %collective-permute-start.91 = (bf16[512,1024]{1,0:T(8,128)(2,1)}, bf16[512,1024]{1,0:T(8,128)(2,1)}, u32[]{:S(2)}, u32[]{:S(2)}) collective-permute-start(bf16[512,1024]{1,0:T(8,128)(2,1)} %copy-done.73), channel_id=1, source_target_pairs={{0,16},{16,0},{1,17},{17,1},{2,18},{18,2},{3,19},{19,3},{4,20},{20... | collective-permute-start | bytes 3145736 | tf_op jit(solution)/shard_map/ppermute | solution.py:466
  318.7 26.3 %collective-permute-start.99 = (bf16[256,1024]{1,0:T(8,128)(2,1)S(1)}, bf16[256,1024]{1,0:T(8,128)(2,1)}, u32[]{:S(2)}, u32[]{:S(2)}) collective-permute-start(bf16[256,1024]{1,0:T(8,128)(2,1)S(1)} %constant_dynamic-update-slice_fusion.refs_4_), channel_id=1, source_target_pairs={{16,17},{17,16},{18,19},{19,18},{20,21},{21,20},{22,23},{23,22},{2... | collective-permute-start | bytes 1572872 | tf_op jit(solution)/shard_map/ppermute | solution.py:478
  325.8 38.4 %collective-permute-start.95 = (bf16[512,1024]{1,0:T(8,128)(2,1)S(1)}, bf16[512,1024]{1,0:T(8,128)(2,1)S(1)}, u32[]{:S(2)}, u32[]{:S(2)}) collective-permute-start(bf16[512,1024]{1,0:T(8,128)(2,1)S(1)} %pad_maximum_fusion.refs_4_), channel_id=1, source_target_pairs={{16,17},{17,16},{18,19},{19,18},{20,21},{21,20},{22,23},{23,22},{2... | collective-permute-start | bytes 3145736 | tf_op jit(solution)/shard_map/ppermute | solution.py:478
  331.7 19.4 %collective-permute-start.100 = (bf16[256,1024]{1,0:T(8,128)(2,1)S(1)}, bf16[256,1024]{1,0:T(8,128)(2,1)}, u32[]{:S(2)}, u32[]{:S(2)}) collective-permute-start(bf16[256,1024]{1,0:T(8,128)(2,1)S(1)} %constant_dynamic-update-slice_fusion.refs_4_), channel_id=1, source_target_pairs={{16,18},{17,19},{18,16},{19,17},{20,22},{21,23},{22,20},{23,21},{2... | collective-permute-start | bytes 1572872 | tf_op jit(solution)/shard_map/ppermute | solution.py:478
  333.2 27.5 %collective-permute-start.101 = (bf16[256,1024]{1,0:T(8,128)(2,1)S(1)}, bf16[256,1024]{1,0:T(8,128)(2,1)}, u32[]{:S(2)}, u32[]{:S(2)}) collective-permute-start(bf16[256,1024]{1,0:T(8,128)(2,1)S(1)} %constant_dynamic-update-slice_fusion.refs_4_), channel_id=1, source_target_pairs={{16,19},{17,18},{18,17},{19,16},{20,23},{21,22},{22,21},{23,20},{2... | collective-permute-start | bytes 1572872 | tf_op jit(solution)/shard_map/ppermute | solution.py:478
  345.0 43.6 %collective-permute-start.96 = (bf16[512,1024]{1,0:T(8,128)(2,1)S(1)}, bf16[512,1024]{1,0:T(8,128)(2,1)}, u32[]{:S(2)}, u32[]{:S(2)}) collective-permute-start(bf16[512,1024]{1,0:T(8,128)(2,1)S(1)} %pad_maximum_fusion.refs_4_), channel_id=1, source_target_pairs={{16,18},{17,19},{18,16},{19,17},{20,22},{21,23},{22,20},{23,21},{2... | collective-permute-start | bytes 3145736 | tf_op jit(solution)/shard_map/ppermute | solution.py:478
  346.7 42.0 %collective-permute-start.97 = (bf16[512,1024]{1,0:T(8,128)(2,1)S(1)}, bf16[512,1024]{1,0:T(8,128)(2,1)}, u32[]{:S(2)}, u32[]{:S(2)}) collective-permute-start(bf16[512,1024]{1,0:T(8,128)(2,1)S(1)} %pad_maximum_fusion.refs_4_), channel_id=1, source_target_pairs={{16,19},{17,18},{18,17},{19,16},{20,23},{21,22},{22,21},{23,20},{2... | collective-permute-start | bytes 3145736 | tf_op jit(solution)/shard_map/ppermute | solution.py:478
  364.2 20.1 %collective-permute-start.93 = (bf16[128,1024]{1,0:T(8,128)(2,1)S(1)}, bf16[128,1024]{1,0:T(8,128)(2,1)S(1)}, u32[]{:S(2)}, u32[]{:S(2)}) collective-permute-start(bf16[128,1024]{1,0:T(8,128)(2,1)S(1)} %get-tuple-element.343), channel_id=1, source_target_pairs={{0,8},{4,12},{8,0},{12,4},{1,9},{5,13},{9,1},{13,5},{2,10},{6,14},... | collective-permute-start | bytes 786440 | tf_op jit(solution)/shard_map/ppermute | solution.py:475
  364.2 20.1 %collective-permute-start.92 = (bf16[128,1024]{1,0:T(8,128)(2,1)S(1)}, bf16[128,1024]{1,0:T(8,128)(2,1)S(1)}, u32[]{:S(2)}, u32[]{:S(2)}) collective-permute-start(bf16[128,1024]{1,0:T(8,128)(2,1)S(1)} %get-tuple-element.341), channel_id=1, source_target_pairs={{0,4},{4,0},{8,12},{12,8},{1,5},{5,1},{9,13},{13,9},{2,6},{6,2},{1... | collective-permute-start | bytes 786440 | tf_op jit(solution)/shard_map/ppermute | solution.py:475
  371.8 18.3 %collective-permute-start.113 = (f32[12,256]{1,0:T(8,128)S(1)}, f32[12,256]{1,0:T(8,128)S(1)}, u32[]{:S(2)}, u32[]{:S(2)}) collective-permute-start(f32[12,256]{1,0:T(8,128)S(1)} %get-tuple-element.353), channel_id=1, source_target_pairs={{0,12},{4,8},{8,4},{12,0},{1,13},{5,9},{9,5},{13,1},{2,14},{6,10},... | collective-permute-start | bytes 36872 | tf_op jit(solution)/shard_map/ppermute | solution.py:475
  388.7 16.3 %collective-permute-start.90 = (bf16[96,1024]{1,0:T(8,128)(2,1)}, bf16[96,1024]{1,0:T(8,128)(2,1)}, u32[]{:S(2)}, u32[]{:S(2)}) collective-permute-start(bf16[96,1024]{1,0:T(8,128)(2,1)} %broadcast_select_fusion.6), channel_id=1, source_target_pairs={{0,16},{16,0},{1,17},{17,1},{2,18},{18,2},{3,19},{19,3},{4,20},{20... | collective-permute-start | bytes 589832 | tf_op jit(solution)/shard_map/ppermute | solution.py:466
  392.3 16.8 %collective-permute-start.116 = (f32[12,256]{1,0:T(8,128)S(1)}, f32[12,256]{1,0:T(8,128)S(1)}, u32[]{:S(2)}, u32[]{:S(2)}) collective-permute-start(f32[12,256]{1,0:T(8,128)S(1)} %fusion.5), channel_id=1, source_target_pairs={{0,3},{1,2},{2,1},{3,0},{4,7},{5,6},{6,5},{7,4},{8,11},{9,10},{10,... | collective-permute-start | bytes 36872 | tf_op jit(solution)/shard_map/ppermute | solution.py:475
  394.9 41.9 %collective-permute-start.103 = (bf16[256,1024]{1,0:T(8,128)(2,1)S(1)}, bf16[256,1024]{1,0:T(8,128)(2,1)S(1)}, u32[]{:S(2)}, u32[]{:S(2)}) collective-permute-start(bf16[256,1024]{1,0:T(8,128)(2,1)S(1)} %constant_dynamic-update-slice_fusion.2.refs_0_), channel_id=1, source_target_pairs={{0,1},{1,0},{2,3},{3,2},{4,5},{5,4},{6,7},{7,6},{8,9},{9,8},{10,11... | collective-permute-start | bytes 1572872 | tf_op jit(solution)/shard_map/ppermute | solution.py:478
  399.1 56.6 %collective-permute-start.107 = (bf16[512,1024]{1,0:T(8,128)(2,1)S(1)}, bf16[512,1024]{1,0:T(8,128)(2,1)S(1)}, u32[]{:S(2)}, u32[]{:S(2)}) collective-permute-start(bf16[512,1024]{1,0:T(8,128)(2,1)S(1)} %constant_dynamic-update-slice_fusion.4.refs_0_), channel_id=1, source_target_pairs={{0,1},{1,0},{2,3},{3,2},{4,5},{5,4},{6,7},{7,6},{8,9},{9,8},{10,11... | collective-permute-start | bytes 3145736 | tf_op jit(solution)/shard_map/ppermute | solution.py:478
  401.9 53.8 %collective-permute-start.108 = (bf16[512,1024]{1,0:T(8,128)(2,1)S(1)}, bf16[512,1024]{1,0:T(8,128)(2,1)S(1)}, u32[]{:S(2)}, u32[]{:S(2)}) collective-permute-start(bf16[512,1024]{1,0:T(8,128)(2,1)S(1)} %constant_dynamic-update-slice_fusion.4.refs_0_), channel_id=1, source_target_pairs={{0,2},{1,3},{2,0},{3,1},{4,6},{5,7},{6,4},{7,5},{8,10},{9,11},{10,... | collective-permute-start | bytes 3145736 | tf_op jit(solution)/shard_map/ppermute | solution.py:478
  404.9 50.7 %collective-permute-start.109 = (bf16[512,1024]{1,0:T(8,128)(2,1)S(1)}, bf16[512,1024]{1,0:T(8,128)(2,1)S(1)}, u32[]{:S(2)}, u32[]{:S(2)}) collective-permute-start(bf16[512,1024]{1,0:T(8,128)(2,1)S(1)} %constant_dynamic-update-slice_fusion.4.refs_0_), channel_id=1, source_target_pairs={{0,3},{1,2},{2,1},{3,0},{4,7},{5,6},{6,5},{7,4},{8,11},{9,10},{10,... | collective-permute-start | bytes 3145736 | tf_op jit(solution)/shard_map/ppermute | solution.py:478
  409.1 20.8 %collective-permute-start.115 = (f32[12,256]{1,0:T(8,128)S(1)}, f32[12,256]{1,0:T(8,128)S(1)}, u32[]{:S(2)}, u32[]{:S(2)}) collective-permute-start(f32[12,256]{1,0:T(8,128)S(1)} %fusion.5), channel_id=1, source_target_pairs={{0,2},{1,3},{2,0},{3,1},{4,6},{5,7},{6,4},{7,5},{8,10},{9,11},{10,... | collective-permute-start | bytes 36872 | tf_op jit(solution)/shard_map/ppermute | solution.py:475
  433.7 16.7 %collective-permute-start.104 = (bf16[256,1024]{1,0:T(8,128)(2,1)S(1)}, bf16[256,1024]{1,0:T(8,128)(2,1)S(1)}, u32[]{:S(2)}, u32[]{:S(2)}) collective-permute-start(bf16[256,1024]{1,0:T(8,128)(2,1)S(1)} %constant_dynamic-update-slice_fusion.2.refs_0_), channel_id=1, source_target_pairs={{0,2},{1,3},{2,0},{3,1},{4,6},{5,7},{6,4},{7,5},{8,10},{9,11},{10,... | collective-permute-start | bytes 1572872 | tf_op jit(solution)/shard_map/ppermute | solution.py:478
  (191 other events, 1558.3 us)
Sparse Core Ops, SparseCore 0:
  234.9 43.7 reduce-scatter.3
  284.1 27.2 reduce-scatter.5
  314.3 42.4 reduce-scatter.7
